TPU v7x, 32 devices: a whole 2x2x4 slice. The times are simulated.
32 devices in a mesh: fsdp: 4 (over y, x), expert: 8 (over z, core).
Axes of the slice: x: 2, y: 2, z: 4, core: 2. Of those that a mesh axis runs over, the one named last changes fastest.
Arguments:
- tokens: bfloat16 [4096, 2048], P(('fsdp', 'expert')), may hold values from -6 to 6
- cotangent: bfloat16 [4096, 2048], P(('fsdp', 'expert')), may hold values from -6 to 6
- lengths: int32 [32, 4], P(('fsdp', 'expert')), may hold values from 1 to 64, 128 in all within a row
- routes: int32 [2, 4096, 8], P(None, ('fsdp', 'expert')), may hold values from 0 to 31, all different within a row; in each aligned block of 128 rows (0 to 127, 128 to 255, ..., all dimensions but the last counted through in order) at most 48 rows name the same one
- gains: bfloat16 [2, 4352], P(None, ('fsdp', 'expert')), may hold values from 0.5 to 1.5
- w_query: bfloat16 [2, 2048, 4096], P(None, ('fsdp', 'expert')), may hold values from -0.125 to 0.125
- key_weight: bfloat16 [2, 2048, 512], P(None, ('fsdp', 'expert')), may hold values from -0.125 to 0.125
- value_weight: bfloat16 [2, 2048, 512], P(None, ('fsdp', 'expert')), may hold values from -0.125 to 0.125
- w_out: bfloat16 [2, 4096, 2048], P(None, ('fsdp', 'expert')), may hold values from -0.25 to 0.25
- w_router: bfloat16 [2, 2048, 32], P(None, ('fsdp', 'expert')), may hold values from -0.0625 to 0.0625
- w_gate: bfloat16 [2, 32, 2048, 768], P(None, 'expert', 'fsdp'), may hold values from -0.125 to 0.125
- w_up: bfloat16 [2, 32, 2048, 768], P(None, 'expert', 'fsdp'), may hold values from -0.125 to 0.125
- w_down: bfloat16 [2, 32, 768, 2048], P(None, 'expert', None, 'fsdp'), may hold values from -0.4375 to 0.4375
Outputs:
- output: bfloat16 [4096, 2048], P(('fsdp', 'expert'))
- d_tokens: bfloat16 [4096, 2048], P(('fsdp', 'expert'))
- d_gains: float32 [2, 4352], P(None, ('fsdp', 'expert'))
- d_query: float32 [2, 2048, 4096], P(None, ('fsdp', 'expert'))
- d_key: float32 [2, 2048, 512], P(None, ('fsdp', 'expert'))
- d_value: float32 [2, 2048, 512], P(None, ('fsdp', 'expert'))
- d_out: float32 [2, 4096, 2048], P(None, ('fsdp', 'expert'))
- d_router: float32 [2, 2048, 32], P(None, ('fsdp', 'expert'))
- d_gate: float32 [2, 32, 2048, 768], P(None, 'expert', 'fsdp')
- d_up: float32 [2, 32, 2048, 768], P(None, 'expert', 'fsdp')
- d_down: float32 [2, 32, 768, 2048], P(None, 'expert', None, 'fsdp')
Inputs may be any that keep to these rules, and one draw needn't show every extreme that they name: `routes`: each row names 8 different experts. In each layer the 128 rows of one device name any one expert at most 48 times. The 4 lengths of one device sum to 128.
All inputs are finite; a program needn't handle non-finite values.
Results may differ from a plain program's by a relative error of at most 0.022.
Values may be sent and summed in bfloat16 or wider, within the bound.
A program may use at most 512 MiB of HBM per device.

v0:
```python
from functools import partial
import math

import jax
import jax.numpy as jnp
from jax import lax
from jax.sharding import PartitionSpec as P

MODEL_WIDTH = 2048
QUERY_HEADS = 32
KEY_VALUE_HEADS = 4
HEAD_SIZE = 128
TOP = 8
EXPERTS = 32
DECODER_LAYERS = 2
CAP = 48


EPSILON = 1e-06
ROPE_BASE = 1000000.0


def norm_rows(operand, gain_vec):
    return (
        operand
        * lax.rsqrt(jnp.mean(operand * operand, axis=-1, keepdims=True) + EPSILON)
        * gain_vec
    )


def softmax_last(operand):
    shifted = operand - jnp.max(operand, axis=-1, keepdims=True)
    weights = jnp.exp(shifted)
    return weights / jnp.sum(weights, axis=-1, keepdims=True)


def rotate(operand, cosine, sine):
    half_size = operand.shape[-1] // 2
    front_half = operand[..., :half_size]
    back_half = operand[..., half_size:]
    return jnp.concatenate(
        [front_half * cosine - back_half * sine, back_half * cosine + front_half * sine], axis=-1
    )


def head_piece(query_pre, prerotation_key, g_query, g_key, cosine, sine):
    return (
        rotate(norm_rows(query_pre, g_query), cosine, sine),
        rotate(norm_rows(prerotation_key, g_key), cosine, sine),
    )


def geometry(lengths, local_rows):
    seq_ends = jnp.cumsum(lengths[0])
    seq_starts = seq_ends - lengths[0]
    offsets = jnp.arange(local_rows, dtype=jnp.int32)
    segment = jnp.sum((offsets[:, None] >= seq_ends[None, :]).astype(jnp.int32), axis=1)
    member = segment[:, None] == jnp.arange(seq_ends.shape[0], dtype=jnp.int32)[None, :]
    begins = jnp.sum(jnp.where(member, seq_starts[None, :], 0), axis=1)
    position = (offsets - begins).astype(jnp.float32)
    inverse = jnp.exp(
        -(2.0 * jnp.arange(HEAD_SIZE // 2, dtype=jnp.float32) / HEAD_SIZE) * math.log(ROPE_BASE)
    )
    angles = position[:, None] * inverse[None, :]
    allowed = (segment[:, None] == segment[None, :]) & (offsets[None, :] <= offsets[:, None])
    return (jnp.cos(angles)[:, None, :], jnp.sin(angles)[:, None, :], allowed)


def slot_table(route_rows):
    flat_routes = route_rows.reshape(-1)
    matches = (flat_routes[:, None] == jnp.arange(EXPERTS, dtype=jnp.int32)[None, :]).astype(
        jnp.int32
    )
    rank_in = jnp.sum((jnp.cumsum(matches, axis=0) - 1) * matches, axis=1)
    return flat_routes * CAP + rank_in


def split_gains(gain_vec):
    return (
        gain_vec[:MODEL_WIDTH],
        gain_vec[MODEL_WIDTH : 2 * MODEL_WIDTH],
        gain_vec[2 * MODEL_WIDTH : 2 * MODEL_WIDTH + HEAD_SIZE],
        gain_vec[2 * MODEL_WIDTH + HEAD_SIZE :],
    )


def score_block(query_copy, key_b, allowed):
    local_rows = query_copy.shape[0]
    grouped_rows = query_copy.reshape(
        local_rows, KEY_VALUE_HEADS, QUERY_HEADS // KEY_VALUE_HEADS, HEAD_SIZE
    )
    raw_scores = jnp.einsum(
        "tgjd,sgd->gjts", grouped_rows, key_b, preferred_element_type=jnp.float32
    ) * (1.0 / math.sqrt(HEAD_SIZE))
    return jnp.where(allowed[None, None], raw_scores, -1e30)


def layer_forward(state, dense, experts, route_rows, cosine, sine, allowed, peers):
    w_query, key_weight, value_weight, w_out, w_router, gain_raw = dense
    w_gate, w_up, w_down = experts
    local_rows = state.shape[0]
    experts_here = w_gate.shape[0]
    g_attn, g_ffn, g_query, g_key = split_gains(gain_raw.astype(jnp.float32))
    normalized_input = norm_rows(state, g_attn).astype(jnp.bfloat16)
    query_pre = jnp.dot(normalized_input, w_query, preferred_element_type=jnp.float32).reshape(
        local_rows, QUERY_HEADS, HEAD_SIZE
    )
    prerotation_key = jnp.dot(
        normalized_input, key_weight, preferred_element_type=jnp.float32
    ).reshape(local_rows, KEY_VALUE_HEADS, HEAD_SIZE)
    value_b = (
        jnp.dot(normalized_input, value_weight, preferred_element_type=jnp.float32)
        .astype(jnp.bfloat16)
        .reshape(local_rows, KEY_VALUE_HEADS, HEAD_SIZE)
    )
    query_f, key_f = head_piece(query_pre, prerotation_key, g_query, g_key, cosine, sine)
    query_copy = query_f.astype(jnp.bfloat16)
    key_b = key_f.astype(jnp.bfloat16)
    scores = score_block(query_copy, key_b, allowed)
    peaks = jnp.max(scores, axis=-1, keepdims=True)
    expos = jnp.exp(scores - peaks)
    totals = jnp.sum(expos, axis=-1, keepdims=True)
    log_total = peaks + jnp.log(totals)
    probs_b = (expos / totals).astype(jnp.bfloat16)
    attended = jnp.einsum("gjts,sgd->tgjd", probs_b, value_b, preferred_element_type=jnp.float32)
    attended = attended.reshape(local_rows, QUERY_HEADS * HEAD_SIZE).astype(jnp.bfloat16)
    middle = state + jnp.dot(attended, w_out, preferred_element_type=jnp.float32)
    mixer_in = norm_rows(middle, g_ffn).astype(jnp.bfloat16)
    logits = jnp.dot(mixer_in, w_router, preferred_element_type=jnp.float32)
    gates = softmax_last(jnp.take_along_axis(logits, route_rows, axis=1))
    slot_ids = slot_table(route_rows)
    outgoing = (
        jnp.zeros((EXPERTS * CAP, MODEL_WIDTH), jnp.bfloat16)
        .at[slot_ids]
        .set(jnp.repeat(mixer_in, TOP, axis=0))
    )
    incoming = lax.all_to_all(
        outgoing.reshape(peers, experts_here * CAP, MODEL_WIDTH),
        "expert",
        split_axis=0,
        concat_axis=0,
        tiled=True,
    )
    incoming = incoming.reshape(peers, experts_here, CAP, MODEL_WIDTH)
    gate_pre = jnp.einsum("secd,edf->secf", incoming, w_gate, preferred_element_type=jnp.float32)
    up_pre = jnp.einsum("secd,edf->secf", incoming, w_up, preferred_element_type=jnp.float32)
    hidden_b = (jax.nn.silu(gate_pre) * up_pre).astype(jnp.bfloat16)
    produced = jnp.einsum(
        "secf,efd->secd", hidden_b, w_down, preferred_element_type=jnp.float32
    ).astype(jnp.bfloat16)
    returned = lax.all_to_all(
        produced.reshape(peers, experts_here * CAP, MODEL_WIDTH),
        "expert",
        split_axis=0,
        concat_axis=0,
        tiled=True,
    )
    picked = returned.reshape(EXPERTS * CAP, MODEL_WIDTH)[slot_ids].reshape(
        local_rows, TOP, MODEL_WIDTH
    )
    new_state = middle + jnp.sum(gates[:, :, None] * picked.astype(jnp.float32), axis=1)
    memo = (
        state,
        normalized_input,
        query_pre,
        prerotation_key,
        query_copy,
        key_b,
        value_b,
        log_total,
        attended,
        middle,
        mixer_in,
        gates,
        slot_ids,
        picked,
        incoming,
        gate_pre,
        up_pre,
        hidden_b,
    )
    return (new_state, memo)


def layer_backward(grad_state, memo, dense, experts, route_rows, cosine, sine, allowed, peers):
    (
        state,
        normalized_input,
        query_pre,
        prerotation_key,
        query_copy,
        key_b,
        value_b,
        log_total,
        attended,
        middle,
        mixer_in,
        gates,
        slot_ids,
        picked,
        incoming,
        gate_pre,
        up_pre,
        hidden_b,
    ) = memo
    w_query, key_weight, value_weight, w_out, w_router, gain_raw = dense
    w_gate, w_up, w_down = experts
    local_rows = state.shape[0]
    experts_here = w_gate.shape[0]
    query_group_size = QUERY_HEADS // KEY_VALUE_HEADS
    scale = 1.0 / math.sqrt(HEAD_SIZE)
    g_attn, g_ffn, g_query, g_key = split_gains(gain_raw.astype(jnp.float32))
    grad_gates = jnp.sum(picked.astype(jnp.float32) * grad_state[:, None, :], axis=2)
    grad_chosen = gates * (grad_gates - jnp.sum(gates * grad_gates, axis=1, keepdims=True))
    choose = (route_rows[:, :, None] == jnp.arange(EXPERTS, dtype=jnp.int32)[None, None, :]).astype(
        jnp.float32
    )
    grad_logits = jnp.sum(choose * grad_chosen[:, :, None], axis=1).astype(jnp.bfloat16)
    grad_router = jnp.dot(mixer_in.T, grad_logits, preferred_element_type=jnp.float32)
    grad_mixer = jnp.dot(grad_logits, w_router.T, preferred_element_type=jnp.float32)
    grad_picked = (
        (gates[:, :, None] * grad_state[:, None, :])
        .astype(jnp.bfloat16)
        .reshape(local_rows * TOP, MODEL_WIDTH)
    )
    outgoing = jnp.zeros((EXPERTS * CAP, MODEL_WIDTH), jnp.bfloat16).at[slot_ids].set(grad_picked)
    grad_produced = lax.all_to_all(
        outgoing.reshape(peers, experts_here * CAP, MODEL_WIDTH),
        "expert",
        split_axis=0,
        concat_axis=0,
        tiled=True,
    )
    grad_produced = grad_produced.reshape(peers, experts_here, CAP, MODEL_WIDTH)
    grad_down = jnp.einsum(
        "secf,secd->efd", hidden_b, grad_produced, preferred_element_type=jnp.float32
    )
    grad_hidden = jnp.einsum(
        "secd,efd->secf", grad_produced, w_down, preferred_element_type=jnp.float32
    )
    sigmoid_gate = jax.nn.sigmoid(gate_pre)
    grad_gate_pre = (
        grad_hidden * up_pre * sigmoid_gate * (1.0 + gate_pre * (1.0 - sigmoid_gate))
    ).astype(jnp.bfloat16)
    grad_up_pre = (grad_hidden * gate_pre * sigmoid_gate).astype(jnp.bfloat16)
    grad_wgate = jnp.einsum(
        "secd,secf->edf", incoming, grad_gate_pre, preferred_element_type=jnp.float32
    )
    grad_wup = jnp.einsum(
        "secd,secf->edf", incoming, grad_up_pre, preferred_element_type=jnp.float32
    )
    grad_incoming = jnp.einsum(
        "secf,edf->secd", grad_gate_pre, w_gate, preferred_element_type=jnp.float32
    )
    grad_incoming = grad_incoming + jnp.einsum(
        "secf,edf->secd", grad_up_pre, w_up, preferred_element_type=jnp.float32
    )
    grad_incoming = grad_incoming.astype(jnp.bfloat16).reshape(
        peers, experts_here * CAP, MODEL_WIDTH
    )
    grad_returned = lax.all_to_all(
        grad_incoming, "expert", split_axis=0, concat_axis=0, tiled=True
    ).reshape(EXPERTS * CAP, MODEL_WIDTH)
    grad_mixer = grad_mixer + jnp.sum(
        grad_returned[slot_ids].reshape(local_rows, TOP, MODEL_WIDTH).astype(jnp.float32), axis=1
    )
    unused_mid, norm_back = jax.vjp(norm_rows, middle, g_ffn)
    grad_mid_part, grad_g_ffn = norm_back(grad_mixer)
    grad_middle = grad_state + grad_mid_part
    grad_middle_low = grad_middle.astype(jnp.bfloat16)
    grad_wout = jnp.dot(attended.T, grad_middle_low, preferred_element_type=jnp.float32)
    attended_gradient = jnp.dot(
        grad_middle_low, w_out.T, preferred_element_type=jnp.float32
    ).astype(jnp.bfloat16)
    attended_gradient = attended_gradient.reshape(
        local_rows, KEY_VALUE_HEADS, query_group_size, HEAD_SIZE
    )
    scores = score_block(query_copy, key_b, allowed)
    probs = jnp.exp(scores - log_total)
    probs_b = probs.astype(jnp.bfloat16)
    grad_probs = jnp.einsum(
        "tgjd,sgd->gjts", attended_gradient, value_b, preferred_element_type=jnp.float32
    )
    value_gradient = jnp.einsum(
        "gjts,tgjd->sgd", probs_b, attended_gradient, preferred_element_type=jnp.float32
    )
    value_gradient_copy = value_gradient.astype(jnp.bfloat16).reshape(
        local_rows, KEY_VALUE_HEADS * HEAD_SIZE
    )
    grad_scores = (
        probs * (grad_probs - jnp.sum(grad_probs * probs, axis=-1, keepdims=True))
    ).astype(jnp.bfloat16)
    grad_query = (
        jnp.einsum("gjts,sgd->tgjd", grad_scores, key_b, preferred_element_type=jnp.float32) * scale
    )
    query_grouped = query_copy.reshape(local_rows, KEY_VALUE_HEADS, query_group_size, HEAD_SIZE)
    grad_key = (
        jnp.einsum("gjts,tgjd->sgd", grad_scores, query_grouped, preferred_element_type=jnp.float32)
        * scale
    )
    unused_heads, head_back = jax.vjp(
        partial(head_piece, cosine=cosine, sine=sine), query_pre, prerotation_key, g_query, g_key
    )
    grad_qpre, prekey_gradient, grad_gq, grad_gk = head_back(
        (grad_query.reshape(local_rows, QUERY_HEADS, HEAD_SIZE), grad_key)
    )
    grad_qpre_b = grad_qpre.astype(jnp.bfloat16).reshape(local_rows, QUERY_HEADS * HEAD_SIZE)
    prekey_gradient_copy = prekey_gradient.astype(jnp.bfloat16).reshape(
        local_rows, KEY_VALUE_HEADS * HEAD_SIZE
    )
    grad_wquery = jnp.dot(normalized_input.T, grad_qpre_b, preferred_element_type=jnp.float32)
    grad_wkey = jnp.dot(
        normalized_input.T, prekey_gradient_copy, preferred_element_type=jnp.float32
    )
    grad_wvalue = jnp.dot(
        normalized_input.T, value_gradient_copy, preferred_element_type=jnp.float32
    )
    grad_normed = jnp.dot(grad_qpre_b, w_query.T, preferred_element_type=jnp.float32)
    grad_normed = grad_normed + jnp.dot(
        prekey_gradient_copy, key_weight.T, preferred_element_type=jnp.float32
    )
    grad_normed = grad_normed + jnp.dot(
        value_gradient_copy, value_weight.T, preferred_element_type=jnp.float32
    )
    unused_state, norm_front = jax.vjp(norm_rows, state, g_attn)
    grad_in_part, grad_g_attn = norm_front(grad_normed)
    grad_input = grad_middle + grad_in_part
    grad_gains = jnp.concatenate([grad_g_attn, grad_g_ffn, grad_gq, grad_gk])
    dense_grads = (grad_wquery, grad_wkey, grad_wvalue, grad_wout, grad_router, grad_gains)
    expert_grads = (grad_wgate, grad_wup, grad_down)
    return (grad_input, dense_grads, expert_grads)


def shards(
    tokens,
    cotangent,
    lengths,
    routes,
    gains,
    w_query,
    key_weight,
    value_weight,
    w_out,
    w_router,
    w_gate,
    w_up,
    w_down,
):
    local_rows = tokens.shape[0]
    peers = lax.axis_size("expert")
    cosine, sine, allowed = geometry(lengths, local_rows)
    state = tokens.astype(jnp.float32)
    memos = []
    for number in range(DECODER_LAYERS):
        dense = (
            lax.all_gather(w_query[number], ("fsdp", "expert"), axis=0, tiled=True),
            lax.all_gather(key_weight[number], ("fsdp", "expert"), axis=0, tiled=True),
            lax.all_gather(value_weight[number], ("fsdp", "expert"), axis=0, tiled=True),
            lax.all_gather(w_out[number], ("fsdp", "expert"), axis=0, tiled=True),
            lax.all_gather(w_router[number], ("fsdp", "expert"), axis=0, tiled=True),
            lax.all_gather(gains[number], ("fsdp", "expert"), axis=0, tiled=True),
        )
        experts = (
            lax.all_gather(w_gate[number], "fsdp", axis=1, tiled=True),
            lax.all_gather(w_up[number], "fsdp", axis=1, tiled=True),
            lax.all_gather(w_down[number], "fsdp", axis=2, tiled=True),
        )
        state, memo = layer_forward(
            state, dense, experts, routes[number], cosine, sine, allowed, peers
        )
        memos.append(memo)
    result = state.astype(jnp.bfloat16)
    grad_state = cotangent.astype(jnp.float32)
    dense_list = []
    expert_list = []
    for number in reversed(range(DECODER_LAYERS)):
        dense = (
            lax.all_gather(w_query[number], ("fsdp", "expert"), axis=0, tiled=True),
            lax.all_gather(key_weight[number], ("fsdp", "expert"), axis=0, tiled=True),
            lax.all_gather(value_weight[number], ("fsdp", "expert"), axis=0, tiled=True),
            lax.all_gather(w_out[number], ("fsdp", "expert"), axis=0, tiled=True),
            lax.all_gather(w_router[number], ("fsdp", "expert"), axis=0, tiled=True),
            lax.all_gather(gains[number], ("fsdp", "expert"), axis=0, tiled=True),
        )
        experts = (
            lax.all_gather(w_gate[number], "fsdp", axis=1, tiled=True),
            lax.all_gather(w_up[number], "fsdp", axis=1, tiled=True),
            lax.all_gather(w_down[number], "fsdp", axis=2, tiled=True),
        )
        grad_state, dense_grads, expert_grads = layer_backward(
            grad_state, memos[number], dense, experts, routes[number], cosine, sine, allowed, peers
        )
        dense_shards = (
            lax.psum_scatter(dense_grads[0], ("fsdp", "expert"), scatter_dimension=0, tiled=True),
            lax.psum_scatter(dense_grads[1], ("fsdp", "expert"), scatter_dimension=0, tiled=True),
            lax.psum_scatter(dense_grads[2], ("fsdp", "expert"), scatter_dimension=0, tiled=True),
            lax.psum_scatter(dense_grads[3], ("fsdp", "expert"), scatter_dimension=0, tiled=True),
            lax.psum_scatter(dense_grads[4], ("fsdp", "expert"), scatter_dimension=0, tiled=True),
            lax.psum_scatter(dense_grads[5], ("fsdp", "expert"), scatter_dimension=0, tiled=True),
        )
        expert_shards = (
            lax.psum_scatter(
                expert_grads[0].astype(jnp.bfloat16), "fsdp", scatter_dimension=1, tiled=True
            ).astype(jnp.float32),
            lax.psum_scatter(
                expert_grads[1].astype(jnp.bfloat16), "fsdp", scatter_dimension=1, tiled=True
            ).astype(jnp.float32),
            lax.psum_scatter(
                expert_grads[2].astype(jnp.bfloat16), "fsdp", scatter_dimension=2, tiled=True
            ).astype(jnp.float32),
        )
        dense_list.insert(0, dense_shards)
        expert_list.insert(0, expert_shards)
    d_gains = jnp.stack([entry[5] for entry in dense_list])
    d_query = jnp.stack([entry[0] for entry in dense_list])
    d_key = jnp.stack([entry[1] for entry in dense_list])
    d_value = jnp.stack([entry[2] for entry in dense_list])
    d_out = jnp.stack([entry[3] for entry in dense_list])
    d_router = jnp.stack([entry[4] for entry in dense_list])
    d_gate = jnp.stack([entry[0] for entry in expert_list])
    d_up = jnp.stack([entry[1] for entry in expert_list])
    d_down = jnp.stack([entry[2] for entry in expert_list])
    return (
        result,
        grad_state.astype(jnp.bfloat16),
        d_gains,
        d_query,
        d_key,
        d_value,
        d_out,
        d_router,
        d_gate,
        d_up,
        d_down,
    )


def solution(mesh):
    return jax.shard_map(
        shards,
        mesh=mesh,
        in_specs=(
            P(("fsdp", "expert"), None),
            P(("fsdp", "expert"), None),
            P(("fsdp", "expert"), None),
            P(None, ("fsdp", "expert"), None),
            P(None, ("fsdp", "expert")),
            P(None, ("fsdp", "expert"), None),
            P(None, ("fsdp", "expert"), None),
            P(None, ("fsdp", "expert"), None),
            P(None, ("fsdp", "expert"), None),
            P(None, ("fsdp", "expert"), None),
            P(None, "expert", "fsdp", None),
            P(None, "expert", "fsdp", None),
            P(None, "expert", None, "fsdp"),
        ),
        out_specs=(
            P(("fsdp", "expert"), None),
            P(("fsdp", "expert"), None),
            P(None, ("fsdp", "expert")),
            P(None, ("fsdp", "expert"), None),
            P(None, ("fsdp", "expert"), None),
            P(None, ("fsdp", "expert"), None),
            P(None, ("fsdp", "expert"), None),
            P(None, ("fsdp", "expert"), None),
            P(None, "expert", "fsdp", None),
            P(None, "expert", "fsdp", None),
            P(None, "expert", None, "fsdp"),
        ),
        check_vma=False,
    )
```

profile of v0, /device:TPU:0, one launch (start us, length us, event | category | flops | bytes accessed | tf_op | source)
XLA Modules:
  0.0 5206.8 jit_solution(16427540166503404725)
XLA Ops:
  37.0 42.6 all-reduce.13
  94.1 35.7 all-gather.35.cloned.1.call-done
  133.0 114.1 %all-gather.37.cloned.1.call-done = bf16[1,2048,4096]{2,1,0:T(8,128)(2,1)} async-done(((bf16[1,64,4096]{2,1,0:T(8,128)(2,1)}), bf16[1,2048,4096]{2,1,0:T(8,128)(2,1)}) %all-gather.37.cloned.1.call-update) | async-done | bytes 16777232 | tf_op jit(solution)/shard_map/all_gather | solution.py:356
  263.7 100.0 %all-gather.39.cloned.1.call-done = bf16[1,4096,2048]{2,1,0:T(8,128)(2,1)} async-done(((bf16[1,128,2048]{2,1,0:T(8,128)(2,1)}), bf16[1,4096,2048]{2,1,0:T(8,128)(2,1)}) %all-gather.39.cloned.1.call-update) | async-done | bytes 16777232 | tf_op jit(solution)/shard_map/all_gather | solution.py:359
  387.7 99.0 %all-gather.41.cloned.1.call-done = bf16[1,4,2048,768]{3,2,1,0:T(8,128)(2,1)} async-done(((bf16[1,4,512,768]{3,2,1,0:T(8,128)(2,1)}), bf16[1,4,2048,768]{3,2,1,0:T(8,128)(2,1)}) %all-gather.41.cloned.1.call-update) | async-done | bytes 12582928 | tf_op jit(solution)/shard_map/all_gather | solution.py:364
  486.7 40.0 all-to-all-done
  538.8 72.1 %all-gather.43.cloned.1.call-done = bf16[1,4,2048,768]{3,2,1,0:T(8,128)(2,1)} async-done(((bf16[1,4,512,768]{3,2,1,0:T(8,128)(2,1)}), bf16[1,4,2048,768]{3,2,1,0:T(8,128)(2,1)}) %all-gather.43.cloned.1.call-update) | async-done | bytes 12582928 | tf_op jit(solution)/shard_map/all_gather | solution.py:365
  611.0 13.4 fusion.81
  624.4 110.8 %all-gather.45.cloned.1.call-done = bf16[1,4,768,2048]{3,2,1,0:T(8,128)(2,1)} async-done(((bf16[1,4,768,512]{3,2,1,0:T(8,128)(2,1)}), bf16[1,4,768,2048]{3,2,1,0:T(8,128)(2,1)}) %all-gather.45.cloned.1.call-update) | async-done | bytes 12582928 | tf_op jit(solution)/shard_map/all_gather | solution.py:366
  764.5 186.3 %all-gather.5 = bf16[1,2048,32]{2,0,1:T(2,128)(2,1)} all-gather(bf16[1,64,32]{2,0,1:T(2,128)(2,1)S(1)} %copy.598), channel_id=7, replica_groups=mesh['fsdp'=4,'expert'=8] {'fsdp','expert'}, dimensions={1}, use_global_device_ids=true | all-gather | bytes 135168 | tf_op jit(solution)/shard_map/all_gather | solution.py:360
  988.0 45.6 all-gather.51.cloned.1.call-done
  1049.8 100.5 %all-gather.53.cloned.1.call-done = bf16[1,4096,2048]{2,1,0:T(8,128)(2,1)} async-done(((bf16[1,128,2048]{2,1,0:T(8,128)(2,1)}), bf16[1,4096,2048]{2,1,0:T(8,128)(2,1)}) %all-gather.53.cloned.1.call-update) | async-done | bytes 16777232 | tf_op jit(solution)/shard_map/all_gather | solution.py:359
  1176.0 173.6 %all-gather.14 = bf16[1,2048,32]{2,0,1:T(2,128)(2,1)S(1)} all-gather(bf16[1,64,32]{2,0,1:T(2,128)(2,1)S(1)} %copy.600), channel_id=16, replica_groups=mesh['fsdp'=4,'expert'=8] {'fsdp','expert'}, dimensions={1}, use_global_device_ids=true | all-gather | bytes 135168 | tf_op jit(solution)/shard_map/all_gather | solution.py:360
  1412.4 111.2 %all-gather.59.cloned.1.call-done = bf16[1,4,768,2048]{3,2,1,0:T(8,128)(2,1)} async-done(((bf16[1,4,768,512]{3,2,1,0:T(8,128)(2,1)}), bf16[1,4,768,2048]{3,2,1,0:T(8,128)(2,1)}) %all-gather.59.cloned.1.call-update) | async-done | bytes 12582928 | tf_op jit(solution)/shard_map/all_gather | solution.py:366
  1523.6 16.1 fusion.73
  1551.2 13.6 fusion.46
  1589.8 125.4 %all-to-all-done.5 = bf16[8,192,2048]{2,1,0:T(8,128)(2,1)} async-done(((bf16[8,192,2048]{2,1,0:T(8,128)(2,1)}), bf16[8,192,2048]{2,1,0:T(8,128)(2,1)}, u32[]{:S(2)}, u32[]{:S(2)}) %all-to-all-start.5) | async-done | bytes 6291488 | tf_op jit(solution)/shard_map/all_to_all | solution.py:261
  1738.5 120.4 %all-to-all-done.3 = bf16[8,192,2048]{2,1,0:T(8,128)(2,1)} async-done(((bf16[8,192,2048]{2,1,0:T(8,128)(2,1)}), bf16[8,192,2048]{2,1,0:T(8,128)(2,1)}, u32[]{:S(2)}, u32[]{:S(2)}) %all-to-all-start.3) | async-done | bytes 6291488 | tf_op jit(solution)/shard_map/all_to_all | solution.py:151
  1883.1 12.8 fusion.148
  1931.6 12.9 fusion.4
  1959.4 144.6 %all_to_all.40 = bf16[8,192,2048]{2,1,0:T(8,128)(2,1)} all-to-all(bf16[8,192,2048]{2,1,0:T(8,128)(2,1)} %bitcast.614), channel_id=1, replica_groups=mesh['fsdp'=4,'expert'=8] {'expert'}, dimensions={0} | all-to-all | bytes 12582912 | tf_op jit(solution)/shard_map/all_to_all | solution.py:227
  2104.0 15.1 fusion.68
  2130.6 13.2 fusion.47
  2164.5 140.7 %all-to-all-done.7 = bf16[8,192,2048]{2,1,0:T(8,128)(2,1)} async-done(((bf16[8,192,2048]{2,1,0:T(8,128)(2,1)}), bf16[8,192,2048]{2,1,0:T(8,128)(2,1)}, u32[]{:S(2)}, u32[]{:S(2)}) %all-to-all-start.7) | async-done | bytes 6291488 | tf_op jit(solution)/shard_map/all_to_all | solution.py:261
  2305.2 12.6 gather_fusion.3
  2325.4 12.8 fusion.151
  2389.9 13.4 bitcast_convert_fusion.2
  2404.9 13.4 bitcast_convert_fusion.3
  2420.0 13.4 bitcast_convert_fusion.4
  2435.1 13.6 bitcast_convert_fusion.5
  2450.2 13.2 fusion.197
  2465.0 13.3 fusion.194
  2479.6 13.3 fusion.180
  2511.5 13.4 fusion.177
  2543.1 38.4 all-reduce.12
  2586.5 141.8 %reduce-scatter.29.cloned.1.call-done = f32[64,512]{1,0:T(8,128)} async-done(((f32[2048,512]{1,0:T(8,128)}), f32[64,512]{1,0:T(8,128)}) %reduce-scatter.29.cloned.1.call-update) | async-done | bytes 131088 | tf_op jit(solution)/shard_map/reduce_scatter | solution.py:396
  2730.0 140.3 %reduce-scatter.27.cloned.1.call-done = f32[64,512]{1,0:T(8,128)} async-done(((f32[2048,512]{1,0:T(8,128)}), f32[64,512]{1,0:T(8,128)}) %reduce-scatter.27.cloned.1.call-update) | async-done | bytes 131088 | tf_op jit(solution)/shard_map/reduce_scatter | solution.py:395
  2870.3 141.8 %reduce-scatter.25.cloned.1.call-done = f32[64,512]{1,0:T(8,128)} async-done(((f32[2048,512]{1,0:T(8,128)}), f32[64,512]{1,0:T(8,128)}) %reduce-scatter.25.cloned.1.call-update) | async-done | bytes 131088 | tf_op jit(solution)/shard_map/reduce_scatter | solution.py:395
  3013.8 119.8 %reduce-scatter.47.cloned.1.call-done = bf16[4,768,512]{2,1,0:T(8,128)(2,1)} async-done(((bf16[4,768,2048]{2,1,0:T(8,128)(2,1)}), bf16[4,768,512]{2,1,0:T(8,128)(2,1)}) %reduce-scatter.47.cloned.1.call-update) | async-done | bytes 3145744 | tf_op jit(solution)/shard_map/reduce_scatter | solution.py:408
  3133.6 123.9 %reduce-scatter.45.cloned.1.call-done = bf16[4,768,512]{2,1,0:T(8,128)(2,1)} async-done(((bf16[4,768,2048]{2,1,0:T(8,128)(2,1)}), bf16[4,768,512]{2,1,0:T(8,128)(2,1)}) %reduce-scatter.45.cloned.1.call-update) | async-done | bytes 3145744 | tf_op jit(solution)/shard_map/reduce_scatter | solution.py:408
  3265.9 116.0 %reduce-scatter.43.cloned.1.call-done = bf16[4,512,768]{2,1,0:T(8,128)(2,1)} async-done(((bf16[4,2048,768]{2,1,0:T(8,128)(2,1)}), bf16[4,512,768]{2,1,0:T(8,128)(2,1)}) %reduce-scatter.43.cloned.1.call-update) | async-done | bytes 3145744 | tf_op jit(solution)/shard_map/reduce_scatter | solution.py:405
  3381.9 123.7 %reduce-scatter.41.cloned.1.call-done = bf16[4,512,768]{2,1,0:T(8,128)(2,1)} async-done(((bf16[4,2048,768]{2,1,0:T(8,128)(2,1)}), bf16[4,512,768]{2,1,0:T(8,128)(2,1)}) %reduce-scatter.41.cloned.1.call-update) | async-done | bytes 3145744 | tf_op jit(solution)/shard_map/reduce_scatter | solution.py:405
  3514.1 116.0 %reduce-scatter.39.cloned.1.call-done = bf16[4,512,768]{2,1,0:T(8,128)(2,1)} async-done(((bf16[4,2048,768]{2,1,0:T(8,128)(2,1)}), bf16[4,512,768]{2,1,0:T(8,128)(2,1)}) %reduce-scatter.39.cloned.1.call-update) | async-done | bytes 3145744 | tf_op jit(solution)/shard_map/reduce_scatter | solution.py:402
  3630.1 123.7 %reduce-scatter.37.cloned.1.call-done = bf16[4,512,768]{2,1,0:T(8,128)(2,1)} async-done(((bf16[4,2048,768]{2,1,0:T(8,128)(2,1)}), bf16[4,512,768]{2,1,0:T(8,128)(2,1)}) %reduce-scatter.37.cloned.1.call-update) | async-done | bytes 3145744 | tf_op jit(solution)/shard_map/reduce_scatter | solution.py:402
  3762.3 354.7 %reduce-scatter.35.cloned.1.call-done = f32[128,2048]{1,0:T(8,128)} async-done(((f32[4096,2048]{1,0:T(8,128)}), f32[128,2048]{1,0:T(8,128)}) %reduce-scatter.35.cloned.1.call-update) | async-done | bytes 1048592 | tf_op jit(solution)/shard_map/reduce_scatter | solution.py:397
  4117.0 360.0 %reduce-scatter.33.cloned.1.call-done = f32[128,2048]{1,0:T(8,128)} async-done(((f32[4096,2048]{1,0:T(8,128)}), f32[128,2048]{1,0:T(8,128)}) %reduce-scatter.33.cloned.1.call-update) | async-done | bytes 1048592 | tf_op jit(solution)/shard_map/reduce_scatter | solution.py:397
  4480.1 356.8 %reduce-scatter.23.cloned.1.call-done = f32[64,4096]{1,0:T(8,128)} async-done(((f32[2048,4096]{1,0:T(8,128)}), f32[64,4096]{1,0:T(8,128)}) %reduce-scatter.23.cloned.1.call-update) | async-done | bytes 1048592 | tf_op jit(solution)/shard_map/reduce_scatter | solution.py:394
  4836.9 359.8 %reduce-scatter.21.cloned.1.call-done = f32[64,4096]{1,0:T(8,128)} async-done(((f32[2048,4096]{1,0:T(8,128)}), f32[64,4096]{1,0:T(8,128)}) %reduce-scatter.21.cloned.1.call-update) | async-done | bytes 1048592 | tf_op jit(solution)/shard_map/reduce_scatter | solution.py:394
  (631 shorter events, 580.6 us)
Async XLA Ops:
  7.2 84.1 %all-gather.33.cloned.1.call-start = ((), (), s32[]{:S(2)}) async-start(), calls=%async_computation.38 | async-start | bytes 2162688 | tf_op jit(solution)/shard_map/all_gather | solution.py:358
  8.8 121.0 %all-gather.35.cloned.1.call-start = ((), (), s32[]{:S(2)}) async-start(), calls=%async_computation.39 | async-start | bytes 2162688 | tf_op jit(solution)/shard_map/all_gather | solution.py:357
  10.4 236.8 %all-gather.37.cloned.1.call-start = ((), (), s32[]{:S(2)}) async-start(), calls=%async_computation.40 | async-start | bytes 17301504 | tf_op jit(solution)/shard_map/all_gather | solution.py:356
  12.7 351.0 %all-gather.39.cloned.1.call-start = ((), (), s32[]{:S(2)}) async-start(), calls=%async_computation.41 | async-start | bytes 17301504 | tf_op jit(solution)/shard_map/all_gather | solution.py:359
  15.1 471.6 %all-gather.41.cloned.1.call-start = ((), (), s32[]{:S(2)}) async-start(), calls=%async_computation.42 | async-start | bytes 15728640 | tf_op jit(solution)/shard_map/all_gather | solution.py:364
  21.1 589.9 %all-gather.43.cloned.1.call-start = ((), (), s32[]{:S(2)}) async-start(), calls=%async_computation.43 | async-start | bytes 15728640 | tf_op jit(solution)/shard_map/all_gather | solution.py:365
  27.1 708.1 %all-gather.45.cloned.1.call-start = ((), (), s32[]{:S(2)}) async-start(), calls=%async_computation.44 | async-start | bytes 15728640 | tf_op jit(solution)/shard_map/all_gather | solution.py:366
  33.1 948.1 %all-gather.47.cloned.1.call-start = ((), (), s32[]{:S(2)}) async-start(), calls=%async_computation.45 | async-start | bytes 2162688 | tf_op jit(solution)/shard_map/all_gather | solution.py:358
  33.8 950.8 %all-gather.49.cloned.1.call-start = ((), (), s32[]{:S(2)}) async-start(), calls=%async_computation.46 | async-start | bytes 2162688 | tf_op jit(solution)/shard_map/all_gather | solution.py:357
  34.5 999.0 %all-gather.51.cloned.1.call-start = ((), (), s32[]{:S(2)}) async-start(), calls=%async_computation.47 | async-start | bytes 17301504 | tf_op jit(solution)/shard_map/all_gather | solution.py:356
  35.1 1115.1 %all-gather.53.cloned.1.call-start = ((), (), s32[]{:S(2)}) async-start(), calls=%async_computation.48 | async-start | bytes 17301504 | tf_op jit(solution)/shard_map/all_gather | solution.py:359
  35.9 1340.6 %all-gather.57.cloned.1.call-start = ((), (), s32[]{:S(2)}) async-start(), calls=%async_computation.50 | async-start | bytes 15728640 | tf_op jit(solution)/shard_map/all_gather | solution.py:365
  79.7 176.9 %copy-start.127 = (f32[128]{0:T(128)}, f32[128]{0:T(128)S(1)}, u32[]{:S(2)}) copy-start(f32[128]{0:T(128)S(1)} %get-tuple-element.90) | copy-start | bytes 1540
  79.7 167.5 %copy-start.60 = (f32[1,2048]{1,0:T(1,128)}, f32[1,2048]{1,0:T(1,128)S(1)}, u32[]{:S(2)}) copy-start(f32[1,2048]{1,0:T(1,128)S(1)} %get-tuple-element.88) | copy-start | bytes 24580
  79.7 292.6 %copy-start.96 = (f32[1,2048]{1,0:T(1,128)}, f32[1,2048]{1,0:T(1,128)S(1)}, u32[]{:S(2)}) copy-start(f32[1,2048]{1,0:T(1,128)S(1)} %get-tuple-element.87) | copy-start | bytes 24580
  81.1 166.1 %copy-start.102 = (f32[128]{0:T(128)}, f32[128]{0:T(128)S(1)}, u32[]{:S(2)}) copy-start(f32[128]{0:T(128)S(1)} %fusion.233) | copy-start | bytes 1540
  91.2 955.0 %copy-start.48 = (f32[128,64]{1,0:T(8,128)}, f32[128,64]{1,0:T(8,128)S(1)}, u32[]{:S(2)}) copy-start(f32[128,64]{1,0:T(8,128)S(1)} %get-tuple-element.97) | copy-start | bytes 98308
  91.2 955.0 %copy-start.51 = (f32[128,64]{1,0:T(8,128)}, f32[128,64]{1,0:T(8,128)S(1)}, u32[]{:S(2)}) copy-start(f32[128,64]{1,0:T(8,128)S(1)} %get-tuple-element.98) | copy-start | bytes 98308
  91.3 861.9 %copy-start.118 = (s32[1024,1]{0,1:T(1,128)}, s32[1024,1]{0,1:T(1,128)S(1)}, u32[]{:S(2)}) copy-start(s32[1024,1]{0,1:T(1,128)S(1)} %compare_select_fusion.3) | copy-start | bytes 12292
  372.3 608.4 %copy-start.12 = (f32[128,2048]{1,0:T(8,128)}, f32[128,2048]{1,0:T(8,128)S(1)}, u32[]{:S(2)}) copy-start(f32[128,2048]{1,0:T(8,128)S(1)} %get-tuple-element.102) | copy-start | bytes 3145732
  372.5 580.8 %copy-start.40 = (bf16[128,2048]{1,0:T(8,128)(2,1)}, bf16[128,2048]{1,0:T(8,128)(2,1)S(1)}, u32[]{:S(2)}) copy-start(bf16[128,2048]{1,0:T(8,128)(2,1)S(1)} %multiply_convert_fusion.2) | copy-start | bytes 1572868
  382.9 143.8 %all-to-all-start = ((bf16[8,192,2048]{2,1,0:T(8,128)(2,1)}), bf16[8,192,2048]{2,1,0:T(8,128)(2,1)}, u32[]{:S(2)}, u32[]{:S(2)}) async-start(bf16[8,192,2048]{2,1,0:T(8,128)(2,1)} %bitcast.613), calls=%async_computation | async-start | bytes 12582912 | tf_op jit(solution)/shard_map/all_to_all | solution.py:137
  748.7 212.8 %all-to-all-start.1 = ((bf16[8,192,2048]{2,1,0:T(8,128)(2,1)}), bf16[8,192,2048]{2,1,0:T(8,128)(2,1)}, u32[]{:S(2)}, u32[]{:S(2)}) async-start(bf16[8,192,2048]{2,1,0:T(8,128)(2,1)} %bitcast.607), calls=%async_computation.1 | async-start | bytes 12582912 | tf_op jit(solution)/shard_map/all_to_all | solution.py:151
  753.7 646.6 %all-gather.55.cloned.1.call-start = ((), (), s32[]{:S(2)}) async-start(), calls=%async_computation.49 | async-start | bytes 15728640 | tf_op jit(solution)/shard_map/all_gather | solution.py:364
  980.9 169.3 %copy-start.14 = (f32[128,2048]{1,0:T(8,128)}, f32[128,2048]{1,0:T(8,128)S(1)}, u32[]{:S(2)}) copy-start(f32[128,2048]{1,0:T(8,128)S(1)} %get-tuple-element.37) | copy-start | bytes 3145732
  1170.4 201.0 %all-to-all-start.2 = ((bf16[8,192,2048]{2,1,0:T(8,128)(2,1)}), bf16[8,192,2048]{2,1,0:T(8,128)(2,1)}, u32[]{:S(2)}, u32[]{:S(2)}) async-start(bf16[8,192,2048]{2,1,0:T(8,128)(2,1)} %bitcast.609), calls=%async_computation.2 | async-start | bytes 12582912 | tf_op jit(solution)/shard_map/all_to_all | solution.py:137
  1175.2 348.4 %all-gather.59.cloned.1.call-start = ((), (), s32[]{:S(2)}) async-start(), calls=%async_computation.51 | async-start | bytes 15728640 | tf_op jit(solution)/shard_map/all_gather | solution.py:366
  1371.4 152.2 %all-to-all-start.4 = ((bf16[8,192,2048]{2,1,0:T(8,128)(2,1)}), bf16[8,192,2048]{2,1,0:T(8,128)(2,1)}, u32[]{:S(2)}, u32[]{:S(2)}) async-start(bf16[8,192,2048]{2,1,0:T(8,128)(2,1)} %bitcast.610), calls=%async_computation.4 | async-start | bytes 12582912 | tf_op jit(solution)/shard_map/all_to_all | solution.py:227
  1571.5 143.7 %all-to-all-start.5 = ((bf16[8,192,2048]{2,1,0:T(8,128)(2,1)}), bf16[8,192,2048]{2,1,0:T(8,128)(2,1)}, u32[]{:S(2)}, u32[]{:S(2)}) async-start(bf16[8,192,2048]{2,1,0:T(8,128)(2,1)} %bitcast.612), calls=%async_computation.5 | async-start | bytes 12582912 | tf_op jit(solution)/shard_map/all_to_all | solution.py:261
  1715.2 143.7 %all-to-all-start.3 = ((bf16[8,192,2048]{2,1,0:T(8,128)(2,1)}), bf16[8,192,2048]{2,1,0:T(8,128)(2,1)}, u32[]{:S(2)}, u32[]{:S(2)}) async-start(bf16[8,192,2048]{2,1,0:T(8,128)(2,1)} %bitcast.611), calls=%async_computation.3 | async-start | bytes 12582912 | tf_op jit(solution)/shard_map/all_to_all | solution.py:151
  2150.4 154.8 %all-to-all-start.7 = ((bf16[8,192,2048]{2,1,0:T(8,128)(2,1)}), bf16[8,192,2048]{2,1,0:T(8,128)(2,1)}, u32[]{:S(2)}, u32[]{:S(2)}) async-start(bf16[8,192,2048]{2,1,0:T(8,128)(2,1)} %bitcast.608), calls=%async_computation.7 | async-start | bytes 12582912 | tf_op jit(solution)/shard_map/all_to_all | solution.py:261
  2155.3 370.3 %reduce-scatter.51.cloned.1.call-start = ((), (), s32[]{:S(2)}) async-start(), calls=%async_computation.53 | async-start | bytes 1081344
  2156.8 369.7 %reduce-scatter.49.cloned.1.call-start = ((), (), s32[]{:S(2)}) async-start(), calls=%async_computation.52 | async-start | bytes 1081344
  2161.6 143.6 %copy-start.106 = (s32[1024]{0:T(1024)S(1)}, s32[1024]{0:T(1024)}, u32[]{:S(2)}) copy-start(s32[1024]{0:T(1024)} %copy-done.105) | copy-start | bytes 12292
  2161.7 424.8 %reduce-scatter.31.cloned.1.call-start = ((), (), s32[]{:S(2)}) async-start(), calls=%async_computation.29 | async-start | bytes 4325376 | tf_op jit(solution)/shard_map/reduce_scatter | solution.py:396
  2164.5 563.8 %reduce-scatter.29.cloned.1.call-start = ((), (), s32[]{:S(2)}) async-start(), calls=%async_computation.28 | async-start | bytes 4325376 | tf_op jit(solution)/shard_map/reduce_scatter | solution.py:396
  2350.1 520.2 %reduce-scatter.27.cloned.1.call-start = ((), (), s32[]{:S(2)}) async-start(), calls=%async_computation.27 | async-start | bytes 4325376 | tf_op jit(solution)/shard_map/reduce_scatter | solution.py:395
  2353.4 658.7 %reduce-scatter.25.cloned.1.call-start = ((), (), s32[]{:S(2)}) async-start(), calls=%async_computation.26 | async-start | bytes 4325376 | tf_op jit(solution)/shard_map/reduce_scatter | solution.py:395
  2360.0 773.6 %reduce-scatter.47.cloned.1.call-start = ((), (), s32[]{:S(2)}) async-start(), calls=%async_computation.37 | async-start | bytes 15728640 | tf_op jit(solution)/shard_map/reduce_scatter | solution.py:408
  2374.1 883.3 %reduce-scatter.45.cloned.1.call-start = ((), (), s32[]{:S(2)}) async-start(), calls=%async_computation.36 | async-start | bytes 15728640 | tf_op jit(solution)/shard_map/reduce_scatter | solution.py:408
  2388.2 993.7 %reduce-scatter.43.cloned.1.call-start = ((), (), s32[]{:S(2)}) async-start(), calls=%async_computation.35 | async-start | bytes 15728640 | tf_op jit(solution)/shard_map/reduce_scatter | solution.py:405
  2403.3 1102.4 %reduce-scatter.41.cloned.1.call-start = ((), (), s32[]{:S(2)}) async-start(), calls=%async_computation.34 | async-start | bytes 15728640 | tf_op jit(solution)/shard_map/reduce_scatter | solution.py:405
  2418.4 1211.7 %reduce-scatter.39.cloned.1.call-start = ((), (), s32[]{:S(2)}) async-start(), calls=%async_computation.33 | async-start | bytes 15728640 | tf_op jit(solution)/shard_map/reduce_scatter | solution.py:402
  2433.4 1320.4 %reduce-scatter.37.cloned.1.call-start = ((), (), s32[]{:S(2)}) async-start(), calls=%async_computation.32 | async-start | bytes 15728640 | tf_op jit(solution)/shard_map/reduce_scatter | solution.py:402
  2448.6 1668.4 %reduce-scatter.35.cloned.1.call-start = ((), (), s32[]{:S(2)}) async-start(), calls=%async_computation.31 | async-start | bytes 34603008 | tf_op jit(solution)/shard_map/reduce_scatter | solution.py:397
  2463.4 2013.5 %reduce-scatter.33.cloned.1.call-start = ((), (), s32[]{:S(2)}) async-start(), calls=%async_computation.30 | async-start | bytes 34603008 | tf_op jit(solution)/shard_map/reduce_scatter | solution.py:397
  2478.2 2358.7 %reduce-scatter.23.cloned.1.call-start = ((), (), s32[]{:S(2)}) async-start(), calls=%async_computation.25 | async-start | bytes 34603008 | tf_op jit(solution)/shard_map/reduce_scatter | solution.py:394
  2493.0 2703.7 %reduce-scatter.21.cloned.1.call-start = ((), (), s32[]{:S(2)}) async-start(), calls=%async_computation.24 | async-start | bytes 34603008 | tf_op jit(solution)/shard_map/reduce_scatter | solution.py:394
  (141 other events, 1745.9 us)
Sparse Core Ops, SparseCore 0:
  11.6 59.1 all-gather.32
  74.4 55.3 all-gather.34
  133.4 113.7 all-gather.36
  250.6 113.0 all-gather.38
  366.0 120.6 all-gather.40
  488.4 122.5 all-gather.42
  612.8 122.3 all-gather.44
  738.2 77.4 all-gather.46
  819.2 93.0 all-gather.48
  915.7 117.8 all-gather.50
  1037.1 113.0 all-gather.52
  1151.9 120.6 all-gather.56
  1274.5 125.6 all-gather.54
  1401.9 121.6 all-gather.58
  2158.1 151.7 reduce-scatter.50
  2312.1 133.2 reduce-scatter.48
  2447.5 138.8 reduce-scatter.30
  2588.6 139.6 reduce-scatter.28
  2730.6 139.7 reduce-scatter.26
  2872.4 139.6 reduce-scatter.24
  3015.8 117.7 reduce-scatter.46
  3136.7 120.7 reduce-scatter.44
  3261.2 120.7 reduce-scatter.42
  3384.9 120.7 reduce-scatter.40
  3509.3 120.7 reduce-scatter.38
  3633.0 120.7 reduce-scatter.36
  3755.9 361.0 reduce-scatter.34
  4119.3 357.6 reduce-scatter.32
  4479.3 357.5 reduce-scatter.22
  4839.1 357.5 reduce-scatter.20
where the time goes:
time: 5220 us; the launch traced here: 5210 us
  waiting for transfers between devices  3810 us (73%)
  blocking collectives  586 us (11%)
  matrix products  418 us (8%)
  local copies, waits for them, and re-layouts  189 us (4%)
  other arithmetic  147 us (3%)
    reduce_scatter x2, waiting for transfers between devices, shards(): lax.psum_scatter(dense_grads[0], ('fsdp', 'expert'), scatter_dimension=0,...  717 us
    reduce_scatter x2, waiting for transfers between devices, shards(): lax.psum_scatter(dense_grads[3], ('fsdp', 'expert'), scatter_dimension=0,...  715 us
    all_gather x2, blocking collectives, shards(): lax.all_gather(w_router[number], ('fsdp', 'expert'), axis=0, tiled=True)  360 us
    reduce_scatter x2, waiting for transfers between devices, shards(): lax.psum_scatter(dense_grads[1], ('fsdp', 'expert'), scatter_dimension=0,...  282 us
    all_to_all x2, waiting for transfers between devices, layer_backward(): lax.all_to_all(grad_incoming, 'expert', split_axis=0, concat_axis=0, tile...  266 us
    reduce_scatter x2, waiting for transfers between devices, shards(): lax.psum_scatter(expert_grads[2].astype(jnp.bfloat16), 'fsdp', scatter_di...  244 us
    reduce_scatter x2, waiting for transfers between devices, shards(): lax.psum_scatter(expert_grads[1].astype(jnp.bfloat16), 'fsdp', scatter_di...  240 us
    reduce_scatter x2, waiting for transfers between devices, shards(): lax.psum_scatter(expert_grads[0].astype(jnp.bfloat16), 'fsdp', scatter_di...  240 us
  transfers between devices with their start and end apart: 37, of which 28 were waited for; matrix products, arithmetic and copies ran while one was open for 10% of the time, Pallas kernels for 0%

commit v1 on v0

--- a/solution.py
+++ b/solution.py
@@ -4,6 +4,9 @@
 import jax
 import jax.numpy as jnp
 from jax import lax
+from jax.experimental import pallas as pl
+from jax.experimental.pallas import tpu as pltpu
+from jax.sharding import Mesh
 from jax.sharding import PartitionSpec as P
 
 MODEL_WIDTH = 2048
@@ -435,7 +438,7 @@
     )
 
 
-def solution(mesh):
+def general(mesh):
     return jax.shard_map(
         shards,
         mesh=mesh,
@@ -469,3 +472,887 @@
         ),
         check_vma=False,
     )
+
+
+CHIPS = ("fsdp", "line")
+EVERY = ("fsdp", "line", "core")
+
+
+def swap(operand):
+    return lax.ppermute(operand, "core", [(0, 1), (1, 0)])
+
+
+def by_core(core, mine, other, axis):
+    return jnp.where(
+        core == 0,
+        jnp.concatenate([mine, other], axis=axis),
+        jnp.concatenate([other, mine], axis=axis),
+    )
+
+
+def turned(operand):
+    half_rows = operand.shape[0] // 2
+    return jnp.concatenate([operand[half_rows:], operand[:half_rows]], axis=0)
+
+
+def offload_gather(operand):
+    return lax.all_gather(operand, CHIPS, axis=0, tiled=True)
+
+
+def offload_scatter(operand):
+    return lax.psum_scatter(operand, CHIPS, scatter_dimension=0, tiled=True)
+
+
+PAIR = 4
+ROW_UNITS = 8
+
+
+def routes_of_shards(depth):
+    offsets = [s * k for k in range(1, depth) for s in (-1, 1)]
+
+    def source(offset):
+        return "below" if offset < 0 else "above"
+
+    def onward(offset):
+        return "above" if offset < 0 else "below"
+
+    def further(offset):
+        return offset - 1 if offset < 0 else offset + 1
+
+    def line_hops(bits, first, last, offset):
+        if offset == 0:
+            return [
+                ("above", first, last, (bits, -1, first, last, "below")),
+                ("below", first, last, (bits, 1, first, last, "above")),
+            ]
+        if abs(further(offset)) >= depth:
+            return []
+        return [(onward(offset), first, last, (bits, further(offset), first, last, source(offset)))]
+
+    plan = []
+    own = [("x", 0, 8, (1, 0, 0, 8, "x")), ("y", 0, 8, (2, 0, 0, 8, "y"))]
+    plan.append((None, own + line_hops(0, 0, 8, 0)))
+    plan.append(
+        ((1, 0, 0, 8, "x"), [("y", 3, 7, (3, 0, 3, 7, "y"))] + line_hops(1, 6, 8, 0))
+    )
+    plan.append(
+        (
+            (2, 0, 0, 8, "y"),
+            [("x", 0, 3, (3, 0, 0, 3, "x")), ("x", 7, 8, (3, 0, 7, 8, "x"))]
+            + line_hops(2, 6, 8, 0),
+        )
+    )
+
+    def spread(offset):
+        return (
+            (0, offset, 0, 8, source(offset)),
+            line_hops(0, 0, 8, offset)
+            + [("x", 0, 6, (1, offset, 0, 6, "x")), ("y", 0, 6, (2, offset, 0, 6, "y"))],
+        )
+
+    def crossed(offset):
+        return [
+            ((1, offset, 0, 6, "x"), [("y", 3, 6, (3, offset, 3, 6, "y"))]),
+            ((2, offset, 0, 6, "y"), [("x", 0, 3, (3, offset, 0, 3, "x"))]),
+        ]
+
+    def lined(offset):
+        return [
+            ((bits, offset, 6, 8, source(offset)), line_hops(bits, 6, 8, offset))
+            for bits in (1, 2, 3)
+        ]
+
+    def last(offset):
+        return [((3, offset, 3, 6, "y"), []), ((3, offset, 0, 3, "x"), [])]
+
+    steps = [(-k, k) for k in range(1, depth)]
+    plan += [spread(o) for o in steps[0]]
+    plan += [
+        ((3, 0, 3, 7, "y"), []),
+        ((3, 0, 0, 3, "x"), []),
+        ((3, 0, 7, 8, "x"), line_hops(3, 6, 8, 0)),
+    ]
+    for number, pair in enumerate(steps):
+        for offset in pair:
+            plan += crossed(offset)
+        if number + 1 < len(steps):
+            plan += [spread(o) for o in steps[number + 1]]
+        for offset in pair:
+            plan += lined(offset)
+        for offset in pair:
+            plan += last(offset)
+    return plan
+
+
+class Place:
+    def __init__(self, depth):
+        self.depth = depth
+        self.pair = lax.axis_index("fsdp")
+        self.line = lax.axis_index("line")
+        self.core = lax.axis_index("core")
+        x = lax.rem(self.pair, 2)
+        y = lax.div(self.pair, 2)
+        self.pairs = [
+            self.pair,
+            self.pair + 1 - 2 * x,
+            self.pair + 2 - 4 * y,
+            PAIR - 1 - self.pair,
+        ]
+
+    def shard(self, bits, offset):
+        return self.pairs[bits] * self.depth + self.line + offset
+
+    def device(self, neighbour):
+        if neighbour == "x":
+            return (self.pairs[1], self.line, self.core)
+        if neighbour == "y":
+            return (self.pairs[2], self.line, self.core)
+        step = 1 if neighbour == "above" else -1
+        return (self.pair, self.line + step, self.core)
+
+    def holds(self, offset, neighbour=None):
+        low, high = min(offset, 0), max(offset, 0)
+        if neighbour == "above":
+            high = max(high, 1)
+        if neighbour == "below":
+            low = min(low, -1)
+        tests = []
+        if low < 0:
+            tests.append(self.line >= -low)
+        if high > 0:
+            tests.append(self.line < self.depth - high)
+        if not tests:
+            return None
+        return tests[0] if len(tests) == 1 else jnp.logical_and(tests[0], tests[1])
+
+    def meet(self):
+        barrier = pltpu.get_barrier_semaphore()
+        for neighbour in ("x", "y", "above", "below"):
+
+            def greet(neighbour=neighbour):
+                pl.semaphore_signal(
+                    barrier,
+                    inc=1,
+                    device_id=self.device(neighbour),
+                    device_id_type=pl.DeviceIdType.MESH,
+                )
+
+            when(self.holds(0, neighbour), greet)
+        ends = (self.line == 0).astype(jnp.int32) + (self.line == self.depth - 1).astype(jnp.int32)
+        pl.semaphore_wait(barrier, 4 - ends)
+
+
+def when(test, action):
+    if test is None:
+        action()
+    else:
+        pl.when(test)(action)
+
+
+def gather_kernel(depth, x_ref, out_ref, own_sem, send_sems, recv_sems):
+    plan = routes_of_shards(depth)
+    number_of = {item: i for i, (item, _) in enumerate(plan)}
+    unit = x_ref.shape[0] // ROW_UNITS
+    here = Place(depth)
+    own = pltpu.make_async_copy(x_ref, out_ref.at[here.shard(0, 0)], own_sem)
+    own.start()
+    here.meet()
+    sent = []
+    for item, hops in plan:
+        bits, offset = (0, 0) if item is None else item[:2]
+
+        def step(item=item, hops=hops, bits=bits, offset=offset, site=len(sent)):
+            if item is not None:
+                piece = out_ref.at[
+                    here.shard(bits, offset), pl.ds(item[2] * unit, (item[3] - item[2]) * unit)
+                ]
+                pltpu.make_async_remote_copy(
+                    src_ref=piece,
+                    dst_ref=piece,
+                    send_sem=send_sems.at[0],
+                    recv_sem=recv_sems.at[number_of[item]],
+                    device_id=here.device("x"),
+                    device_id_type=pl.DeviceIdType.MESH,
+                ).wait_recv()
+            for hop, (neighbour, first, last, there) in enumerate(hops):
+                when(
+                    here.holds(0, neighbour) if neighbour in ("above", "below") else None,
+                    lambda n=neighbour, f=first, l=last, t=there, s=site + hop: passing(
+                        bits, offset, n, f, l, t, s, item is None
+                    ).start(),
+                )
+
+        def passing(bits, offset, neighbour, first, last, there, site, own_piece):
+            rows = pl.ds(first * unit, (last - first) * unit)
+            target = out_ref.at[here.shard(bits, offset), rows]
+            return pltpu.make_async_remote_copy(
+                src_ref=x_ref.at[rows] if own_piece else target,
+                dst_ref=target,
+                send_sem=send_sems.at[site],
+                recv_sem=recv_sems.at[number_of[there]],
+                device_id=here.device(neighbour),
+                device_id_type=pl.DeviceIdType.MESH,
+            )
+
+        when(None if item is None else here.holds(offset), step)
+        for neighbour, first, last, there in hops:
+            sent.append((bits, offset, neighbour, first, last, there, len(sent), item is None))
+    for bits, offset, neighbour, first, last, there, site, own_piece in sent:
+
+        def finish(a=(bits, offset, neighbour, first, last, there, site, own_piece)):
+            passing(*a).wait_send()
+
+        when(here.holds(offset, neighbour), finish)
+    own.wait()
+
+
+def count_plan(depth):
+    plan = routes_of_shards(depth)
+    return len(plan), sum(len(hops) for _, hops in plan)
+
+
+def gather_chips(operand, collective_id):
+    depth = lax.axis_size("line")
+    items, hops = count_plan(depth)
+    chips = PAIR * depth
+    rows, columns = operand.shape
+    return pl.pallas_call(
+        partial(gather_kernel, depth),
+        out_shape=jax.ShapeDtypeStruct((chips, rows, columns), operand.dtype),
+        in_specs=[pl.BlockSpec(memory_space=pl.ANY)],
+        out_specs=pl.BlockSpec(memory_space=pl.ANY),
+        scratch_shapes=[
+            pltpu.SemaphoreType.DMA,
+            pltpu.SemaphoreType.DMA((hops,)),
+            pltpu.SemaphoreType.DMA((items,)),
+        ],
+        compiler_params=pltpu.CompilerParams(collective_id=collective_id, has_side_effects=True),
+        cost_estimate=pl.CostEstimate(
+            flops=0, bytes_accessed=8 * chips * rows * columns, transcendentals=0
+        ),
+        name="gather_chips",
+    )(operand).reshape(chips * rows, columns)
+
+
+def scatter_kernel(depth, x_ref, out_ref, sums, landed, own_sem, send_sems, recv_sems):
+    plan = routes_of_shards(depth)
+    number_of = {item: i for i, (item, _) in enumerate(plan)}
+    unit = x_ref.shape[1] // ROW_UNITS
+    here = Place(depth)
+    own = pltpu.make_async_copy(x_ref, sums, own_sem)
+    own.start()
+    here.meet()
+    own.wait()
+    sites = {}
+    start = 0
+    for item, hops in plan:
+        for neighbour, first, last, there in hops:
+            sites[there] = (number_of[there] - 1, start)
+            start += (last - first) * unit
+
+    def total(shard, first, last, base):
+        @pl.loop(0, (last - first) * unit // 16)
+        def _(i):
+            rows = pl.ds(first * unit + i * 16, 16)
+            value = sums[shard, rows].astype(jnp.float32)
+            value = value + landed[pl.ds(base + i * 16, 16)].astype(jnp.float32)
+            sums[shard, rows] = value.astype(sums.dtype)
+
+    def sending(item):
+        bits, offset, first, last, neighbour = item
+        sem, base = sites[item]
+        size = (last - first) * unit
+        return pltpu.make_async_remote_copy(
+            src_ref=sums.at[here.shard(bits, offset), pl.ds(first * unit, size)],
+            dst_ref=landed.at[pl.ds(base, size)],
+            send_sem=send_sems.at[number_of[item]],
+            recv_sem=recv_sems.at[sem],
+            device_id=here.device(neighbour),
+            device_id_type=pl.DeviceIdType.MESH,
+        )
+
+    for item, hops in reversed(plan):
+        bits, offset = (0, 0) if item is None else item[:2]
+
+        def step(item=item, hops=hops, bits=bits, offset=offset):
+            for neighbour, first, last, there in hops:
+
+                def take(first=first, last=last, there=there):
+                    sem, base = sites[there]
+                    size = (last - first) * unit
+                    pltpu.make_async_remote_copy(
+                        src_ref=landed.at[pl.ds(base, size)],
+                        dst_ref=landed.at[pl.ds(base, size)],
+                        send_sem=send_sems.at[0],
+                        recv_sem=recv_sems.at[sem],
+                        device_id=here.device("x"),
+                        device_id_type=pl.DeviceIdType.MESH,
+                    ).wait_recv()
+                    total(here.shard(bits, offset), first, last, base)
+
+                when(
+                    here.holds(0, neighbour) if neighbour in ("above", "below") else None,
+                    take,
+                )
+            if item is not None:
+                sending(item).start()
+
+        when(None if item is None else here.holds(offset), step)
+    out_ref[...] = sums[here.shard(0, 0)]
+    for item, hops in plan:
+        if item is not None:
+            when(here.holds(item[1]), lambda item=item: sending(item).wait_send())
+
+
+def scatter_chips(operand, collective_id):
+    depth = lax.axis_size("line")
+    chips = PAIR * depth
+    items, hops = count_plan(depth)
+    rows, columns = operand.shape[0] // chips, operand.shape[1]
+    landed = sum(
+        (last - first) * rows // ROW_UNITS
+        for _, row in routes_of_shards(depth)
+        for _, first, last, _ in row
+    )
+    return pl.pallas_call(
+        partial(scatter_kernel, depth),
+        out_shape=jax.ShapeDtypeStruct((rows, columns), operand.dtype),
+        in_specs=[pl.BlockSpec(memory_space=pl.ANY)],
+        out_specs=pl.BlockSpec(memory_space=pltpu.VMEM),
+        scratch_shapes=[
+            pltpu.VMEM((chips, rows, columns), operand.dtype),
+            pltpu.VMEM((landed, columns), operand.dtype),
+            pltpu.SemaphoreType.DMA,
+            pltpu.SemaphoreType.DMA((items,)),
+            pltpu.SemaphoreType.DMA((hops,)),
+        ],
+        compiler_params=pltpu.CompilerParams(
+            collective_id=collective_id, has_side_effects=True, vmem_limit_bytes=50 * 2**20
+        ),
+        cost_estimate=pl.CostEstimate(
+            flops=0, bytes_accessed=8 * chips * rows * columns, transcendentals=0
+        ),
+        name="scatter_chips",
+    )(operand.reshape(chips, rows, columns))
+
+
+def spread_experts(operand, place, width):
+    own = lax.dynamic_index_in_dim(operand, place, 0, keepdims=False)
+    pieces = jnp.zeros_like(operand)
+    pieces = lax.dynamic_update_index_in_dim(pieces, own, place, 0)
+    for step in range(1, width):
+        sent = lax.dynamic_index_in_dim(operand, place ^ step, 0, keepdims=False)
+        got = lax.ppermute(sent, "fsdp", [(i, i ^ step) for i in range(width)])
+        pieces = lax.dynamic_update_index_in_dim(pieces, got, place ^ step, 0)
+    return pieces
+
+
+def spread_columns(operand, place, width):
+    columns = operand.shape[2]
+    own = lax.dynamic_index_in_dim(operand, place, 0, keepdims=False)
+    whole = jnp.zeros((operand.shape[1], width * columns), operand.dtype)
+    whole = lax.dynamic_update_slice_in_dim(whole, own, place * columns, 1)
+    for step in range(1, width):
+        sent = lax.dynamic_index_in_dim(operand, place ^ step, 0, keepdims=False)
+        got = lax.ppermute(sent, "fsdp", [(i, i ^ step) for i in range(width)])
+        whole = lax.dynamic_update_slice_in_dim(whole, got, (place ^ step) * columns, 1)
+    return whole
+
+
+def pair_scores(query_copy, key_b, allowed):
+    return jnp.where(
+        allowed[:, None, None],
+        jnp.einsum("btgjd,bsgd->bgjts", query_copy, key_b, preferred_element_type=jnp.float32)
+        * (1.0 / math.sqrt(HEAD_SIZE)),
+        -1e30,
+    )
+
+
+def attention_forward(state, dense, angles):
+    core, cosine, sine, allowed = angles
+    w_qkv, w_out, g_attn, g_query, g_key = dense
+    rows = state.shape[0]
+    heads = QUERY_HEADS // 2
+    pairs = KEY_VALUE_HEADS // 2
+    group = heads // KEY_VALUE_HEADS
+    normed = norm_rows(state, g_attn).astype(jnp.bfloat16)
+    normed = jnp.concatenate([normed, swap(normed)], axis=0)
+    qkv = jnp.dot(normed, w_qkv, preferred_element_type=jnp.float32)
+    query_pre = qkv[:, : heads * HEAD_SIZE].reshape(2 * rows, heads, HEAD_SIZE)
+    key_pre = qkv[:, heads * HEAD_SIZE : (heads + pairs) * HEAD_SIZE].reshape(
+        2 * rows, pairs, HEAD_SIZE
+    )
+    value_half = qkv[:, (heads + pairs) * HEAD_SIZE :].astype(jnp.bfloat16)
+    query_f, key_f = head_piece(query_pre, key_pre, g_query, g_key, cosine, sine)
+    query_b = query_f.astype(jnp.bfloat16).reshape(2, rows, KEY_VALUE_HEADS, group, HEAD_SIZE)
+    key_half = key_f.astype(jnp.bfloat16).reshape(2 * rows, pairs * HEAD_SIZE)
+    both = jnp.concatenate([key_half, value_half], axis=1)
+    other = turned(swap(both))
+    width = pairs * HEAD_SIZE
+    key_b = by_core(core, key_half, other[:, :width], 1)
+    value_b = by_core(core, value_half, other[:, width:], 1)
+    key_b = key_b.reshape(2, rows, KEY_VALUE_HEADS, HEAD_SIZE)
+    value_b = value_b.reshape(2, rows, KEY_VALUE_HEADS, HEAD_SIZE)
+    scores = pair_scores(query_b, key_b, allowed)
+    peaks = jnp.max(scores, axis=-1, keepdims=True)
+    expos = jnp.exp(scores - peaks)
+    totals = jnp.sum(expos, axis=-1, keepdims=True)
+    log_total = peaks + jnp.log(totals)
+    probs_b = (expos / totals).astype(jnp.bfloat16)
+    attended = jnp.einsum("bgjts,bsgd->btgjd", probs_b, value_b, preferred_element_type=jnp.float32)
+    attended = attended.reshape(2 * rows, heads * HEAD_SIZE).astype(jnp.bfloat16)
+    partial_out = jnp.dot(attended, w_out, preferred_element_type=jnp.float32)
+    middle = state + (partial_out[:rows] + swap(partial_out[rows:]))
+    return middle, (normed, query_pre, key_pre, query_b, key_b, value_b, log_total, attended)
+
+
+def attention_backward(grad_middle, memo, dense, angles):
+    core, cosine, sine, allowed = angles
+    normed, query_pre, key_pre, query_b, key_b, value_b, log_total, attended = memo
+    w_qkv, w_out, g_attn, g_query, g_key = dense
+    rows = grad_middle.shape[0]
+    heads = QUERY_HEADS // 2
+    pairs = KEY_VALUE_HEADS // 2
+    width = pairs * HEAD_SIZE
+    scale = 1.0 / math.sqrt(HEAD_SIZE)
+    low = grad_middle.astype(jnp.bfloat16)
+    low = jnp.concatenate([low, swap(low)], axis=0)
+    grad_attended = lax.dot_general(
+        low, w_out, (((1,), (1,)), ((), ())), preferred_element_type=jnp.float32
+    ).astype(jnp.bfloat16)
+    grad_wout = lax.dot_general(
+        attended, low, (((0,), (0,)), ((), ())), preferred_element_type=jnp.float32
+    ).astype(jnp.bfloat16)
+    grad_attended = grad_attended.reshape(query_b.shape)
+    probs = jnp.exp(pair_scores(query_b, key_b, allowed) - log_total)
+    probs_b = probs.astype(jnp.bfloat16)
+    grad_probs = jnp.einsum(
+        "btgjd,bsgd->bgjts", grad_attended, value_b, preferred_element_type=jnp.float32
+    )
+    grad_value = jnp.einsum(
+        "bgjts,btgjd->bsgd", probs_b, grad_attended, preferred_element_type=jnp.float32
+    ).reshape(2 * rows, 2 * width)
+    grad_scores = (
+        probs * (grad_probs - jnp.sum(grad_probs * probs, axis=-1, keepdims=True))
+    ).astype(jnp.bfloat16)
+    grad_query = (
+        jnp.einsum("bgjts,bsgd->btgjd", grad_scores, key_b, preferred_element_type=jnp.float32)
+        * scale
+    ).reshape(2 * rows, heads, HEAD_SIZE)
+    grad_key = (
+        jnp.einsum("bgjts,btgjd->bsgd", grad_scores, query_b, preferred_element_type=jnp.float32)
+        * scale
+    ).reshape(2 * rows, 2 * width)
+    mine = jnp.where(core == 0, 0, width)
+    theirs = width - mine
+    sent = jnp.concatenate(
+        [
+            lax.dynamic_slice_in_dim(grad_key, theirs, width, 1),
+            lax.dynamic_slice_in_dim(grad_value, theirs, width, 1),
+        ],
+        axis=1,
+    )
+    got = turned(swap(sent))
+    grad_key = lax.dynamic_slice_in_dim(grad_key, mine, width, 1) + got[:, :width]
+    grad_value = lax.dynamic_slice_in_dim(grad_value, mine, width, 1) + got[:, width:]
+    unused_heads, head_back = jax.vjp(
+        partial(head_piece, cosine=cosine, sine=sine), query_pre, key_pre, g_query, g_key
+    )
+    grad_qpre, grad_kpre, grad_gq, grad_gk = head_back(
+        (grad_query, grad_key.reshape(2 * rows, pairs, HEAD_SIZE))
+    )
+    grad_qkv = jnp.concatenate(
+        [
+            grad_qpre.astype(jnp.bfloat16).reshape(2 * rows, heads * HEAD_SIZE),
+            grad_kpre.astype(jnp.bfloat16).reshape(2 * rows, width),
+            grad_value.astype(jnp.bfloat16),
+        ],
+        axis=1,
+    )
+    grad_wqkv = lax.dot_general(
+        normed, grad_qkv, (((0,), (0,)), ((), ())), preferred_element_type=jnp.float32
+    ).astype(jnp.bfloat16)
+    grad_normed = lax.dot_general(
+        grad_qkv, w_qkv, (((1,), (1,)), ((), ())), preferred_element_type=jnp.float32
+    )
+    grad_normed = grad_normed[:rows] + swap(grad_normed[rows:])
+    return grad_normed, grad_wqkv, grad_wout, grad_gq, grad_gk
+
+
+def expert_forward(gathered, picks, row_gates, weights):
+    blocks = picks[0].shape[0]
+    width = gathered.shape[1]
+    grouped = gathered.reshape(blocks, -1, width)
+    memo = []
+    total = None
+    for pick, row_gate, (w_up_gate, w_down) in zip(picks, row_gates, weights):
+        hidden_size = w_down.shape[0]
+        rows = jnp.einsum("bst,btd->bsd", pick, grouped, preferred_element_type=jnp.float32)
+        rows = rows.astype(jnp.bfloat16).reshape(-1, width)
+        pre = jnp.dot(rows, w_up_gate, preferred_element_type=jnp.float32)
+        gate_pre = pre[:, :hidden_size]
+        up_pre = pre[:, hidden_size:]
+        hidden = (jax.nn.silu(gate_pre) * up_pre).astype(jnp.bfloat16)
+        produced = jnp.dot(hidden, w_down, preferred_element_type=jnp.float32)
+        produced = (produced * row_gate).astype(jnp.bfloat16)
+        back = jnp.einsum(
+            "bst,bsd->btd",
+            pick,
+            produced.reshape(blocks, -1, width),
+            preferred_element_type=jnp.float32,
+        )
+        total = back if total is None else total + back
+        memo.append((rows, gate_pre, up_pre, hidden))
+    return total.reshape(-1, width).astype(jnp.bfloat16), memo
+
+
+def expert_backward(gathered, picks, row_gates, weights, memo):
+    blocks = picks[0].shape[0]
+    width = gathered.shape[1]
+    grouped = gathered.reshape(blocks, -1, width)
+    total = None
+    grads = []
+    gate_grads = []
+    for pick, row_gate, (w_up_gate, w_down), kept in zip(picks, row_gates, weights, memo):
+        rows, gate_pre, up_pre, hidden = kept
+        grad_rows = jnp.einsum("bst,btd->bsd", pick, grouped, preferred_element_type=jnp.float32)
+        grad_rows = grad_rows.astype(jnp.bfloat16).reshape(-1, width)
+        through = lax.dot_general(
+            grad_rows, w_down, (((1,), (1,)), ((), ())), preferred_element_type=jnp.float32
+        )
+        hidden_f = hidden.astype(jnp.float32)
+        gate_grad = jnp.sum(hidden_f * through, axis=1)
+        gate_grads.append(
+            jnp.sum(
+                pick.astype(jnp.float32) * gate_grad.reshape(blocks, -1)[:, :, None], axis=1
+            ).reshape(-1)
+        )
+        grad_hidden = through * row_gate
+        sigmoid_gate = jax.nn.sigmoid(gate_pre)
+        grad_pre = jnp.concatenate(
+            [
+                (
+                    grad_hidden * up_pre * sigmoid_gate * (1.0 + gate_pre * (1.0 - sigmoid_gate))
+                ).astype(jnp.bfloat16),
+                (grad_hidden * gate_pre * sigmoid_gate).astype(jnp.bfloat16),
+            ],
+            axis=1,
+        )
+        grad_down = lax.dot_general(
+            (hidden_f * row_gate).astype(jnp.bfloat16),
+            grad_rows,
+            (((0,), (0,)), ((), ())),
+            preferred_element_type=jnp.float32,
+        ).astype(jnp.bfloat16)
+        grad_up_gate = lax.dot_general(
+            rows, grad_pre, (((0,), (0,)), ((), ())), preferred_element_type=jnp.float32
+        ).astype(jnp.bfloat16)
+        grad_in = lax.dot_general(
+            grad_pre, w_up_gate, (((1,), (1,)), ((), ())), preferred_element_type=jnp.float32
+        ).astype(jnp.bfloat16)
+        back = jnp.einsum(
+            "bst,bsd->btd",
+            pick,
+            grad_in.reshape(blocks, -1, width),
+            preferred_element_type=jnp.float32,
+        )
+        total = back if total is None else total + back
+        grads.append((grad_up_gate, grad_down))
+    return total.reshape(-1, width).astype(jnp.bfloat16), grads, gate_grads
+
+
+def chip_shards(
+    tokens,
+    cotangent,
+    lengths,
+    routes,
+    gains,
+    w_query,
+    key_weight,
+    value_weight,
+    w_out,
+    w_router,
+    w_gate,
+    w_up,
+    w_down,
+):
+    rows = tokens.shape[0]
+    width = lax.axis_size("fsdp")
+    place = lax.axis_index("fsdp")
+    line = lax.axis_index("line")
+    core = lax.axis_index("core")
+    devices = width * lax.axis_size("line") * 2
+    chips = devices // 2
+    chip = place * lax.axis_size("line") + line
+    half_heads = QUERY_HEADS // 2
+    ff = w_gate.shape[3]
+    short = w_query.shape[1]
+    experts_here = w_gate.shape[1]
+    gain_columns = -(-gains.size // short)
+    side = jnp.concatenate(
+        [w_router[number] for number in range(DECODER_LAYERS)]
+        + [jnp.pad(gains.reshape(-1), (0, gain_columns * short - gains.size)).reshape(short, -1)],
+        axis=1,
+    )
+    side = by_core(core, side, swap(side), 0)
+    router_columns = DECODER_LAYERS * EXPERTS
+    cut = side.shape[1]
+    small = jnp.concatenate(
+        [side] + [routes[number].astype(jnp.bfloat16) for number in range(DECODER_LAYERS)], axis=1
+    )
+    small = offload_gather(jnp.pad(small, ((0, 0), (0, -small.shape[1] % 128))))
+    routers = [
+        small[:, number * EXPERTS : (number + 1) * EXPERTS] for number in range(DECODER_LAYERS)
+    ]
+    all_gains = (
+        small[:, router_columns:cut]
+        .reshape(devices, -1)[:, : gains.size]
+        .reshape(devices, DECODER_LAYERS, -1)
+        .transpose(1, 0, 2)
+        .reshape(DECODER_LAYERS, -1)
+        .astype(jnp.float32)
+    )
+    all_routes = (
+        small[:, cut : cut + DECODER_LAYERS * TOP]
+        .reshape(chips, rows, DECODER_LAYERS, TOP)
+        .transpose(0, 2, 1, 3)
+    )
+    chosen = jnp.any(
+        all_routes[..., None] == jnp.arange(EXPERTS, dtype=jnp.bfloat16), axis=3
+    )
+    chosen_f = chosen.astype(jnp.bfloat16)
+    before = jnp.tril(jnp.ones((rows, rows), jnp.bfloat16), -1)
+    ranks = jnp.einsum(
+        "ts,clse->clte", before, chosen_f, preferred_element_type=jnp.float32
+    )
+    first = (line * 2 + core) * experts_here + place
+    second = (line * 2 + (1 - core)) * experts_here + place
+    slots = jnp.arange(CAP, dtype=jnp.float32)
+
+    def pick_of(number, expert):
+        named = lax.dynamic_index_in_dim(chosen[:, number], expert, 2, keepdims=False)
+        rank = lax.dynamic_index_in_dim(ranks[:, number], expert, 2, keepdims=False)
+        return (
+            (rank[:, None, :] == slots[None, :, None]) & named[:, None, :]
+        ).astype(jnp.bfloat16)
+
+    picks = [(pick_of(number, first), pick_of(number, second)) for number in range(DECODER_LAYERS)]
+
+    other_lengths = swap(lengths)
+    here = geometry(lengths, rows)
+    there = geometry(other_lengths, rows)
+    cosine = jnp.concatenate([here[0], there[0]], axis=0)
+    sine = jnp.concatenate([here[1], there[1]], axis=0)
+    allowed = jnp.stack([here[2], there[2]])
+    angles = (core, cosine, sine, allowed)
+
+    heads = w_query.reshape(DECODER_LAYERS, short, half_heads, 2, HEAD_SIZE)
+    pair_width = KEY_VALUE_HEADS // 2 * HEAD_SIZE
+
+    def columns_of(which):
+        return jnp.concatenate(
+            [
+                lax.dynamic_index_in_dim(heads, which, 3, keepdims=False).reshape(
+                    DECODER_LAYERS, short, half_heads * HEAD_SIZE
+                ),
+                lax.dynamic_slice_in_dim(key_weight, which * pair_width, pair_width, 2),
+                lax.dynamic_slice_in_dim(value_weight, which * pair_width, pair_width, 2),
+            ],
+            axis=2,
+        )
+
+    chip_qkv = by_core(core, columns_of(core), swap(columns_of(1 - core)), 1)
+    g_attn, g_ffn, g_query, g_key = zip(*[split_gains(all_gains[i]) for i in range(DECODER_LAYERS)])
+
+    state = tokens.astype(jnp.float32)
+    kept = []
+    for number in range(DECODER_LAYERS):
+        first_layer = number == 0
+        dense = (
+            gather_chips(chip_qkv[number], 1) if first_layer else offload_gather(chip_qkv[number]),
+            offload_gather(w_out[number]),
+            g_attn[number],
+            g_query[number],
+            g_key[number],
+        )
+        up_gate = spread_experts(
+            jnp.concatenate([w_gate[number], w_up[number]], axis=2), place, width
+        ).reshape(MODEL_WIDTH, 2 * ff)
+        down = spread_columns(w_down[number], place, width)
+        weights = ((up_gate, down), (swap(up_gate), swap(down)))
+        middle, memo = attention_forward(state, dense, angles)
+        mixer_in = norm_rows(middle, g_ffn[number]).astype(jnp.bfloat16)
+        gathered = gather_chips(mixer_in, 2)
+        logits = jnp.dot(gathered, routers[number], preferred_element_type=jnp.float32)
+        named = chosen[:, number].reshape(chips * rows, EXPERTS)
+        gates = softmax_last(jnp.where(named, logits, -1e30))
+        row_gates = []
+        for pick, expert in zip(picks[number], (first, second)):
+            gate = lax.dynamic_index_in_dim(gates, expert, 1, keepdims=False)
+            row_gates.append(
+                jnp.sum(
+                    pick.astype(jnp.float32) * gate.reshape(chips, 1, rows), axis=2
+                ).reshape(-1, 1)
+            )
+        produced, expert_memo = expert_forward(gathered, picks[number], row_gates, weights)
+        new_state = middle + scatter_chips(produced, 3).astype(jnp.float32)
+        own_gates = lax.dynamic_slice_in_dim(gates, chip * rows, rows, 0)
+        kept.append(
+            (state, middle, mixer_in, own_gates, row_gates, dense, weights, memo, expert_memo)
+        )
+        state = new_state
+    result = state.astype(jnp.bfloat16)
+
+    grad_state = cotangent.astype(jnp.float32)
+    grad_low = cotangent
+    grad_gathered = offload_gather(cotangent)
+    outs = []
+    small_grads = []
+    for number in reversed(range(DECODER_LAYERS)):
+        state, middle, mixer_in, own_gates, row_gates, dense, weights, memo, expert_memo = kept[
+            number
+        ]
+        back, expert_grads, gate_grads = expert_backward(
+            grad_gathered, picks[number], row_gates, weights, expert_memo
+        )
+        spread = jnp.zeros((chips * rows, EXPERTS), jnp.float32)
+        for gate_grad, expert in zip(gate_grads, (first, second)):
+            spread = lax.dynamic_update_index_in_dim(spread, gate_grad, expert, 1)
+        grad_gates = offload_scatter(spread)
+        grad_logits = (
+            own_gates
+            * (grad_gates - jnp.sum(own_gates * grad_gates, axis=1, keepdims=True))
+        ).astype(jnp.bfloat16)
+        grad_router = lax.dot_general(
+            mixer_in, grad_logits, (((0,), (0,)), ((), ())), preferred_element_type=jnp.float32
+        )
+        grad_mixer = scatter_chips(back, 3).astype(jnp.float32) + lax.dot_general(
+            grad_logits,
+            routers[number],
+            (((1,), (1,)), ((), ())),
+            preferred_element_type=jnp.float32,
+        )
+        unused_mid, norm_back = jax.vjp(norm_rows, middle, g_ffn[number])
+        grad_mid_part, grad_g_ffn = norm_back(grad_mixer)
+        grad_middle = grad_state + grad_mid_part
+        grad_normed, grad_wqkv, grad_wout, grad_gq, grad_gk = attention_backward(
+            grad_middle, memo, dense, angles
+        )
+        unused_state, norm_front = jax.vjp(norm_rows, state, g_attn[number])
+        grad_in_part, grad_g_attn = norm_front(grad_normed)
+        grad_state = grad_middle + grad_in_part
+        grad_low = grad_state.astype(jnp.bfloat16)
+        if number > 0:
+            grad_gathered = gather_chips(grad_low, 2)
+
+        (own_up_gate, own_down), (other_up_gate, other_down) = expert_grads
+        grad_up_gate = own_up_gate + swap(other_up_gate)
+        grad_down = own_down + swap(other_down)
+        d_up_gate = spread_experts(
+            grad_up_gate.reshape(width, MODEL_WIDTH // width, 2 * ff), place, width
+        ).astype(jnp.float32)
+        d_down = spread_experts(
+            grad_down.reshape(ff, width, MODEL_WIDTH // width).transpose(1, 0, 2), place, width
+        ).astype(jnp.float32)
+        d_out = offload_scatter(grad_wout).astype(jnp.float32)
+        gain_grads = jnp.concatenate([grad_g_attn, grad_g_ffn, grad_gq, grad_gk])
+        outs.insert(
+            0, (d_out, d_up_gate[:, :, :ff], d_up_gate[:, :, ff:], d_down)
+        )
+        small_grads.insert(0, (grad_router, gain_grads.reshape(devices, -1)))
+        if number > 0:
+            d_qkv = offload_scatter(grad_wqkv)
+    d_out, d_gate, d_up, d_down = [jnp.stack([entry[i] for entry in outs]) for i in range(4)]
+    own_gains = jnp.concatenate([gain_grad for _, gain_grad in small_grads], axis=1)
+    own_gains = jnp.pad(own_gains, ((0, 0), (0, gain_columns * short - gains.size)))
+    side = jnp.concatenate(
+        [router_grad for router_grad, _ in small_grads] + [own_gains.reshape(MODEL_WIDTH, -1)],
+        axis=1,
+    ).astype(jnp.bfloat16)
+    side = jnp.pad(side, ((0, 0), (0, -side.shape[1] % 128)))
+    qkv_columns = grad_wqkv.shape[1]
+    last = scatter_chips(jnp.concatenate([grad_wqkv, side], axis=1), 4).astype(jnp.float32)
+    d_qkv = d_qkv.astype(jnp.float32)
+    first_qkv = last[:, :qkv_columns]
+    side = last[:, qkv_columns:]
+    d_qkv = jnp.stack([first_qkv, d_qkv])
+    mine = lax.dynamic_slice_in_dim(d_qkv, core * short, short, 1)
+    got = swap(lax.dynamic_slice_in_dim(d_qkv, (1 - core) * short, short, 1))
+    small = lax.dynamic_slice_in_dim(side, core * short, short, 0) + swap(
+        lax.dynamic_slice_in_dim(side, (1 - core) * short, short, 0)
+    )
+    d_router = jnp.stack(
+        [small[:, number * EXPERTS : (number + 1) * EXPERTS] for number in range(DECODER_LAYERS)]
+    )
+    d_gains = small[:, router_columns : router_columns + gain_columns].reshape(-1)[: gains.size]
+    d_gains = d_gains.reshape(gains.shape)
+    q_width = half_heads * HEAD_SIZE
+    side = (DECODER_LAYERS, short, half_heads, 1, HEAD_SIZE)
+    d_query = by_core(
+        core, mine[..., :q_width].reshape(side), got[..., :q_width].reshape(side), 3
+    ).reshape(w_query.shape)
+    cut = q_width + pair_width
+    d_key = by_core(core, mine[..., q_width:cut], got[..., q_width:cut], 2)
+    d_value = by_core(core, mine[..., cut:], got[..., cut:], 2)
+    return (
+        result,
+        grad_low,
+        d_gains,
+        d_query,
+        d_key,
+        d_value,
+        d_out,
+        d_router,
+        d_gate,
+        d_up,
+        d_down,
+    )
+
+
+def by_chip(mesh):
+    grid = Mesh(
+        mesh.devices.reshape(mesh.shape["fsdp"], mesh.shape["expert"] // 2, 2),
+        ("fsdp", "line", "core"),
+    )
+    experts = ("line", "core")
+    return jax.shard_map(
+        chip_shards,
+        mesh=grid,
+        in_specs=(
+            P(EVERY, None),
+            P(EVERY, None),
+            P(EVERY, None),
+            P(None, EVERY, None),
+            P(None, EVERY),
+            P(None, EVERY, None),
+            P(None, EVERY, None),
+            P(None, EVERY, None),
+            P(None, EVERY, None),
+            P(None, EVERY, None),
+            P(None, experts, "fsdp", None),
+            P(None, experts, "fsdp", None),
+            P(None, experts, None, "fsdp"),
+        ),
+        out_specs=(
+            P(EVERY, None),
+            P(EVERY, None),
+            P(None, EVERY),
+            P(None, EVERY, None),
+            P(None, EVERY, None),
+            P(None, EVERY, None),
+            P(None, EVERY, None),
+            P(None, EVERY, None),
+            P(None, experts, "fsdp", None),
+            P(None, experts, "fsdp", None),
+            P(None, experts, None, "fsdp"),
+        ),
+        check_vma=False,
+    )
+
+
+def solution(mesh):
+    width = mesh.shape["fsdp"]
+    peers = mesh.shape["expert"]
+    if width == 4 and peers % 2 == 0 and peers * width == EXPERTS:
+        return by_chip(mesh)
+    return general(mesh)

time: 5220 us -> 2290 us (0.44)
  waiting for transfers between devices: 3810 us -> 474 us
  Pallas kernels: 0 us -> 931 us
  blocking collectives: 586 us -> 51.3 us
  local copies, waits for them, and re-layouts: 189 us -> 245 us
    reduce_scatter x14 -> x5, waiting for transfers between devices: 2580 us -> 69.2 us  [offload_scatter(): return lax.psum_scatter(operand, CHIPS, scatter_dimension=0, tiled=True)]
    pallas_call x0 -> x9, Pallas kernels: none -> 931 us  [the longest x5 535 us: scatter_chips(): pl.pallas_call(partial(scatter_kernel, depth), out_shape=jax.ShapeDtypeSt...]
    all_gather x14 -> x4, waiting for transfers between devices: 801 us -> 0.03 us  [offload_gather(): return lax.all_gather(operand, CHIPS, axis=0, tiled=True)]
    all_to_all x7 -> x0, waiting for transfers between devices: 426 us -> none  [the longest x2 266 us: layer_backward(): lax.all_to_all(grad_incoming, 'expert', split_axis=0, concat_axis=0, tile...]
    ppermute x0 -> x49, waiting for transfers between devices: none -> 404 us  [the longest x18 382 us: spread_experts(): got = lax.ppermute(sent, 'fsdp', [(i, i ^ step) for i in range(width)])]
    all_gather x2 -> x1, blocking collectives: 360 us -> 51.3 us  [offload_gather(): return lax.all_gather(operand, CHIPS, axis=0, tiled=True)]
    all_to_all x1 -> x0, blocking collectives: 145 us -> none  [layer_backward(): lax.all_to_all(outgoing.reshape(peers, experts_here * CAP, MODEL_WIDTH),...]
    unnamed x2 -> x0, blocking collectives: 81 us -> none
  transfers between devices with their start and end apart: 37 -> 58, of which waited for: 28 -> 14; matrix products, arithmetic and copies ran while one was open for 10% -> 27% of each run, Pallas kernels for 0% -> 35%
where the time goes in v1:
time: 2290 us; the launch traced here: 2280 us
  Pallas kernels  931 us (41%)
  waiting for transfers between devices  474 us (21%)
  matrix products  393 us (17%)
  local copies, waits for them, and re-layouts  245 us (11%)
  other arithmetic  127 us (6%)
  blocking collectives  51.3 us (2%)
  starting transfers between devices  36.8 us (2%)
    pallas_call x5, Pallas kernels, scatter_chips(): pl.pallas_call(partial(scatter_kernel, depth), out_shape=jax.ShapeDtypeSt...  535 us
    pallas_call x4, Pallas kernels, gather_chips(): pl.pallas_call(partial(gather_kernel, depth), out_shape=jax.ShapeDtypeStr...  397 us
    ppermute x18, waiting for transfers between devices, spread_experts(): got = lax.ppermute(sent, 'fsdp', [(i, i ^ step) for i in range(width)])  382 us
    reduce_scatter x5, waiting for transfers between devices, offload_scatter(): return lax.psum_scatter(operand, CHIPS, scatter_dimension=0, tiled=True)  69.2 us
    all_gather x1, blocking collectives, offload_gather(): return lax.all_gather(operand, CHIPS, axis=0, tiled=True)  51.3 us
    unnamed x488, local copies, waits for them, and re-layouts  51.2 us
  transfers between devices with their start and end apart: 58, of which 14 were waited for; matrix products, arithmetic and copies ran while one was open for 27% of the time, Pallas kernels for 35%

profile of v1, /device:TPU:0, one launch (start us, length us, event | category | flops | bytes accessed | tf_op | source)
XLA Modules:
  0.0 2276.3 jit_solution(1800954093616224081)
XLA Ops:
  47.0 9.3 slice_bitcast_fusion.4
  74.7 51.3 %all_gather.15 = bf16[2048,128]{0,1:T(8,128)(2,1)S(1)} all-gather(bf16[128,128]{0,1:T(8,128)(2,1)S(1)} %fusion.217), channel_id=1, replica_groups=mesh['fsdp'=4,'line'=4,'core'=2] {'fsdp','line'}, dimensions={0}, use_global_device_ids=true | all-gather | bytes 557056 | tf_op jit(solution)/shard_map/all_gather | solution.py:499
  131.9 132.9 %gather_chips.4 = bf16[16,128,2560]{2,1,0:T(8,128)(2,1)} custom-call(bf16[128,2560]{1,0:T(8,128)(2,1)} %get-tuple-element.204.x_ref), custom_call_target="tpu_custom_call" | custom-call | bytes 41943040 | tf_op jit(solution)/shard_map/gather_chips/pallas_call | solution.py:719
  296.2 19.0 collective-permute-done.21
  337.5 18.8 collective-permute-done.6
  360.5 45.9 %collective-permute-done.7 = bf16[512,1536]{1,0:T(8,128)(2,1)} collective-permute-done((bf16[512,1536]{1,0:T(8,128)(2,1)}, bf16[512,1536]{1,0:T(8,128)(2,1)}, u32[]{:S(2)}, u32[]{:S(2)}) %collective-permute-start.7) | collective-permute-done | bytes 1572896 | tf_op jit(solution)/shard_map/ppermute | solution.py:845
  426.4 50.6 %collective-permute-done.18 = bf16[512,1536]{1,0:T(8,128)(2,1)} collective-permute-done((bf16[512,1536]{1,0:T(8,128)(2,1)}, bf16[512,1536]{1,0:T(8,128)(2,1)}, u32[]{:S(2)}, u32[]{:S(2)}) %collective-permute-start.18) | collective-permute-done | bytes 1572896 | tf_op jit(solution)/shard_map/ppermute | solution.py:845
  482.0 127.1 %gather_chips.5 = bf16[16,128,2048]{2,1,0:T(8,128)(2,1)} custom-call(bf16[128,2048]{1,0:T(8,128)(2,1)} %multiply_convert_fusion.18.x_ref), custom_call_target="tpu_custom_call" | custom-call | bytes 33554432 | tf_op jit(solution)/shard_map/gather_chips/pallas_call | solution.py:719
  620.9 8.7 fusion.276
  633.7 8.3 fusion.277
  654.7 8.2 fusion.116
  662.8 11.9 add_convert_fusion.3.x_ref
  674.8 106.1 %scatter_chips.5 = bf16[128,2048]{1,0:T(8,128)(2,1)S(1)} custom-call(bf16[16,128,2048]{2,1,0:T(8,128)(2,1)} %add_convert_fusion.3.x_ref), custom_call_target="tpu_custom_call" | custom-call | bytes 33554432 | tf_op jit(solution)/shard_map/scatter_chips/pallas_call | solution.py:817
  833.2 71.5 %gather_chips.6 = bf16[16,128,2048]{2,1,0:T(8,128)(2,1)} custom-call(bf16[128,2048]{1,0:T(8,128)(2,1)} %multiply_convert_fusion.16.x_ref), custom_call_target="tpu_custom_call" | custom-call | bytes 33554432 | tf_op jit(solution)/shard_map/gather_chips/pallas_call | solution.py:719
  909.4 8.9 fusion.278
  918.3 8.3 fusion.24
  943.0 9.4 convolution_convert_fusion.23
  952.4 8.2 fusion.127
  967.9 8.4 fusion.26
  981.0 9.1 convolution_convert_fusion.22
  990.1 11.6 add_convert_fusion.1.x_ref
  1001.8 63.7 %scatter_chips.7 = bf16[128,2048]{1,0:T(8,128)(2,1)S(1)} custom-call(bf16[16,128,2048]{2,1,0:T(8,128)(2,1)} %add_convert_fusion.1.x_ref), custom_call_target="tpu_custom_call" | custom-call | bytes 33554432 | tf_op jit(solution)/shard_map/scatter_chips/pallas_call | solution.py:817
  1073.3 69.2 %reduce-scatter.6.cloned.1.call-done = f32[128,32]{0,1:T(8,128)} async-done(((f32[2048,32]{0,1:T(8,128)}), f32[128,32]{0,1:T(8,128)}) %reduce-scatter.6.cloned.1.call-update) | async-done | bytes 16400 | tf_op jit(solution)/shard_map/reduce_scatter | solution.py:503
  1146.9 8.2 fusion.130
  1197.0 11.6 add_convert_fusion.2.x_ref
  1208.6 67.1 %scatter_chips.6 = bf16[128,2048]{1,0:T(8,128)(2,1)S(1)} custom-call(bf16[16,128,2048]{2,1,0:T(8,128)(2,1)} %add_convert_fusion.2.x_ref), custom_call_target="tpu_custom_call" | custom-call | bytes 33554432 | tf_op jit(solution)/shard_map/scatter_chips/pallas_call | solution.py:817
  1279.3 65.2 %gather_chips.7 = bf16[16,128,2048]{2,1,0:T(8,128)(2,1)} custom-call(bf16[128,2048]{1,0:T(8,128)(2,1)} %get-tuple-element.123.x_ref), custom_call_target="tpu_custom_call" | custom-call | bytes 33554432 | tf_op jit(solution)/shard_map/gather_chips/pallas_call | solution.py:719
  1361.7 8.1 multiply_convert_fusion.5
  1372.0 8.6 convolution_convert_fusion
  1389.8 9.2 convolution_convert_fusion.2
  1413.6 8.2 fusion.113
  1421.8 8.1 convolution_convert_fusion.20
  1429.9 11.7 add_convert_fusion.x_ref
  1441.5 119.3 %scatter_chips.8 = bf16[128,2048]{1,0:T(8,128)(2,1)S(1)} custom-call(bf16[16,128,2048]{2,1,0:T(8,128)(2,1)} %add_convert_fusion.x_ref), custom_call_target="tpu_custom_call" | custom-call | bytes 33554432 | tf_op jit(solution)/shard_map/scatter_chips/pallas_call | solution.py:817
  1561.0 9.4 convolution_convert_fusion.4
  1654.4 55.6 %collective-permute-done.47 = bf16[768,512]{1,0:T(8,128)(2,1)} collective-permute-done((bf16[768,512]{1,0:T(8,128)(2,1)}, bf16[768,512]{1,0:T(8,128)(2,1)}, u32[]{:S(2)}, u32[]{:S(2)}) %collective-permute-start.47) | collective-permute-done | bytes 786464 | tf_op jit(solution)/shard_map/ppermute | solution.py:845
  1725.2 9.5 fusion.1
  1734.7 178.6 %scatter_chips.9 = bf16[128,2688]{1,0:T(8,128)(2,1)S(1)} custom-call(bf16[16,128,2688]{2,1,0:T(8,128)(2,1)} %bitcast.512), custom_call_target="tpu_custom_call" | custom-call | bytes 44040192 | tf_op jit(solution)/shard_map/scatter_chips/pallas_call | solution.py:817
  1958.8 16.8 collective-permute-done.42
  1980.1 82.0 %collective-permute-done.44 = bf16[768,512]{1,0:T(8,128)(2,1)S(1)} collective-permute-done((bf16[768,512]{1,0:T(8,128)(2,1)S(1)}, bf16[768,512]{1,0:T(8,128)(2,1)S(1)}, u32[]{:S(2)}, u32[]{:S(2)}) %collective-permute-start.44) | collective-permute-done | bytes 786464 | tf_op jit(solution)/shard_map/ppermute | solution.py:845
  2084.6 48.1 %collective-permute-done.39 = bf16[512,1536]{1,0:T(8,128)(2,1)S(1)} collective-permute-done((bf16[512,1536]{1,0:T(8,128)(2,1)S(1)}, bf16[512,1536]{1,0:T(8,128)(2,1)S(1)}, u32[]{:S(2)}, u32[]{:S(2)}) %collective-permute-start.39) | collective-permute-done | bytes 1572896 | tf_op jit(solution)/shard_map/ppermute | solution.py:845
  2135.7 9.4 convert_element_type.482
  2145.1 10.1 slice_bitcast_fusion
  2155.2 24.0 %collective-permute-done.34 = bf16[512,1536]{1,0:T(8,128)(2,1)} collective-permute-done((bf16[512,1536]{1,0:T(8,128)(2,1)}, bf16[512,1536]{1,0:T(8,128)(2,1)}, u32[]{:S(2)}, u32[]{:S(2)}) %collective-permute-start.34) | collective-permute-done | bytes 1572896 | tf_op jit(solution)/shard_map/ppermute | solution.py:845
  2180.8 34.5 %collective-permute-done.35 = bf16[512,1536]{1,0:T(8,128)(2,1)} collective-permute-done((bf16[512,1536]{1,0:T(8,128)(2,1)}, bf16[512,1536]{1,0:T(8,128)(2,1)}, u32[]{:S(2)}, u32[]{:S(2)}) %collective-permute-start.35) | collective-permute-done | bytes 1572896 | tf_op jit(solution)/shard_map/ppermute | solution.py:845
  2225.0 10.2 slice_bitcast_fusion.1
  2238.4 10.5 pad_maximum_fusion
  2248.9 9.1 pad_maximum_fusion.1
  (949 shorter events, 559.1 us)
Async XLA Ops:
  7.2 405.1 %all-gather.10.cloned.1.call-start = ((), (), s32[]{:S(2)}) async-start(), calls=%async_computation.11 | async-start | bytes 8912896 | tf_op jit(solution)/shard_map/all_gather | solution.py:499
  9.6 776.0 %all-gather.12.cloned.1.call-start = ((), (), s32[]{:S(2)}) async-start(), calls=%async_computation.12 | async-start | bytes 11141120 | tf_op jit(solution)/shard_map/all_gather | solution.py:499
  20.8 790.9 %all-gather.14.cloned.1.call-start = ((), (), s32[]{:S(2)}) async-start(), calls=%async_computation.13 | async-start | bytes 8912896 | tf_op jit(solution)/shard_map/all_gather | solution.py:499
  21.5 798.9 %all-gather.8.cloned.1.call-start = ((), (), s32[]{:S(2)}) async-start(), calls=%async_computation.5 | async-start | bytes 8912896 | tf_op jit(solution)/shard_map/all_gather | solution.py:499
  21.9 52.7 %collective-permute-start = (bf16[64,69]{0,1:T(8,128)(2,1)S(1)}, bf16[64,69]{0,1:T(8,128)(2,1)S(1)}, u32[]{:S(2)}, u32[]{:S(2)}) collective-permute-start(bf16[64,69]{0,1:T(8,128)(2,1)S(1)} %pad_maximum_fusion.51), channel_id=1, source_target_pairs={{0,1},{1,0},{2,3},{3,2},{4,5},{5,4},{6,7},{7,6},{8,9},{9,8},{10,11... | collective-permute-start | bytes 26504 | tf_op jit(solution)/shard_map/ppermute | solution.py:482
  22.4 49.0 %collective-permute-start.3 = (s32[1,4]{1,0:T(1,128)S(1)}, s32[1,4]{1,0:T(1,128)S(1)}, u32[]{:S(2)}, u32[]{:S(2)}) collective-permute-start(s32[1,4]{1,0:T(1,128)S(1)} %copy-done.208), channel_id=1, source_target_pairs={{0,1},{1,0},{2,3},{3,2},{4,5},{5,4},{6,7},{7,6},{8,9},{9,8},{10,11... | collective-permute-start | bytes 56 | tf_op jit(solution)/shard_map/ppermute | solution.py:482
  30.2 254.6 %collective-permute-start.9 = (bf16[768,512]{1,0:T(8,128)(2,1)}, bf16[768,512]{1,0:T(8,128)(2,1)}, u32[]{:S(2)}, u32[]{:S(2)}) collective-permute-start(bf16[768,512]{1,0:T(8,128)(2,1)} %get-tuple-element.182), channel_id=1, source_target_pairs={{0,8},{8,0},{16,24},{24,16},{1,9},{9,1},{17,25},{25,17},{2,10},{10... | collective-permute-start | bytes 2359304 | tf_op jit(solution)/shard_map/ppermute | solution.py:857
  32.9 260.6 %collective-permute-start.10 = (bf16[768,512]{1,0:T(8,128)(2,1)}, bf16[768,512]{1,0:T(8,128)(2,1)}, u32[]{:S(2)}, u32[]{:S(2)}) collective-permute-start(bf16[768,512]{1,0:T(8,128)(2,1)} %get-tuple-element.181), channel_id=1, source_target_pairs={{0,16},{8,24},{16,0},{24,8},{1,17},{9,25},{17,1},{25,9},{2,18},{10... | collective-permute-start | bytes 2359304 | tf_op jit(solution)/shard_map/ppermute | solution.py:857
  34.5 284.8 %collective-permute-start.11 = (bf16[768,512]{1,0:T(8,128)(2,1)}, bf16[768,512]{1,0:T(8,128)(2,1)}, u32[]{:S(2)}, u32[]{:S(2)}) collective-permute-start(bf16[768,512]{1,0:T(8,128)(2,1)} %get-tuple-element.180), channel_id=1, source_target_pairs={{0,24},{8,16},{16,8},{24,0},{1,25},{9,17},{17,9},{25,1},{2,26},{10... | collective-permute-start | bytes 2359304 | tf_op jit(solution)/shard_map/ppermute | solution.py:857
  34.5 1107.9 %reduce-scatter.6.cloned.1.call-start = ((), (), s32[]{:S(2)}) async-start(), calls=%async_computation.6 | async-start | bytes 278528 | tf_op jit(solution)/shard_map/reduce_scatter | solution.py:503
  71.3 219.3 %collective-permute-start.20 = (bf16[768,512]{1,0:T(8,128)(2,1)}, bf16[768,512]{1,0:T(8,128)(2,1)}, u32[]{:S(2)}, u32[]{:S(2)}) collective-permute-start(bf16[768,512]{1,0:T(8,128)(2,1)} %get-tuple-element.179), channel_id=1, source_target_pairs={{0,8},{8,0},{16,24},{24,16},{1,9},{9,1},{17,25},{25,17},{2,10},{10... | collective-permute-start | bytes 2359304 | tf_op jit(solution)/shard_map/ppermute | solution.py:857
  129.0 135.8 %collective-permute-start.1 = (bf16[128,2048]{1,0:T(8,128)(2,1)S(1)}, bf16[128,2048]{1,0:T(8,128)(2,1)S(1)}, u32[]{:S(2)}, u32[]{:S(2)}) collective-permute-start(bf16[128,2048]{1,0:T(8,128)(2,1)S(1)} %fusion.82), channel_id=1, source_target_pairs={{0,1},{1,0},{2,3},{3,2},{4,5},{5,4},{6,7},{7,6},{8,9},{9,8},{10,11... | collective-permute-start | bytes 1572872 | tf_op jit(solution)/shard_map/ppermute | solution.py:482
  264.8 50.4 %collective-permute-start.21 = (bf16[768,512]{1,0:T(8,128)(2,1)}, bf16[768,512]{1,0:T(8,128)(2,1)}, u32[]{:S(2)}, u32[]{:S(2)}) collective-permute-start(bf16[768,512]{1,0:T(8,128)(2,1)} %get-tuple-element.178), channel_id=1, source_target_pairs={{0,16},{8,24},{16,0},{24,8},{1,17},{9,25},{17,1},{25,9},{2,18},{10... | collective-permute-start | bytes 2359304 | tf_op jit(solution)/shard_map/ppermute | solution.py:857
  284.9 38.2 %collective-permute-start.22 = (bf16[768,512]{1,0:T(8,128)(2,1)S(1)}, bf16[768,512]{1,0:T(8,128)(2,1)S(1)}, u32[]{:S(2)}, u32[]{:S(2)}) collective-permute-start(bf16[768,512]{1,0:T(8,128)(2,1)S(1)} %copy-done.125), channel_id=1, source_target_pairs={{0,24},{8,16},{16,8},{24,0},{1,25},{9,17},{17,9},{25,1},{2,26},{10... | collective-permute-start | bytes 2359304 | tf_op jit(solution)/shard_map/ppermute | solution.py:857
  290.7 65.7 %collective-permute-start.6 = (bf16[512,1536]{1,0:T(8,128)(2,1)}, bf16[512,1536]{1,0:T(8,128)(2,1)}, u32[]{:S(2)}, u32[]{:S(2)}) collective-permute-start(bf16[512,1536]{1,0:T(8,128)(2,1)} %get-tuple-element.167), channel_id=1, source_target_pairs={{0,8},{8,0},{16,24},{24,16},{1,9},{9,1},{17,25},{25,17},{2,10},{10... | collective-permute-start | bytes 4718600 | tf_op jit(solution)/shard_map/ppermute | solution.py:845
  293.5 113.0 %collective-permute-start.7 = (bf16[512,1536]{1,0:T(8,128)(2,1)}, bf16[512,1536]{1,0:T(8,128)(2,1)}, u32[]{:S(2)}, u32[]{:S(2)}) collective-permute-start(bf16[512,1536]{1,0:T(8,128)(2,1)} %get-tuple-element.168), channel_id=1, source_target_pairs={{0,16},{8,24},{16,0},{24,8},{1,17},{9,25},{17,1},{25,9},{2,18},{10... | collective-permute-start | bytes 4718600 | tf_op jit(solution)/shard_map/ppermute | solution.py:845
  315.2 93.9 %collective-permute-start.8 = (bf16[512,1536]{1,0:T(8,128)(2,1)}, bf16[512,1536]{1,0:T(8,128)(2,1)}, u32[]{:S(2)}, u32[]{:S(2)}) collective-permute-start(bf16[512,1536]{1,0:T(8,128)(2,1)} %get-tuple-element.165), channel_id=1, source_target_pairs={{0,24},{8,16},{16,8},{24,0},{1,25},{9,17},{17,9},{25,1},{2,26},{10... | collective-permute-start | bytes 4718600 | tf_op jit(solution)/shard_map/ppermute | solution.py:845
  323.1 100.7 %collective-permute-start.17 = (bf16[512,1536]{1,0:T(8,128)(2,1)}, bf16[512,1536]{1,0:T(8,128)(2,1)}, u32[]{:S(2)}, u32[]{:S(2)}) collective-permute-start(bf16[512,1536]{1,0:T(8,128)(2,1)} %get-tuple-element.157), channel_id=1, source_target_pairs={{0,8},{8,0},{16,24},{24,16},{1,9},{9,1},{17,25},{25,17},{2,10},{10... | collective-permute-start | bytes 4718600 | tf_op jit(solution)/shard_map/ppermute | solution.py:845
  325.1 152.0 %collective-permute-start.18 = (bf16[512,1536]{1,0:T(8,128)(2,1)}, bf16[512,1536]{1,0:T(8,128)(2,1)}, u32[]{:S(2)}, u32[]{:S(2)}) collective-permute-start(bf16[512,1536]{1,0:T(8,128)(2,1)} %get-tuple-element.158), channel_id=1, source_target_pairs={{0,16},{8,24},{16,0},{24,8},{1,17},{9,25},{17,1},{25,9},{2,18},{10... | collective-permute-start | bytes 4718600 | tf_op jit(solution)/shard_map/ppermute | solution.py:845
  356.3 426.1 %collective-permute-start.19 = (bf16[512,1536]{1,0:T(8,128)(2,1)}, bf16[512,1536]{1,0:T(8,128)(2,1)}, u32[]{:S(2)}, u32[]{:S(2)}) collective-permute-start(bf16[512,1536]{1,0:T(8,128)(2,1)} %get-tuple-element.155), channel_id=1, source_target_pairs={{0,24},{8,16},{16,8},{24,0},{1,25},{9,17},{17,9},{25,1},{2,26},{10... | collective-permute-start | bytes 4718600 | tf_op jit(solution)/shard_map/ppermute | solution.py:845
  406.5 242.9 %collective-permute-start.13 = (bf16[768,2048]{1,0:T(8,128)(2,1)}, bf16[768,2048]{1,0:T(8,128)(2,1)}, u32[]{:S(2)}, u32[]{:S(2)}) collective-permute-start(bf16[768,2048]{1,0:T(8,128)(2,1)} %constant_dynamic-update-slice_fusion.3), channel_id=1, source_target_pairs={{0,1},{1,0},{2,3},{3,2},{4,5},{5,4},{6,7},{7,6},{8,9},{9,8},{10,11... | collective-permute-start | bytes 9437192 | tf_op jit(solution)/shard_map/ppermute | solution.py:482
  411.8 221.9 %collective-permute-start.12 = (bf16[2048,1536]{1,0:T(8,128)(2,1)}, bf16[2048,1536]{1,0:T(8,128)(2,1)}, u32[]{:S(2)}, u32[]{:S(2)}) collective-permute-start(bf16[2048,1536]{1,0:T(8,128)(2,1)} %bitcast.549), channel_id=1, source_target_pairs={{0,1},{1,0},{2,3},{3,2},{4,5},{5,4},{6,7},{7,6},{8,9},{9,8},{10,11... | collective-permute-start | bytes 18874376 | tf_op jit(solution)/shard_map/ppermute | solution.py:482
  423.8 56.3 %collective-permute-start.5 = (f32[128,2048]{1,0:T(8,128)S(1)}, f32[128,2048]{1,0:T(8,128)S(1)}, u32[]{:S(2)}, u32[]{:S(2)}) collective-permute-start(f32[128,2048]{1,0:T(8,128)S(1)} %slice.420), channel_id=1, source_target_pairs={{0,1},{1,0},{2,3},{3,2},{4,5},{5,4},{6,7},{7,6},{8,9},{9,8},{10,11... | collective-permute-start | bytes 3145736 | tf_op jit(solution)/shard_map/ppermute | solution.py:482
  477.0 490.8 %collective-permute-start.24 = (bf16[768,2048]{1,0:T(8,128)(2,1)}, bf16[768,2048]{1,0:T(8,128)(2,1)}, u32[]{:S(2)}, u32[]{:S(2)}) collective-permute-start(bf16[768,2048]{1,0:T(8,128)(2,1)} %constant_dynamic-update-slice_fusion), channel_id=1, source_target_pairs={{0,1},{1,0},{2,3},{3,2},{4,5},{5,4},{6,7},{7,6},{8,9},{9,8},{10,11... | collective-permute-start | bytes 9437192 | tf_op jit(solution)/shard_map/ppermute | solution.py:482
  785.2 175.4 %collective-permute-start.23 = (bf16[2048,1536]{1,0:T(8,128)(2,1)}, bf16[2048,1536]{1,0:T(8,128)(2,1)}, u32[]{:S(2)}, u32[]{:S(2)}) collective-permute-start(bf16[2048,1536]{1,0:T(8,128)(2,1)} %bitcast.77), channel_id=1, source_target_pairs={{0,1},{1,0},{2,3},{3,2},{4,5},{5,4},{6,7},{7,6},{8,9},{9,8},{10,11... | collective-permute-start | bytes 18874376 | tf_op jit(solution)/shard_map/ppermute | solution.py:482
  1066.7 520.6 %reduce-scatter.8.cloned.1.call-start = ((), (), s32[]{:S(2)}) async-start(), calls=%async_computation.7 | async-start | bytes 278528 | tf_op jit(solution)/shard_map/reduce_scatter | solution.py:503
  1191.5 84.3 %collective-permute-start.27 = (f32[128,2048]{1,0:T(8,128)S(1)}, f32[128,2048]{1,0:T(8,128)S(1)}, u32[]{:S(2)}, u32[]{:S(2)}) collective-permute-start(f32[128,2048]{1,0:T(8,128)S(1)} %slice.460), channel_id=1, source_target_pairs={{0,1},{1,0},{2,3},{3,2},{4,5},{5,4},{6,7},{7,6},{8,9},{9,8},{10,11... | collective-permute-start | bytes 3145736 | tf_op jit(solution)/shard_map/ppermute | solution.py:482
  1371.9 863.3 %reduce-scatter.10.cloned.1.call-start = ((), (), s32[]{:S(2)}) async-start(), calls=%async_computation.8 | async-start | bytes 11141120 | tf_op jit(solution)/shard_map/reduce_scatter | solution.py:503
  1380.6 877.3 %reduce-scatter.14.cloned.1.call-start = ((), (), s32[]{:S(2)}) async-start(), calls=%async_computation.10 | async-start | bytes 8912896 | tf_op jit(solution)/shard_map/reduce_scatter | solution.py:503
  1387.9 870.1 %reduce-scatter.12.cloned.1.call-start = ((), (), s32[]{:S(2)}) async-start(), calls=%async_computation.9 | async-start | bytes 8912896 | tf_op jit(solution)/shard_map/reduce_scatter | solution.py:503
  1399.1 541.1 %collective-permute-start.37 = (bf16[2048,1536]{1,0:T(8,128)(2,1)}, bf16[2048,1536]{1,0:T(8,128)(2,1)}, u32[]{:S(2)}, u32[]{:S(2)}) collective-permute-start(bf16[2048,1536]{1,0:T(8,128)(2,1)} %convolution_convert_fusion.2), channel_id=1, source_target_pairs={{0,1},{1,0},{2,3},{3,2},{4,5},{5,4},{6,7},{7,6},{8,9},{9,8},{10,11... | collective-permute-start | bytes 18874376 | tf_op jit(solution)/shard_map/ppermute | solution.py:482
  1403.4 171.9 %collective-permute-start.45 = (bf16[768,2048]{1,0:T(8,128)(2,1)}, bf16[768,2048]{1,0:T(8,128)(2,1)}, u32[]{:S(2)}, u32[]{:S(2)}) collective-permute-start(bf16[768,2048]{1,0:T(8,128)(2,1)} %convolution_convert_fusion.8), channel_id=1, source_target_pairs={{0,1},{1,0},{2,3},{3,2},{4,5},{5,4},{6,7},{7,6},{8,9},{9,8},{10,11... | collective-permute-start | bytes 9437192 | tf_op jit(solution)/shard_map/ppermute | solution.py:482
  1570.4 500.7 %collective-permute-start.33 = (bf16[2048,1536]{1,0:T(8,128)(2,1)}, bf16[2048,1536]{1,0:T(8,128)(2,1)}, u32[]{:S(2)}, u32[]{:S(2)}) collective-permute-start(bf16[2048,1536]{1,0:T(8,128)(2,1)} %convolution_convert_fusion.4), channel_id=1, source_target_pairs={{0,1},{1,0},{2,3},{3,2},{4,5},{5,4},{6,7},{7,6},{8,9},{9,8},{10,11... | collective-permute-start | bytes 18874376 | tf_op jit(solution)/shard_map/ppermute | solution.py:482
  1574.8 342.6 %collective-permute-start.41 = (bf16[768,2048]{1,0:T(8,128)(2,1)}, bf16[768,2048]{1,0:T(8,128)(2,1)}, u32[]{:S(2)}, u32[]{:S(2)}) collective-permute-start(bf16[768,2048]{1,0:T(8,128)(2,1)} %convolution_convert_fusion.10), channel_id=1, source_target_pairs={{0,1},{1,0},{2,3},{3,2},{4,5},{5,4},{6,7},{7,6},{8,9},{9,8},{10,11... | collective-permute-start | bytes 9437192 | tf_op jit(solution)/shard_map/ppermute | solution.py:482
  1599.9 37.8 %collective-permute-start.46 = (bf16[768,512]{1,0:T(8,128)(2,1)}, bf16[768,512]{1,0:T(8,128)(2,1)}, u32[]{:S(2)}, u32[]{:S(2)}) collective-permute-start(bf16[768,512]{1,0:T(8,128)(2,1)} %bitcast.483), channel_id=1, source_target_pairs={{0,8},{8,0},{16,24},{24,16},{1,9},{9,1},{17,25},{25,17},{2,10},{10... | collective-permute-start | bytes 2359304 | tf_op jit(solution)/shard_map/ppermute | solution.py:845
  1622.2 20.5 collective-permute-start.29
  1637.7 72.3 %collective-permute-start.47 = (bf16[768,512]{1,0:T(8,128)(2,1)}, bf16[768,512]{1,0:T(8,128)(2,1)}, u32[]{:S(2)}, u32[]{:S(2)}) collective-permute-start(bf16[768,512]{1,0:T(8,128)(2,1)} %bitcast.482), channel_id=1, source_target_pairs={{0,16},{8,24},{16,0},{24,8},{1,17},{9,25},{17,1},{25,9},{2,18},{10... | collective-permute-start | bytes 2359304 | tf_op jit(solution)/shard_map/ppermute | solution.py:845
  1642.7 69.4 %collective-permute-start.48 = (bf16[768,512]{1,0:T(8,128)(2,1)}, bf16[768,512]{1,0:T(8,128)(2,1)}, u32[]{:S(2)}, u32[]{:S(2)}) collective-permute-start(bf16[768,512]{1,0:T(8,128)(2,1)} %bitcast.481), channel_id=1, source_target_pairs={{0,24},{8,16},{16,8},{24,0},{1,25},{9,17},{17,9},{25,1},{2,26},{10... | collective-permute-start | bytes 2359304 | tf_op jit(solution)/shard_map/ppermute | solution.py:845
  1939.0 36.6 %collective-permute-start.42 = (bf16[768,512]{1,0:T(8,128)(2,1)}, bf16[768,512]{1,0:T(8,128)(2,1)}, u32[]{:S(2)}, u32[]{:S(2)}) collective-permute-start(bf16[768,512]{1,0:T(8,128)(2,1)} %bitcast.486), channel_id=1, source_target_pairs={{0,8},{8,0},{16,24},{24,16},{1,9},{9,1},{17,25},{25,17},{2,10},{10... | collective-permute-start | bytes 2359304 | tf_op jit(solution)/shard_map/ppermute | solution.py:845
  1940.1 36.7 %collective-permute-start.43 = (bf16[768,512]{1,0:T(8,128)(2,1)}, bf16[768,512]{1,0:T(8,128)(2,1)}, u32[]{:S(2)}, u32[]{:S(2)}) collective-permute-start(bf16[768,512]{1,0:T(8,128)(2,1)} %bitcast.485), channel_id=1, source_target_pairs={{0,16},{8,24},{16,0},{24,8},{1,17},{9,25},{17,1},{25,9},{2,18},{10... | collective-permute-start | bytes 2359304 | tf_op jit(solution)/shard_map/ppermute | solution.py:845
  1954.3 115.5 %collective-permute-start.38 = (bf16[512,1536]{1,0:T(8,128)(2,1)}, bf16[512,1536]{1,0:T(8,128)(2,1)S(1)}, u32[]{:S(2)}, u32[]{:S(2)}) collective-permute-start(bf16[512,1536]{1,0:T(8,128)(2,1)} %get-tuple-element.153), channel_id=1, source_target_pairs={{0,8},{8,0},{16,24},{24,16},{1,9},{9,1},{17,25},{25,17},{2,10},{10... | collective-permute-start | bytes 4718600 | tf_op jit(solution)/shard_map/ppermute | solution.py:845
  1956.7 105.4 %collective-permute-start.44 = (bf16[768,512]{1,0:T(8,128)(2,1)S(1)}, bf16[768,512]{1,0:T(8,128)(2,1)S(1)}, u32[]{:S(2)}, u32[]{:S(2)}) collective-permute-start(bf16[768,512]{1,0:T(8,128)(2,1)S(1)} %bitcast.616), channel_id=1, source_target_pairs={{0,24},{8,16},{16,8},{24,0},{1,25},{9,17},{17,9},{25,1},{2,26},{10... | collective-permute-start | bytes 2359304 | tf_op jit(solution)/shard_map/ppermute | solution.py:845
  1975.6 157.1 %collective-permute-start.39 = (bf16[512,1536]{1,0:T(8,128)(2,1)S(1)}, bf16[512,1536]{1,0:T(8,128)(2,1)S(1)}, u32[]{:S(2)}, u32[]{:S(2)}) collective-permute-start(bf16[512,1536]{1,0:T(8,128)(2,1)S(1)} %copy-done.105), channel_id=1, source_target_pairs={{0,16},{8,24},{16,0},{24,8},{1,17},{9,25},{17,1},{25,9},{2,18},{10... | collective-permute-start | bytes 4718600 | tf_op jit(solution)/shard_map/ppermute | solution.py:845
  1976.8 157.7 %collective-permute-start.40 = (bf16[512,1536]{1,0:T(8,128)(2,1)S(1)}, bf16[512,1536]{1,0:T(8,128)(2,1)S(1)}, u32[]{:S(2)}, u32[]{:S(2)}) collective-permute-start(bf16[512,1536]{1,0:T(8,128)(2,1)S(1)} %copy-done.104), channel_id=1, source_target_pairs={{0,24},{8,16},{16,8},{24,0},{1,25},{9,17},{17,9},{25,1},{2,26},{10... | collective-permute-start | bytes 4718600 | tf_op jit(solution)/shard_map/ppermute | solution.py:845
  2083.1 96.1 %collective-permute-start.34 = (bf16[512,1536]{1,0:T(8,128)(2,1)}, bf16[512,1536]{1,0:T(8,128)(2,1)}, u32[]{:S(2)}, u32[]{:S(2)}) collective-permute-start(bf16[512,1536]{1,0:T(8,128)(2,1)} %get-tuple-element.149), channel_id=1, source_target_pairs={{0,8},{8,0},{16,24},{24,16},{1,9},{9,1},{17,25},{25,17},{2,10},{10... | collective-permute-start | bytes 4718600 | tf_op jit(solution)/shard_map/ppermute | solution.py:845
  2134.0 81.3 %collective-permute-start.35 = (bf16[512,1536]{1,0:T(8,128)(2,1)}, bf16[512,1536]{1,0:T(8,128)(2,1)}, u32[]{:S(2)}, u32[]{:S(2)}) collective-permute-start(bf16[512,1536]{1,0:T(8,128)(2,1)} %get-tuple-element.148), channel_id=1, source_target_pairs={{0,16},{8,24},{16,0},{24,8},{1,17},{9,25},{17,1},{25,9},{2,18},{10... | collective-permute-start | bytes 4718600 | tf_op jit(solution)/shard_map/ppermute | solution.py:845
  2145.1 71.7 %collective-permute-start.36 = (bf16[512,1536]{1,0:T(8,128)(2,1)}, bf16[512,1536]{1,0:T(8,128)(2,1)}, u32[]{:S(2)}, u32[]{:S(2)}) collective-permute-start(bf16[512,1536]{1,0:T(8,128)(2,1)} %get-tuple-element.147), channel_id=1, source_target_pairs={{0,24},{8,16},{16,8},{24,0},{1,25},{9,17},{17,9},{25,1},{2,26},{10... | collective-permute-start | bytes 4718600 | tf_op jit(solution)/shard_map/ppermute | solution.py:845
  2238.4 22.7 collective-permute-start.32
  (240 other events, 6956.3 us)
Sparse Core Ops, SparseCore 0:
  11.4 155.1 all-gather.9
  169.3 246.9 all-gather.11
  419.7 188.3 all-gather.13
  610.7 143.4 all-gather.7
  1066.8 75.5 reduce-scatter.5
  1372.0 74.6 reduce-scatter.7
  1449.7 268.2 reduce-scatter.9
  1720.2 259.1 reduce-scatter.13
  1981.7 179.8 reduce-scatter.11

commit v2 on v1

--- a/solution.py
+++ b/solution.py
@@ -474,12 +474,16 @@
     )
 
 
-CHIPS = ("fsdp", "line")
-EVERY = ("fsdp", "line", "core")
+FSDP, LINE, CORE = "fsdp", "line", "core"
+CHIPS = (FSDP, LINE)
+EVERY = (FSDP, LINE, CORE)
+X, Y, ABOVE, BELOW = range(4)
+GATE_COLUMNS = 128
+PICK, SPREAD = "bst,btd->bsd", "bst,bsd->btd"
 
 
 def swap(operand):
-    return lax.ppermute(operand, "core", [(0, 1), (1, 0)])
+    return lax.ppermute(operand, CORE, [(0, 1), (1, 0)])
 
 
 def by_core(core, mine, other, axis):
@@ -499,46 +503,52 @@
     return lax.all_gather(operand, CHIPS, axis=0, tiled=True)
 
 
-def offload_scatter(operand):
-    return lax.psum_scatter(operand, CHIPS, scatter_dimension=0, tiled=True)
-
-
 PAIR = 4
 ROW_UNITS = 8
 
 
-def routes_of_shards(depth):
+ALL_CHIPS, PLANE, LINE_ONLY = range(3)
+
+
+def routes_of_shards(grid, depth):
+    depth = 1 if grid == PLANE else depth
     offsets = [s * k for k in range(1, depth) for s in (-1, 1)]
 
     def source(offset):
-        return "below" if offset < 0 else "above"
+        return BELOW if offset < 0 else ABOVE
 
     def onward(offset):
-        return "above" if offset < 0 else "below"
+        return ABOVE if offset < 0 else BELOW
 
     def further(offset):
         return offset - 1 if offset < 0 else offset + 1
 
     def line_hops(bits, first, last, offset):
+        if depth == 1:
+            return []
         if offset == 0:
             return [
-                ("above", first, last, (bits, -1, first, last, "below")),
-                ("below", first, last, (bits, 1, first, last, "above")),
+                (ABOVE, first, last, (bits, -1, first, last, BELOW)),
+                (BELOW, first, last, (bits, 1, first, last, ABOVE)),
             ]
         if abs(further(offset)) >= depth:
             return []
         return [(onward(offset), first, last, (bits, further(offset), first, last, source(offset)))]
 
+    if grid == LINE_ONLY:
+        return [(None, line_hops(0, 0, 8, 0))] + [
+            ((0, offset, 0, 8, source(offset)), line_hops(0, 0, 8, offset)) for offset in offsets
+        ]
     plan = []
-    own = [("x", 0, 8, (1, 0, 0, 8, "x")), ("y", 0, 8, (2, 0, 0, 8, "y"))]
+    own = [(X, 0, 8, (1, 0, 0, 8, X)), (Y, 0, 8, (2, 0, 0, 8, Y))]
     plan.append((None, own + line_hops(0, 0, 8, 0)))
     plan.append(
-        ((1, 0, 0, 8, "x"), [("y", 3, 7, (3, 0, 3, 7, "y"))] + line_hops(1, 6, 8, 0))
+        ((1, 0, 0, 8, X), [(Y, 3, 7, (3, 0, 3, 7, Y))] + line_hops(1, 6, 8, 0))
     )
     plan.append(
         (
-            (2, 0, 0, 8, "y"),
-            [("x", 0, 3, (3, 0, 0, 3, "x")), ("x", 7, 8, (3, 0, 7, 8, "x"))]
+            (2, 0, 0, 8, Y),
+            [(X, 0, 3, (3, 0, 0, 3, X)), (X, 7, 8, (3, 0, 7, 8, X))]
             + line_hops(2, 6, 8, 0),
         )
     )
@@ -547,13 +557,13 @@
         return (
             (0, offset, 0, 8, source(offset)),
             line_hops(0, 0, 8, offset)
-            + [("x", 0, 6, (1, offset, 0, 6, "x")), ("y", 0, 6, (2, offset, 0, 6, "y"))],
+            + [(X, 0, 6, (1, offset, 0, 6, X)), (Y, 0, 6, (2, offset, 0, 6, Y))],
         )
 
     def crossed(offset):
         return [
-            ((1, offset, 0, 6, "x"), [("y", 3, 6, (3, offset, 3, 6, "y"))]),
-            ((2, offset, 0, 6, "y"), [("x", 0, 3, (3, offset, 0, 3, "x"))]),
+            ((1, offset, 0, 6, X), [(Y, 3, 6, (3, offset, 3, 6, Y))]),
+            ((2, offset, 0, 6, Y), [(X, 0, 3, (3, offset, 0, 3, X))]),
         ]
 
     def lined(offset):
@@ -563,14 +573,14 @@
         ]
 
     def last(offset):
-        return [((3, offset, 3, 6, "y"), []), ((3, offset, 0, 3, "x"), [])]
+        return [((3, offset, 3, 6, Y), []), ((3, offset, 0, 3, X), [])]
 
     steps = [(-k, k) for k in range(1, depth)]
-    plan += [spread(o) for o in steps[0]]
+    plan += [spread(o) for pair in steps[:1] for o in pair]
     plan += [
-        ((3, 0, 3, 7, "y"), []),
-        ((3, 0, 0, 3, "x"), []),
-        ((3, 0, 7, 8, "x"), line_hops(3, 6, 8, 0)),
+        ((3, 0, 3, 7, Y), []),
+        ((3, 0, 0, 3, X), []),
+        ((3, 0, 7, 8, X), line_hops(3, 6, 8, 0)),
     ]
     for number, pair in enumerate(steps):
         for offset in pair:
@@ -585,11 +595,12 @@
 
 
 class Place:
-    def __init__(self, depth):
+    def __init__(self, grid, depth):
+        self.grid = grid
         self.depth = depth
-        self.pair = lax.axis_index("fsdp")
-        self.line = lax.axis_index("line")
-        self.core = lax.axis_index("core")
+        self.pair = lax.axis_index(FSDP)
+        self.line = lax.axis_index(LINE)
+        self.core = lax.axis_index(CORE)
         x = lax.rem(self.pair, 2)
         y = lax.div(self.pair, 2)
         self.pairs = [
@@ -600,21 +611,25 @@
         ]
 
     def shard(self, bits, offset):
+        if self.grid == PLANE:
+            return self.pairs[bits]
+        if self.grid == LINE_ONLY:
+            return self.line + offset
         return self.pairs[bits] * self.depth + self.line + offset
 
     def device(self, neighbour):
-        if neighbour == "x":
+        if neighbour == X:
             return (self.pairs[1], self.line, self.core)
-        if neighbour == "y":
+        if neighbour == Y:
             return (self.pairs[2], self.line, self.core)
-        step = 1 if neighbour == "above" else -1
+        step = 1 if neighbour == ABOVE else -1
         return (self.pair, self.line + step, self.core)
 
     def holds(self, offset, neighbour=None):
         low, high = min(offset, 0), max(offset, 0)
-        if neighbour == "above":
+        if neighbour == ABOVE:
             high = max(high, 1)
-        if neighbour == "below":
+        if neighbour == BELOW:
             low = min(low, -1)
         tests = []
         if low < 0:
@@ -627,7 +642,10 @@
 
     def meet(self):
         barrier = pltpu.get_barrier_semaphore()
-        for neighbour in ("x", "y", "above", "below"):
+        neighbours = (() if self.grid == LINE_ONLY else (X, Y)) + (
+            () if self.grid == PLANE else (ABOVE, BELOW)
+        )
+        for neighbour in neighbours:
 
             def greet(neighbour=neighbour):
                 pl.semaphore_signal(
@@ -638,8 +656,12 @@
                 )
 
             when(self.holds(0, neighbour), greet)
-        ends = (self.line == 0).astype(jnp.int32) + (self.line == self.depth - 1).astype(jnp.int32)
-        pl.semaphore_wait(barrier, 4 - ends)
+        ends = 0
+        if self.grid != PLANE:
+            ends = (self.line == 0).astype(jnp.int32) + (self.line == self.depth - 1).astype(
+                jnp.int32
+            )
+        pl.semaphore_wait(barrier, len(neighbours) - ends)
 
 
 def when(test, action):
@@ -649,11 +671,11 @@
         pl.when(test)(action)
 
 
-def gather_kernel(depth, x_ref, out_ref, own_sem, send_sems, recv_sems):
-    plan = routes_of_shards(depth)
+def gather_kernel(grid, depth, x_ref, out_ref, own_sem, send_sems, recv_sems):
+    plan = routes_of_shards(grid, depth)
     number_of = {item: i for i, (item, _) in enumerate(plan)}
     unit = x_ref.shape[0] // ROW_UNITS
-    here = Place(depth)
+    here = Place(grid, depth)
     own = pltpu.make_async_copy(x_ref, out_ref.at[here.shard(0, 0)], own_sem)
     own.start()
     here.meet()
@@ -671,12 +693,12 @@
                     dst_ref=piece,
                     send_sem=send_sems.at[0],
                     recv_sem=recv_sems.at[number_of[item]],
-                    device_id=here.device("x"),
+                    device_id=here.device(X),
                     device_id_type=pl.DeviceIdType.MESH,
                 ).wait_recv()
             for hop, (neighbour, first, last, there) in enumerate(hops):
                 when(
-                    here.holds(0, neighbour) if neighbour in ("above", "below") else None,
+                    here.holds(0, neighbour) if neighbour in (ABOVE, BELOW) else None,
                     lambda n=neighbour, f=first, l=last, t=there, s=site + hop: passing(
                         bits, offset, n, f, l, t, s, item is None
                     ).start(),
@@ -706,18 +728,22 @@
     own.wait()
 
 
-def count_plan(depth):
-    plan = routes_of_shards(depth)
+def count_plan(grid, depth):
+    plan = routes_of_shards(grid, depth)
     return len(plan), sum(len(hops) for _, hops in plan)
 
 
-def gather_chips(operand, collective_id):
-    depth = lax.axis_size("line")
-    items, hops = count_plan(depth)
-    chips = PAIR * depth
+def chips_in(grid, depth):
+    return {ALL_CHIPS: PAIR * depth, PLANE: PAIR, LINE_ONLY: depth}[grid]
+
+
+def gather_chips(operand, collective_id, grid=ALL_CHIPS):
+    depth = lax.axis_size(LINE)
+    items, hops = count_plan(grid, depth)
+    chips = chips_in(grid, depth)
     rows, columns = operand.shape
     return pl.pallas_call(
-        partial(gather_kernel, depth),
+        partial(gather_kernel, grid, depth),
         out_shape=jax.ShapeDtypeStruct((chips, rows, columns), operand.dtype),
         in_specs=[pl.BlockSpec(memory_space=pl.ANY)],
         out_specs=pl.BlockSpec(memory_space=pl.ANY),
@@ -728,17 +754,16 @@
         ],
         compiler_params=pltpu.CompilerParams(collective_id=collective_id, has_side_effects=True),
         cost_estimate=pl.CostEstimate(
-            flops=0, bytes_accessed=8 * chips * rows * columns, transcendentals=0
+            flops=0, bytes_accessed=66 * chips * rows * columns, transcendentals=0
         ),
-        name="gather_chips",
     )(operand).reshape(chips * rows, columns)
 
 
-def scatter_kernel(depth, x_ref, out_ref, sums, landed, own_sem, send_sems, recv_sems):
-    plan = routes_of_shards(depth)
+def scatter_kernel(grid, depth, x_ref, out_ref, sums, landed, own_sem, send_sems, recv_sems):
+    plan = routes_of_shards(grid, depth)
     number_of = {item: i for i, (item, _) in enumerate(plan)}
     unit = x_ref.shape[1] // ROW_UNITS
-    here = Place(depth)
+    here = Place(grid, depth)
     own = pltpu.make_async_copy(x_ref, sums, own_sem)
     own.start()
     here.meet()
@@ -785,13 +810,13 @@
                         dst_ref=landed.at[pl.ds(base, size)],
                         send_sem=send_sems.at[0],
                         recv_sem=recv_sems.at[sem],
-                        device_id=here.device("x"),
+                        device_id=here.device(X),
                         device_id_type=pl.DeviceIdType.MESH,
                     ).wait_recv()
                     total(here.shard(bits, offset), first, last, base)
 
                 when(
-                    here.holds(0, neighbour) if neighbour in ("above", "below") else None,
+                    here.holds(0, neighbour) if neighbour in (ABOVE, BELOW) else None,
                     take,
                 )
             if item is not None:
@@ -804,18 +829,18 @@
             when(here.holds(item[1]), lambda item=item: sending(item).wait_send())
 
 
-def scatter_chips(operand, collective_id):
-    depth = lax.axis_size("line")
-    chips = PAIR * depth
-    items, hops = count_plan(depth)
+def scatter_chips(operand, collective_id, grid=ALL_CHIPS):
+    depth = lax.axis_size(LINE)
+    chips = chips_in(grid, depth)
+    items, hops = count_plan(grid, depth)
     rows, columns = operand.shape[0] // chips, operand.shape[1]
     landed = sum(
         (last - first) * rows // ROW_UNITS
-        for _, row in routes_of_shards(depth)
+        for _, row in routes_of_shards(grid, depth)
         for _, first, last, _ in row
     )
     return pl.pallas_call(
-        partial(scatter_kernel, depth),
+        partial(scatter_kernel, grid, depth),
         out_shape=jax.ShapeDtypeStruct((rows, columns), operand.dtype),
         in_specs=[pl.BlockSpec(memory_space=pl.ANY)],
         out_specs=pl.BlockSpec(memory_space=pltpu.VMEM),
@@ -830,93 +855,86 @@
             collective_id=collective_id, has_side_effects=True, vmem_limit_bytes=50 * 2**20
         ),
         cost_estimate=pl.CostEstimate(
-            flops=0, bytes_accessed=8 * chips * rows * columns, transcendentals=0
+            flops=0, bytes_accessed=66 * chips * rows * columns, transcendentals=0
         ),
-        name="scatter_chips",
     )(operand.reshape(chips, rows, columns))
 
 
-def spread_experts(operand, place, width):
-    own = lax.dynamic_index_in_dim(operand, place, 0, keepdims=False)
-    pieces = jnp.zeros_like(operand)
-    pieces = lax.dynamic_update_index_in_dim(pieces, own, place, 0)
+def after(operand, *others):
+    there = None
+    for other in others:
+        corner = other[(0,) * other.ndim].astype(jnp.float32)
+        there = (corner == corner) if there is None else there & (corner == corner)
+    return jnp.where(there, operand, jnp.zeros_like(operand))
+
+
+def swap_pieces(piece_of, place, width):
+    pieces = [(place, piece_of(place))]
     for step in range(1, width):
-        sent = lax.dynamic_index_in_dim(operand, place ^ step, 0, keepdims=False)
-        got = lax.ppermute(sent, "fsdp", [(i, i ^ step) for i in range(width)])
-        pieces = lax.dynamic_update_index_in_dim(pieces, got, place ^ step, 0)
+        sent = piece_of(place ^ step)
+        got = lax.ppermute(sent, FSDP, [(i, i ^ step) for i in range(width)])
+        pieces.append((place ^ step, got))
     return pieces
 
 
-def spread_columns(operand, place, width):
-    columns = operand.shape[2]
-    own = lax.dynamic_index_in_dim(operand, place, 0, keepdims=False)
-    whole = jnp.zeros((operand.shape[1], width * columns), operand.dtype)
-    whole = lax.dynamic_update_slice_in_dim(whole, own, place * columns, 1)
-    for step in range(1, width):
-        sent = lax.dynamic_index_in_dim(operand, place ^ step, 0, keepdims=False)
-        got = lax.ppermute(sent, "fsdp", [(i, i ^ step) for i in range(width)])
-        whole = lax.dynamic_update_slice_in_dim(whole, got, (place ^ step) * columns, 1)
-    return whole
-
-
-def pair_scores(query_copy, key_b, allowed):
+def block_scores(query_copy, key_b, allowed):
     return jnp.where(
-        allowed[:, None, None],
-        jnp.einsum("btgjd,bsgd->bgjts", query_copy, key_b, preferred_element_type=jnp.float32)
+        allowed[:, None],
+        jnp.einsum("btjd,bsd->bjts", query_copy, key_b, preferred_element_type=jnp.float32)
         * (1.0 / math.sqrt(HEAD_SIZE)),
         -1e30,
     )
 
 
+def by_owner(operand, width):
+    rows = operand.shape[0]
+    depth = lax.axis_size(LINE)
+    return (
+        operand.reshape(rows, width, depth, 2, -1).transpose(0, 3, 2, 1, 4).reshape(rows, -1)
+    )
+
+
+def by_place(operand, width):
+    rows = operand.shape[0]
+    depth = lax.axis_size(LINE)
+    return (
+        operand.reshape(rows, 2, depth, width, -1).transpose(0, 3, 2, 1, 4).reshape(rows, -1)
+    )
+
+
 def attention_forward(state, dense, angles):
-    core, cosine, sine, allowed = angles
-    w_qkv, w_out, g_attn, g_query, g_key = dense
+    cosine, sine, allowed = angles
+    w_qkv, w_out, normed, g_query, g_key = dense
     rows = state.shape[0]
-    heads = QUERY_HEADS // 2
-    pairs = KEY_VALUE_HEADS // 2
-    group = heads // KEY_VALUE_HEADS
-    normed = norm_rows(state, g_attn).astype(jnp.bfloat16)
-    normed = jnp.concatenate([normed, swap(normed)], axis=0)
+    blocks = allowed.shape[0]
+    heads = QUERY_HEADS // KEY_VALUE_HEADS
+    cut = heads * HEAD_SIZE
     qkv = jnp.dot(normed, w_qkv, preferred_element_type=jnp.float32)
-    query_pre = qkv[:, : heads * HEAD_SIZE].reshape(2 * rows, heads, HEAD_SIZE)
-    key_pre = qkv[:, heads * HEAD_SIZE : (heads + pairs) * HEAD_SIZE].reshape(
-        2 * rows, pairs, HEAD_SIZE
-    )
-    value_half = qkv[:, (heads + pairs) * HEAD_SIZE :].astype(jnp.bfloat16)
+    query_pre = qkv[:, :cut].reshape(-1, heads, HEAD_SIZE)
+    key_pre = qkv[:, cut : cut + HEAD_SIZE].reshape(-1, 1, HEAD_SIZE)
+    value_b = qkv[:, cut + HEAD_SIZE :].astype(jnp.bfloat16).reshape(blocks, rows, HEAD_SIZE)
     query_f, key_f = head_piece(query_pre, key_pre, g_query, g_key, cosine, sine)
-    query_b = query_f.astype(jnp.bfloat16).reshape(2, rows, KEY_VALUE_HEADS, group, HEAD_SIZE)
-    key_half = key_f.astype(jnp.bfloat16).reshape(2 * rows, pairs * HEAD_SIZE)
-    both = jnp.concatenate([key_half, value_half], axis=1)
-    other = turned(swap(both))
-    width = pairs * HEAD_SIZE
-    key_b = by_core(core, key_half, other[:, :width], 1)
-    value_b = by_core(core, value_half, other[:, width:], 1)
-    key_b = key_b.reshape(2, rows, KEY_VALUE_HEADS, HEAD_SIZE)
-    value_b = value_b.reshape(2, rows, KEY_VALUE_HEADS, HEAD_SIZE)
-    scores = pair_scores(query_b, key_b, allowed)
+    query_b = query_f.astype(jnp.bfloat16).reshape(blocks, rows, heads, HEAD_SIZE)
+    key_b = key_f.astype(jnp.bfloat16).reshape(blocks, rows, HEAD_SIZE)
+    scores = block_scores(query_b, key_b, allowed)
     peaks = jnp.max(scores, axis=-1, keepdims=True)
     expos = jnp.exp(scores - peaks)
     totals = jnp.sum(expos, axis=-1, keepdims=True)
     log_total = peaks + jnp.log(totals)
     probs_b = (expos / totals).astype(jnp.bfloat16)
-    attended = jnp.einsum("bgjts,bsgd->btgjd", probs_b, value_b, preferred_element_type=jnp.float32)
-    attended = attended.reshape(2 * rows, heads * HEAD_SIZE).astype(jnp.bfloat16)
+    attended = jnp.einsum("bjts,bsd->btjd", probs_b, value_b, preferred_element_type=jnp.float32)
+    attended = attended.reshape(blocks * rows, cut).astype(jnp.bfloat16)
     partial_out = jnp.dot(attended, w_out, preferred_element_type=jnp.float32)
-    middle = state + (partial_out[:rows] + swap(partial_out[rows:]))
+    middle = state + scatter_chips(partial_out.astype(jnp.bfloat16), 7, PLANE).astype(jnp.float32)
     return middle, (normed, query_pre, key_pre, query_b, key_b, value_b, log_total, attended)
 
 
-def attention_backward(grad_middle, memo, dense, angles):
-    core, cosine, sine, allowed = angles
+def attention_backward(low, memo, dense, angles):
+    cosine, sine, allowed = angles
     normed, query_pre, key_pre, query_b, key_b, value_b, log_total, attended = memo
-    w_qkv, w_out, g_attn, g_query, g_key = dense
-    rows = grad_middle.shape[0]
-    heads = QUERY_HEADS // 2
-    pairs = KEY_VALUE_HEADS // 2
-    width = pairs * HEAD_SIZE
+    w_qkv, w_out, unused_normed, g_query, g_key = dense
+    blocks, rows, heads, size = query_b.shape
     scale = 1.0 / math.sqrt(HEAD_SIZE)
-    low = grad_middle.astype(jnp.bfloat16)
-    low = jnp.concatenate([low, swap(low)], axis=0)
     grad_attended = lax.dot_general(
         low, w_out, (((1,), (1,)), ((), ())), preferred_element_type=jnp.float32
     ).astype(jnp.bfloat16)
@@ -924,48 +942,35 @@
         attended, low, (((0,), (0,)), ((), ())), preferred_element_type=jnp.float32
     ).astype(jnp.bfloat16)
     grad_attended = grad_attended.reshape(query_b.shape)
-    probs = jnp.exp(pair_scores(query_b, key_b, allowed) - log_total)
+    probs = jnp.exp(block_scores(query_b, key_b, allowed) - log_total)
     probs_b = probs.astype(jnp.bfloat16)
     grad_probs = jnp.einsum(
-        "btgjd,bsgd->bgjts", grad_attended, value_b, preferred_element_type=jnp.float32
+        "btjd,bsd->bjts", grad_attended, value_b, preferred_element_type=jnp.float32
     )
     grad_value = jnp.einsum(
-        "bgjts,btgjd->bsgd", probs_b, grad_attended, preferred_element_type=jnp.float32
-    ).reshape(2 * rows, 2 * width)
+        "bjts,btjd->bsd", probs_b, grad_attended, preferred_element_type=jnp.float32
+    )
     grad_scores = (
         probs * (grad_probs - jnp.sum(grad_probs * probs, axis=-1, keepdims=True))
     ).astype(jnp.bfloat16)
     grad_query = (
-        jnp.einsum("bgjts,bsgd->btgjd", grad_scores, key_b, preferred_element_type=jnp.float32)
+        jnp.einsum("bjts,bsd->btjd", grad_scores, key_b, preferred_element_type=jnp.float32) * scale
+    )
+    grad_key = (
+        jnp.einsum("bjts,btjd->bsd", grad_scores, query_b, preferred_element_type=jnp.float32)
         * scale
-    ).reshape(2 * rows, heads, HEAD_SIZE)
-    grad_key = (
-        jnp.einsum("bgjts,btgjd->bsgd", grad_scores, query_b, preferred_element_type=jnp.float32)
-        * scale
-    ).reshape(2 * rows, 2 * width)
-    mine = jnp.where(core == 0, 0, width)
-    theirs = width - mine
-    sent = jnp.concatenate(
-        [
-            lax.dynamic_slice_in_dim(grad_key, theirs, width, 1),
-            lax.dynamic_slice_in_dim(grad_value, theirs, width, 1),
-        ],
-        axis=1,
-    )
-    got = turned(swap(sent))
-    grad_key = lax.dynamic_slice_in_dim(grad_key, mine, width, 1) + got[:, :width]
-    grad_value = lax.dynamic_slice_in_dim(grad_value, mine, width, 1) + got[:, width:]
+    )
     unused_heads, head_back = jax.vjp(
         partial(head_piece, cosine=cosine, sine=sine), query_pre, key_pre, g_query, g_key
     )
     grad_qpre, grad_kpre, grad_gq, grad_gk = head_back(
-        (grad_query, grad_key.reshape(2 * rows, pairs, HEAD_SIZE))
+        (grad_query.reshape(query_pre.shape), grad_key.reshape(key_pre.shape))
     )
     grad_qkv = jnp.concatenate(
         [
-            grad_qpre.astype(jnp.bfloat16).reshape(2 * rows, heads * HEAD_SIZE),
-            grad_kpre.astype(jnp.bfloat16).reshape(2 * rows, width),
-            grad_value.astype(jnp.bfloat16),
+            grad_qpre.astype(jnp.bfloat16).reshape(blocks * rows, heads * size),
+            grad_kpre.astype(jnp.bfloat16).reshape(blocks * rows, size),
+            grad_value.astype(jnp.bfloat16).reshape(blocks * rows, size),
         ],
         axis=1,
     )
@@ -974,9 +979,21 @@
     ).astype(jnp.bfloat16)
     grad_normed = lax.dot_general(
         grad_qkv, w_qkv, (((1,), (1,)), ((), ())), preferred_element_type=jnp.float32
-    )
-    grad_normed = grad_normed[:rows] + swap(grad_normed[rows:])
-    return grad_normed, grad_wqkv, grad_wout, grad_gq, grad_gk
+    ).astype(jnp.bfloat16)
+    return scatter_chips(grad_normed, 7, PLANE), grad_wqkv, grad_wout, grad_gq, grad_gk
+
+
+def send_back(picks, pieces):
+    return (
+        jnp.einsum(
+            SPREAD,
+            jnp.concatenate(picks, axis=1),
+            jnp.concatenate(pieces, axis=1),
+            preferred_element_type=jnp.float32,
+        )
+        .astype(jnp.bfloat16)
+        .reshape(-1, pieces[0].shape[2])
+    )
 
 
 def expert_forward(gathered, picks, row_gates, weights):
@@ -984,10 +1001,10 @@
     width = gathered.shape[1]
     grouped = gathered.reshape(blocks, -1, width)
     memo = []
-    total = None
+    pieces = []
     for pick, row_gate, (w_up_gate, w_down) in zip(picks, row_gates, weights):
         hidden_size = w_down.shape[0]
-        rows = jnp.einsum("bst,btd->bsd", pick, grouped, preferred_element_type=jnp.float32)
+        rows = jnp.einsum(PICK, pick, grouped, preferred_element_type=jnp.float32)
         rows = rows.astype(jnp.bfloat16).reshape(-1, width)
         pre = jnp.dot(rows, w_up_gate, preferred_element_type=jnp.float32)
         gate_pre = pre[:, :hidden_size]
@@ -995,37 +1012,33 @@
         hidden = (jax.nn.silu(gate_pre) * up_pre).astype(jnp.bfloat16)
         produced = jnp.dot(hidden, w_down, preferred_element_type=jnp.float32)
         produced = (produced * row_gate).astype(jnp.bfloat16)
-        back = jnp.einsum(
-            "bst,bsd->btd",
-            pick,
-            produced.reshape(blocks, -1, width),
-            preferred_element_type=jnp.float32,
-        )
-        total = back if total is None else total + back
+        pieces.append(produced.reshape(blocks, -1, width))
         memo.append((rows, gate_pre, up_pre, hidden))
-    return total.reshape(-1, width).astype(jnp.bfloat16), memo
-
-
-def expert_backward(gathered, picks, row_gates, weights, memo):
+    return send_back(picks, pieces), memo
+
+
+def expert_backward(gathered, picks, row_gates, weights, memo, experts):
     blocks = picks[0].shape[0]
     width = gathered.shape[1]
     grouped = gathered.reshape(blocks, -1, width)
-    total = None
+    pieces = []
     grads = []
-    gate_grads = []
-    for pick, row_gate, (w_up_gate, w_down), kept in zip(picks, row_gates, weights, memo):
+    for pick, row_gate, (w_up_gate, w_down), kept, expert in zip(
+        picks, row_gates, weights, memo, experts
+    ):
         rows, gate_pre, up_pre, hidden = kept
-        grad_rows = jnp.einsum("bst,btd->bsd", pick, grouped, preferred_element_type=jnp.float32)
+        grad_rows = jnp.einsum(PICK, pick, grouped, preferred_element_type=jnp.float32)
         grad_rows = grad_rows.astype(jnp.bfloat16).reshape(-1, width)
         through = lax.dot_general(
             grad_rows, w_down, (((1,), (1,)), ((), ())), preferred_element_type=jnp.float32
         )
         hidden_f = hidden.astype(jnp.float32)
-        gate_grad = jnp.sum(hidden_f * through, axis=1)
-        gate_grads.append(
-            jnp.sum(
-                pick.astype(jnp.float32) * gate_grad.reshape(blocks, -1)[:, :, None], axis=1
-            ).reshape(-1)
+        gate_grad = jnp.sum(hidden_f * through, axis=1, keepdims=True)
+        high = gate_grad.astype(jnp.bfloat16)
+        low = (gate_grad - high.astype(jnp.float32)).astype(jnp.bfloat16)
+        column = jnp.arange(GATE_COLUMNS, dtype=jnp.int32)[None, :]
+        gate_part = jnp.where(
+            column == expert, high, jnp.where(column == expert + EXPERTS, low, 0)
         )
         grad_hidden = through * row_gate
         sigmoid_gate = jax.nn.sigmoid(gate_pre)
@@ -1050,15 +1063,10 @@
         grad_in = lax.dot_general(
             grad_pre, w_up_gate, (((1,), (1,)), ((), ())), preferred_element_type=jnp.float32
         ).astype(jnp.bfloat16)
-        back = jnp.einsum(
-            "bst,bsd->btd",
-            pick,
-            grad_in.reshape(blocks, -1, width),
-            preferred_element_type=jnp.float32,
-        )
-        total = back if total is None else total + back
+        piece = jnp.concatenate([grad_in, gate_part], axis=1)
+        pieces.append(piece.reshape(blocks, -1, width + GATE_COLUMNS))
         grads.append((grad_up_gate, grad_down))
-    return total.reshape(-1, width).astype(jnp.bfloat16), grads, gate_grads
+    return send_back(picks, pieces), grads
 
 
 def chip_shards(
@@ -1077,14 +1085,15 @@
     w_down,
 ):
     rows = tokens.shape[0]
-    width = lax.axis_size("fsdp")
-    place = lax.axis_index("fsdp")
-    line = lax.axis_index("line")
-    core = lax.axis_index("core")
-    devices = width * lax.axis_size("line") * 2
+    width = lax.axis_size(FSDP)
+    place = lax.axis_index(FSDP)
+    line = lax.axis_index(LINE)
+    core = lax.axis_index(CORE)
+    devices = width * lax.axis_size(LINE) * 2
     chips = devices // 2
-    chip = place * lax.axis_size("line") + line
-    half_heads = QUERY_HEADS // 2
+    chip = place * lax.axis_size(LINE) + line
+    depth = lax.axis_size(LINE)
+    group = QUERY_HEADS // KEY_VALUE_HEADS
     ff = w_gate.shape[3]
     short = w_query.shape[1]
     experts_here = w_gate.shape[1]
@@ -1098,9 +1107,53 @@
     router_columns = DECODER_LAYERS * EXPERTS
     cut = side.shape[1]
     small = jnp.concatenate(
-        [side] + [routes[number].astype(jnp.bfloat16) for number in range(DECODER_LAYERS)], axis=1
-    )
-    small = offload_gather(jnp.pad(small, ((0, 0), (0, -small.shape[1] % 128))))
+        [side]
+        + [routes[number].astype(jnp.bfloat16) for number in range(DECODER_LAYERS)]
+        + [jnp.broadcast_to(lengths.astype(jnp.bfloat16), (rows, lengths.shape[1]))],
+        axis=1,
+    )
+    small = jnp.pad(small, ((0, 0), (0, -small.shape[1] % 128)))
+
+    small = gather_chips(small, 1)
+
+    qkv_columns = (group + 2) * HEAD_SIZE
+
+    def columns_of(number):
+        return jnp.concatenate(
+            [
+                w_query[number]
+                .reshape(short, width, depth, 2, HEAD_SIZE)
+                .transpose(1, 0, 3, 2, 4)
+                .reshape(width, short, group * HEAD_SIZE),
+                key_weight[number].reshape(short, width, HEAD_SIZE).transpose(1, 0, 2),
+                value_weight[number].reshape(short, width, HEAD_SIZE).transpose(1, 0, 2),
+            ],
+            axis=2,
+        )
+
+    def rows_by_source(source):
+        whole = jnp.zeros((width, short, qkv_columns), jnp.bfloat16)
+        for origin, piece in swap_pieces(
+            lambda to: lax.dynamic_index_in_dim(source, to, 0, keepdims=False), place, width
+        ):
+            whole = lax.dynamic_update_index_in_dim(whole, piece, origin, 0)
+        return whole.reshape(width * short, qkv_columns)
+
+    def line_gather(operand):
+        return lax.all_gather(operand, LINE, axis=0, tiled=True)
+
+    def both_cores(operand):
+        return by_core(core, operand, swap(operand), 0)
+
+    first_rows = gather_chips(rows_by_source(columns_of(0)), 8, LINE_ONLY)
+    dense_qkv = [both_cores(first_rows)]
+    dense_out = [both_cores(line_gather(w_out[0]))]
+    for number in range(1, DECODER_LAYERS):
+        dense_qkv.append(
+            both_cores(line_gather(after(rows_by_source(columns_of(number)), first_rows)))
+        )
+        dense_out.append(both_cores(line_gather(after(w_out[number], first_rows))))
+    cotangent_all = offload_gather(after(cotangent, first_rows))
     routers = [
         small[:, number * EXPERTS : (number + 1) * EXPERTS] for number in range(DECODER_LAYERS)
     ]
@@ -1117,6 +1170,12 @@
         .reshape(chips, rows, DECODER_LAYERS, TOP)
         .transpose(0, 2, 1, 3)
     )
+    cut = cut + DECODER_LAYERS * TOP
+    all_lengths = (
+        small.reshape(width, depth, rows, -1)[:, :, 0, cut : cut + lengths.shape[1]]
+        .astype(jnp.int32)
+    )
+    all_lengths = lax.dynamic_index_in_dim(all_lengths, line, 1, keepdims=False)
     chosen = jnp.any(
         all_routes[..., None] == jnp.arange(EXPERTS, dtype=jnp.bfloat16), axis=3
     )
@@ -1138,47 +1197,38 @@
 
     picks = [(pick_of(number, first), pick_of(number, second)) for number in range(DECODER_LAYERS)]
 
-    other_lengths = swap(lengths)
-    here = geometry(lengths, rows)
-    there = geometry(other_lengths, rows)
-    cosine = jnp.concatenate([here[0], there[0]], axis=0)
-    sine = jnp.concatenate([here[1], there[1]], axis=0)
-    allowed = jnp.stack([here[2], there[2]])
-    angles = (core, cosine, sine, allowed)
-
-    heads = w_query.reshape(DECODER_LAYERS, short, half_heads, 2, HEAD_SIZE)
-    pair_width = KEY_VALUE_HEADS // 2 * HEAD_SIZE
-
-    def columns_of(which):
-        return jnp.concatenate(
-            [
-                lax.dynamic_index_in_dim(heads, which, 3, keepdims=False).reshape(
-                    DECODER_LAYERS, short, half_heads * HEAD_SIZE
-                ),
-                lax.dynamic_slice_in_dim(key_weight, which * pair_width, pair_width, 2),
-                lax.dynamic_slice_in_dim(value_weight, which * pair_width, pair_width, 2),
-            ],
-            axis=2,
-        )
-
-    chip_qkv = by_core(core, columns_of(core), swap(columns_of(1 - core)), 1)
+    cosine, sine, allowed = jax.vmap(lambda own: geometry(own[None], rows))(all_lengths)
+    angles = (
+        cosine.reshape(width * rows, 1, -1),
+        sine.reshape(width * rows, 1, -1),
+        allowed,
+    )
     g_attn, g_ffn, g_query, g_key = zip(*[split_gains(all_gains[i]) for i in range(DECODER_LAYERS)])
 
     state = tokens.astype(jnp.float32)
     kept = []
     for number in range(DECODER_LAYERS):
-        first_layer = number == 0
-        dense = (
-            gather_chips(chip_qkv[number], 1) if first_layer else offload_gather(chip_qkv[number]),
-            offload_gather(w_out[number]),
-            g_attn[number],
-            g_query[number],
-            g_key[number],
-        )
-        up_gate = spread_experts(
-            jnp.concatenate([w_gate[number], w_up[number]], axis=2), place, width
-        ).reshape(MODEL_WIDTH, 2 * ff)
-        down = spread_columns(w_down[number], place, width)
+        normed = norm_rows(state, g_attn[number]).astype(jnp.bfloat16)
+        normed = gather_chips(by_owner(normed, width), 6, PLANE)
+        dense = (dense_qkv[number], dense_out[number], normed, g_query[number], g_key[number])
+        ready = small if number == 0 else gathered
+        gate_up_source = after(
+            jnp.concatenate([w_gate[number], w_up[number]], axis=2).reshape(-1, 2 * ff), ready
+        ).reshape(width, -1, 2 * ff)
+        down_source = after(w_down[number].reshape(-1, w_down.shape[3]), ready).reshape(
+            width, ff, -1
+        )
+        up_gate = jnp.zeros((width, MODEL_WIDTH // width, 2 * ff), jnp.bfloat16)
+        for origin, piece in swap_pieces(
+            lambda to: lax.dynamic_index_in_dim(gate_up_source, to, 0, keepdims=False), place, width
+        ):
+            up_gate = lax.dynamic_update_index_in_dim(up_gate, piece, origin, 0)
+        up_gate = up_gate.reshape(MODEL_WIDTH, 2 * ff)
+        down = jnp.zeros((ff, MODEL_WIDTH), jnp.bfloat16)
+        for origin, piece in swap_pieces(
+            lambda to: lax.dynamic_index_in_dim(down_source, to, 0, keepdims=False), place, width
+        ):
+            down = lax.dynamic_update_slice_in_dim(down, piece, origin * piece.shape[1], 1)
         weights = ((up_gate, down), (swap(up_gate), swap(down)))
         middle, memo = attention_forward(state, dense, angles)
         mixer_in = norm_rows(middle, g_ffn[number]).astype(jnp.bfloat16)
@@ -1205,20 +1255,41 @@
 
     grad_state = cotangent.astype(jnp.float32)
     grad_low = cotangent
-    grad_gathered = offload_gather(cotangent)
-    outs = []
+    grad_gathered = cotangent_all
     small_grads = []
+    d_out = []
+    d_qkv = []
+    share = MODEL_WIDTH // width
+    d_up_gate = jnp.zeros((DECODER_LAYERS, width, share, 2 * ff), jnp.bfloat16)
+    d_down = jnp.zeros((DECODER_LAYERS, width, ff, share), jnp.bfloat16)
     for number in reversed(range(DECODER_LAYERS)):
         state, middle, mixer_in, own_gates, row_gates, dense, weights, memo, expert_memo = kept[
             number
         ]
-        back, expert_grads, gate_grads = expert_backward(
-            grad_gathered, picks[number], row_gates, weights, expert_memo
-        )
-        spread = jnp.zeros((chips * rows, EXPERTS), jnp.float32)
-        for gate_grad, expert in zip(gate_grads, (first, second)):
-            spread = lax.dynamic_update_index_in_dim(spread, gate_grad, expert, 1)
-        grad_gates = offload_scatter(spread)
+        back, expert_grads = expert_backward(
+            grad_gathered, picks[number], row_gates, weights, expert_memo, (first, second)
+        )
+        (own_up_gate, own_down), (other_up_gate, other_down) = expert_grads
+        grad_up_gate = own_up_gate + swap(other_up_gate)
+        grad_down = own_down + swap(other_down)
+        received = []
+        for origin, piece in swap_pieces(
+            lambda to: lax.dynamic_slice_in_dim(grad_up_gate, to * share, share, 0), place, width
+        ):
+            received.append(piece)
+            d_up_gate = lax.dynamic_update_slice(
+                d_up_gate, piece[None, None], (number, origin, 0, 0)
+            )
+        for origin, piece in swap_pieces(
+            lambda to: lax.dynamic_slice_in_dim(grad_down, to * share, share, 1), place, width
+        ):
+            received.append(piece)
+            d_down = lax.dynamic_update_slice(d_down, piece[None, None], (number, origin, 0, 0))
+        back = scatter_chips(back, 5).astype(jnp.float32)
+        grad_gates = (
+            back[:, MODEL_WIDTH : MODEL_WIDTH + EXPERTS]
+            + back[:, MODEL_WIDTH + EXPERTS : MODEL_WIDTH + 2 * EXPERTS]
+        )
         grad_logits = (
             own_gates
             * (grad_gates - jnp.sum(own_gates * grad_gates, axis=1, keepdims=True))
@@ -1226,7 +1297,7 @@
         grad_router = lax.dot_general(
             mixer_in, grad_logits, (((0,), (0,)), ((), ())), preferred_element_type=jnp.float32
         )
-        grad_mixer = scatter_chips(back, 3).astype(jnp.float32) + lax.dot_general(
+        grad_mixer = back[:, :MODEL_WIDTH] + lax.dot_general(
             grad_logits,
             routers[number],
             (((1,), (1,)), ((), ())),
@@ -1235,34 +1306,38 @@
         unused_mid, norm_back = jax.vjp(norm_rows, middle, g_ffn[number])
         grad_mid_part, grad_g_ffn = norm_back(grad_mixer)
         grad_middle = grad_state + grad_mid_part
+        low = gather_chips(after(grad_middle.astype(jnp.bfloat16), grad_up_gate, grad_down), 6, PLANE)
         grad_normed, grad_wqkv, grad_wout, grad_gq, grad_gk = attention_backward(
-            grad_middle, memo, dense, angles
-        )
+            low, memo, dense, angles
+        )
+        grad_normed = by_place(grad_normed.astype(jnp.float32), width)
         unused_state, norm_front = jax.vjp(norm_rows, state, g_attn[number])
         grad_in_part, grad_g_attn = norm_front(grad_normed)
         grad_state = grad_middle + grad_in_part
         grad_low = grad_state.astype(jnp.bfloat16)
         if number > 0:
-            grad_gathered = gather_chips(grad_low, 2)
-
-        (own_up_gate, own_down), (other_up_gate, other_down) = expert_grads
-        grad_up_gate = own_up_gate + swap(other_up_gate)
-        grad_down = own_down + swap(other_down)
-        d_up_gate = spread_experts(
-            grad_up_gate.reshape(width, MODEL_WIDTH // width, 2 * ff), place, width
-        ).astype(jnp.float32)
-        d_down = spread_experts(
-            grad_down.reshape(ff, width, MODEL_WIDTH // width).transpose(1, 0, 2), place, width
-        ).astype(jnp.float32)
-        d_out = offload_scatter(grad_wout).astype(jnp.float32)
+            grad_gathered = gather_chips(after(grad_low, *received), 2)
+
+        def line_sum(operand):
+            half = operand.shape[0] // 2
+            mine = lax.dynamic_slice_in_dim(operand, core * half, half, 0)
+            other = swap(lax.dynamic_slice_in_dim(operand, (1 - core) * half, half, 0))
+            return lax.psum_scatter(mine + other, LINE, scatter_dimension=0, tiled=True)
+
+        d_out.insert(0, line_sum(grad_wout).astype(jnp.float32))
+        summed = line_sum(grad_wqkv).reshape(width, short, qkv_columns)
+        whole = jnp.zeros_like(summed)
+        for origin, piece in swap_pieces(
+            lambda to: lax.dynamic_index_in_dim(summed, to, 0, keepdims=False), place, width
+        ):
+            whole = lax.dynamic_update_index_in_dim(whole, piece, origin, 0)
+        d_qkv.insert(0, whole)
         gain_grads = jnp.concatenate([grad_g_attn, grad_g_ffn, grad_gq, grad_gk])
-        outs.insert(
-            0, (d_out, d_up_gate[:, :, :ff], d_up_gate[:, :, ff:], d_down)
-        )
         small_grads.insert(0, (grad_router, gain_grads.reshape(devices, -1)))
-        if number > 0:
-            d_qkv = offload_scatter(grad_wqkv)
-    d_out, d_gate, d_up, d_down = [jnp.stack([entry[i] for entry in outs]) for i in range(4)]
+    d_out = jnp.stack(d_out)
+    d_gate = d_up_gate[..., :ff].astype(jnp.float32)
+    d_up = d_up_gate[..., ff:].astype(jnp.float32)
+    d_down = d_down.astype(jnp.float32)
     own_gains = jnp.concatenate([gain_grad for _, gain_grad in small_grads], axis=1)
     own_gains = jnp.pad(own_gains, ((0, 0), (0, gain_columns * short - gains.size)))
     side = jnp.concatenate(
@@ -1270,14 +1345,7 @@
         axis=1,
     ).astype(jnp.bfloat16)
     side = jnp.pad(side, ((0, 0), (0, -side.shape[1] % 128)))
-    qkv_columns = grad_wqkv.shape[1]
-    last = scatter_chips(jnp.concatenate([grad_wqkv, side], axis=1), 4).astype(jnp.float32)
-    d_qkv = d_qkv.astype(jnp.float32)
-    first_qkv = last[:, :qkv_columns]
-    side = last[:, qkv_columns:]
-    d_qkv = jnp.stack([first_qkv, d_qkv])
-    mine = lax.dynamic_slice_in_dim(d_qkv, core * short, short, 1)
-    got = swap(lax.dynamic_slice_in_dim(d_qkv, (1 - core) * short, short, 1))
+    side = scatter_chips(side, 4).astype(jnp.float32)
     small = lax.dynamic_slice_in_dim(side, core * short, short, 0) + swap(
         lax.dynamic_slice_in_dim(side, (1 - core) * short, short, 0)
     )
@@ -1286,14 +1354,16 @@
     )
     d_gains = small[:, router_columns : router_columns + gain_columns].reshape(-1)[: gains.size]
     d_gains = d_gains.reshape(gains.shape)
-    q_width = half_heads * HEAD_SIZE
-    side = (DECODER_LAYERS, short, half_heads, 1, HEAD_SIZE)
-    d_query = by_core(
-        core, mine[..., :q_width].reshape(side), got[..., :q_width].reshape(side), 3
-    ).reshape(w_query.shape)
-    cut = q_width + pair_width
-    d_key = by_core(core, mine[..., q_width:cut], got[..., q_width:cut], 2)
-    d_value = by_core(core, mine[..., cut:], got[..., cut:], 2)
+    d_qkv = jnp.stack(d_qkv).astype(jnp.float32)
+    cut = group * HEAD_SIZE
+    d_query = (
+        d_qkv[..., :cut]
+        .reshape(DECODER_LAYERS, width, short, 2, depth, HEAD_SIZE)
+        .transpose(0, 2, 1, 4, 3, 5)
+        .reshape(w_query.shape)
+    )
+    d_key = d_qkv[..., cut : cut + HEAD_SIZE].transpose(0, 2, 1, 3).reshape(key_weight.shape)
+    d_value = d_qkv[..., cut + HEAD_SIZE :].transpose(0, 2, 1, 3).reshape(value_weight.shape)
     return (
         result,
         grad_low,
@@ -1311,10 +1381,10 @@
 
 def by_chip(mesh):
     grid = Mesh(
-        mesh.devices.reshape(mesh.shape["fsdp"], mesh.shape["expert"] // 2, 2),
-        ("fsdp", "line", "core"),
-    )
-    experts = ("line", "core")
+        mesh.devices.reshape(mesh.shape[FSDP], mesh.shape["expert"] // 2, 2),
+        EVERY,
+    )
+    experts = (LINE, CORE)
     return jax.shard_map(
         chip_shards,
         mesh=grid,
@@ -1329,9 +1399,9 @@
             P(None, EVERY, None),
             P(None, EVERY, None),
             P(None, EVERY, None),
-            P(None, experts, "fsdp", None),
-            P(None, experts, "fsdp", None),
-            P(None, experts, None, "fsdp"),
+            P(None, experts, FSDP, None),
+            P(None, experts, FSDP, None),
+            P(None, experts, None, FSDP),
         ),
         out_specs=(
             P(EVERY, None),
@@ -1342,17 +1412,17 @@
             P(None, EVERY, None),
             P(None, EVERY, None),
             P(None, EVERY, None),
-            P(None, experts, "fsdp", None),
-            P(None, experts, "fsdp", None),
-            P(None, experts, None, "fsdp"),
+            P(None, experts, FSDP, None),
+            P(None, experts, FSDP, None),
+            P(None, experts, None, FSDP),
         ),
         check_vma=False,
     )
 
 
 def solution(mesh):
-    width = mesh.shape["fsdp"]
+    width = mesh.shape[FSDP]
     peers = mesh.shape["expert"]
-    if width == 4 and peers % 2 == 0 and peers * width == EXPERTS:
+    if width == KEY_VALUE_HEADS == PAIR and peers * width == EXPERTS == QUERY_HEADS:
         return by_chip(mesh)
     return general(mesh)

time: 2290 us -> 1830 us (0.80)
  waiting for transfers between devices: 474 us -> 201 us
  matrix products: 393 us -> 296 us
  Pallas kernels: 931 us -> 877 us
  blocking collectives: 51.3 us -> 0 us
  local copies, waits for them, and re-layouts: 245 us -> 219 us
    ppermute x49 -> x54, waiting for transfers between devices: 404 us -> 201 us  [the longest x36 201 us: swap_pieces(): got = lax.ppermute(sent, FSDP, [(i, i ^ step) for i in range(width)])]
    dot_general x28 -> x24, matrix products: 127 us -> 57.2 us  [the longest x4 19.3 us: send_back(): jnp.einsum(SPREAD, jnp.concatenate(picks, axis=1), jnp.concatenate(pieces...]
    reduce_scatter x5 -> x4, waiting for transfers between devices: 69.2 us -> 0.03 us  [line_sum(): return lax.psum_scatter(mine + other, LINE, scatter_dimension=0, tiled=True)]
    pallas_call x9 -> x18, Pallas kernels: 931 us -> 877 us  [the longest x9 448 us: scatter_chips(): pl.pallas_call(partial(scatter_kernel, grid, depth), out_shape=jax.ShapeD...]
    all_gather x1 -> x0, blocking collectives: 51.3 us -> none  [offload_gather(): return lax.all_gather(operand, CHIPS, axis=0, tiled=True)]
    another operation x15 -> x14, local copies, waits for them, and re-layouts: 49.8 us -> 8.73 us
    another operation x14 -> x7, other arithmetic: 38.5 us -> 10.3 us  [the longest x4 30 us: chip_shards(): jnp.stack([entry[i] for entry in outs])]
    unnamed x488 -> x491, local copies, waits for them, and re-layouts: 51.2 us -> 35.7 us
  transfers between devices with their start and end apart: 58 -> 62, of which waited for: 14 -> 13; matrix products, arithmetic and copies ran while one was open for 27% -> 31% of each run, Pallas kernels for 35% -> 44%
where the time goes in v2:
time: 1830 us; the launch traced here: 1820 us
  Pallas kernels  877 us (48%)
  matrix products  296 us (16%)
  local copies, waits for them, and re-layouts  219 us (12%)
  waiting for transfers between devices  201 us (11%)
  other arithmetic  139 us (8%)
  starting transfers between devices  47.5 us (3%)
  between operations  38.2 us (2%)
    pallas_call x9, Pallas kernels, scatter_chips(): pl.pallas_call(partial(scatter_kernel, grid, depth), out_shape=jax.ShapeD...  448 us
    pallas_call x9, Pallas kernels, gather_chips(): pl.pallas_call(partial(gather_kernel, grid, depth), out_shape=jax.ShapeDt...  428 us
    ppermute x36, waiting for transfers between devices, swap_pieces(): got = lax.ppermute(sent, FSDP, [(i, i ^ step) for i in range(width)])  201 us
    ppermute x36, starting transfers between devices, swap_pieces(): got = lax.ppermute(sent, FSDP, [(i, i ^ step) for i in range(width)])  43.8 us
  transfers between devices with their start and end apart: 62, of which 13 were waited for; matrix products, arithmetic and copies ran while one was open for 31% of the time, Pallas kernels for 44%

profile of v2, /device:TPU:0, one launch (start us, length us, event | category | flops | bytes accessed | tf_op | source)
XLA Modules:
  0.0 1816.7 jit_solution(3374251995898517262)
XLA Ops:
  28.8 44.2 %shard_map.214 = bf16[4,256,1280]{2,1,0:T(8,128)(2,1)} custom-call(bf16[256,1280]{1,0:T(8,128)(2,1)} %bitcast.615), custom_call_target="tpu_custom_call" | custom-call | bytes 86507520 | tf_op jit(solution)/shard_map/pallas_call | solution.py:745
  78.6 9.2 slice_bitcast_fusion
  89.3 24.9 %shard_map.212 = bf16[16,128,128]{2,1,0:T(8,128)(2,1)} custom-call(bf16[128,128]{1,0:T(8,128)(2,1)} %pad.42.x_ref), custom_call_target="tpu_custom_call" | custom-call | bytes 17301504 | tf_op jit(solution)/shard_map/pallas_call | solution.py:745
  144.9 40.4 %shard_map.213 = bf16[4,128,2048]{2,1,0:T(8,128)(2,1)} custom-call(bf16[128,2048]{1,0:T(8,128)(2,1)} %copy.414.x_ref), custom_call_target="tpu_custom_call" | custom-call | bytes 69206016 | tf_op jit(solution)/shard_map/pallas_call | solution.py:745
  197.0 17.9 collective-permute-done.8
  216.1 6.3 fusion.94
  250.5 31.0 %shard_map.215 = bf16[128,2048]{1,0:T(8,128)(2,1)S(1)} custom-call(bf16[4,128,2048]{2,1,0:T(8,128)(2,1)S(1)} %bitcast.538), custom_call_target="tpu_custom_call" | custom-call | bytes 69206016 | tf_op jit(solution)/shard_map/pallas_call | solution.py:842
  282.8 115.9 %shard_map.216 = bf16[16,128,2048]{2,1,0:T(8,128)(2,1)} custom-call(bf16[128,2048]{1,0:T(8,128)(2,1)} %multiply_convert_fusion.18.x_ref), custom_call_target="tpu_custom_call" | custom-call | bytes 276824064 | tf_op jit(solution)/shard_map/pallas_call | solution.py:745
  467.0 45.8 %collective-permute-done.24 = bf16[768,512]{1,0:T(8,128)(2,1)} collective-permute-done((bf16[768,512]{1,0:T(8,128)(2,1)}, bf16[768,512]{1,0:T(8,128)(2,1)}, u32[]{:S(2)}, u32[]{:S(2)}) %collective-permute-start.24) | collective-permute-done | bytes 786464 | tf_op jit(solution)/shard_map/ppermute | solution.py:875
  516.3 6.5 multiply_convert_fusion.3
  524.1 21.8 %collective-permute-done.20 = bf16[512,1536]{1,0:T(8,128)(2,1)} collective-permute-done((bf16[512,1536]{1,0:T(8,128)(2,1)}, bf16[512,1536]{1,0:T(8,128)(2,1)}, u32[]{:S(2)}, u32[]{:S(2)}) %collective-permute-start.20) | collective-permute-done | bytes 1572896 | tf_op jit(solution)/shard_map/ppermute | solution.py:875
  551.7 7.1 fusion.231
  571.6 67.6 %shard_map.217 = bf16[128,2048]{1,0:T(8,128)(2,1)S(1)} custom-call(bf16[16,128,2048]{2,1,0:T(8,128)(2,1)} %fusion.19.x_ref), custom_call_target="tpu_custom_call" | custom-call | bytes 276824064 | tf_op jit(solution)/shard_map/pallas_call | solution.py:842
  641.1 20.2 %shard_map.218 = bf16[4,128,2048]{2,1,0:T(8,128)(2,1)} custom-call(bf16[128,2048]{1,0:T(8,128)(2,1)} %copy.434.x_ref), custom_call_target="tpu_custom_call" | custom-call | bytes 69206016 | tf_op jit(solution)/shard_map/pallas_call | solution.py:745
  661.4 7.1 fusion.93
  691.5 17.2 shard_map.219
  710.0 71.3 %shard_map.220 = bf16[16,128,2048]{2,1,0:T(8,128)(2,1)} custom-call(bf16[128,2048]{1,0:T(8,128)(2,1)} %multiply_convert_fusion.16.x_ref), custom_call_target="tpu_custom_call" | custom-call | bytes 276824064 | tf_op jit(solution)/shard_map/pallas_call | solution.py:745
  801.4 10.6 fusion.232
  812.0 9.5 fusion.233
  829.0 8.0 multiply_convert_fusion.11
  842.3 6.8 multiply_convert_fusion.9
  862.8 59.3 %shard_map.221 = bf16[128,2048]{1,0:T(8,128)(2,1)S(1)} custom-call(bf16[16,128,2048]{2,1,0:T(8,128)(2,1)} %fusion.16.x_ref), custom_call_target="tpu_custom_call" | custom-call | bytes 276824064 | tf_op jit(solution)/shard_map/pallas_call | solution.py:842
  922.3 8.1 convolution_convert_fusion.6
  931.4 7.5 convolution_convert_fusion.24
  940.6 8.1 convolution_convert_fusion.25
  953.9 71.2 %shard_map.222 = bf16[128,2176]{1,0:T(8,128)(2,1)S(1)} custom-call(bf16[16,128,2176]{2,1,0:T(8,128)(2,1)} %convolution_convert_fusion.1.x_ref), custom_call_target="tpu_custom_call" | custom-call | bytes 294125568 | tf_op jit(solution)/shard_map/pallas_call | solution.py:842
  1043.9 7.2 collective-permute-done.32
  1052.9 11.3 collective-permute-done.33
  1070.7 7.9 fusion.14
  1085.3 18.8 %shard_map.223 = bf16[4,128,2048]{2,1,0:T(8,128)(2,1)} custom-call(bf16[128,2048]{1,0:T(8,128)(2,1)} %convert_select_fusion.2.x_ref), custom_call_target="tpu_custom_call" | custom-call | bytes 69206016 | tf_op jit(solution)/shard_map/pallas_call | solution.py:745
  1143.8 55.0 %shard_map.224 = bf16[128,2048]{1,0:T(8,128)(2,1)S(1)} custom-call(bf16[4,128,2048]{2,1,0:T(8,128)(2,1)S(1)} %bitcast.537), custom_call_target="tpu_custom_call" | custom-call | bytes 69206016 | tf_op jit(solution)/shard_map/pallas_call | solution.py:842
  1230.7 73.5 %shard_map.225 = bf16[16,128,2048]{2,1,0:T(8,128)(2,1)} custom-call(bf16[128,2048]{1,0:T(8,128)(2,1)} %get-tuple-element.112.x_ref), custom_call_target="tpu_custom_call" | custom-call | bytes 276824064 | tf_op jit(solution)/shard_map/pallas_call | solution.py:745
  1321.3 7.4 convolution_convert_fusion.4
  1329.6 8.4 convolution_convert_fusion.22
  1344.0 6.4 convolution_convert_fusion.23
  1362.6 105.4 %shard_map.226 = bf16[128,2176]{1,0:T(8,128)(2,1)S(1)} custom-call(bf16[16,128,2176]{2,1,0:T(8,128)(2,1)} %convolution_convert_fusion.x_ref), custom_call_target="tpu_custom_call" | custom-call | bytes 294125568 | tf_op jit(solution)/shard_map/pallas_call | solution.py:842
  1501.3 8.8 collective-permute-done.51
  1512.2 14.4 collective-permute-done.52
  1529.7 9.5 convert_element_type.718
  1539.1 8.0 fusion.15
  1552.9 18.9 %shard_map.227 = bf16[4,128,2048]{2,1,0:T(8,128)(2,1)} custom-call(bf16[128,2048]{1,0:T(8,128)(2,1)} %convert_select_fusion.x_ref), custom_call_target="tpu_custom_call" | custom-call | bytes 69206016 | tf_op jit(solution)/shard_map/pallas_call | solution.py:745
  1571.8 6.6 fusion.45
  1623.6 7.0 convolution_convert_fusion.28
  1630.6 22.1 %shard_map.228 = bf16[128,2048]{1,0:T(8,128)(2,1)S(1)} custom-call(bf16[4,128,2048]{2,1,0:T(8,128)(2,1)S(1)} %bitcast.536), custom_call_target="tpu_custom_call" | custom-call | bytes 69206016 | tf_op jit(solution)/shard_map/pallas_call | solution.py:842
  1658.0 19.6 %shard_map.229 = bf16[128,128]{1,0:T(8,128)(2,1)S(1)} custom-call(bf16[16,128,128]{2,1,0:T(8,128)(2,1)S(1)} %bitcast.540), custom_call_target="tpu_custom_call" | custom-call | bytes 17301504 | tf_op jit(solution)/shard_map/pallas_call | solution.py:842
  1704.2 32.0 %collective-permute-done.48 = bf16[512,1536]{1,0:T(8,128)(2,1)} collective-permute-done((bf16[512,1536]{1,0:T(8,128)(2,1)}, bf16[512,1536]{1,0:T(8,128)(2,1)}, u32[]{:S(2)}, u32[]{:S(2)}) %collective-permute-start.48) | collective-permute-done | bytes 1572896 | tf_op jit(solution)/shard_map/ppermute | solution.py:875
  1738.8 31.0 %collective-permute-done.49 = bf16[512,1536]{1,0:T(8,128)(2,1)} collective-permute-done((bf16[512,1536]{1,0:T(8,128)(2,1)}, bf16[512,1536]{1,0:T(8,128)(2,1)}, u32[]{:S(2)}, u32[]{:S(2)}) %collective-permute-start.49) | collective-permute-done | bytes 1572896 | tf_op jit(solution)/shard_map/ppermute | solution.py:875
  1773.8 12.7 slice_convert_fusion
  (979 shorter events, 543.0 us)
Async XLA Ops:
  7.2 224.0 %all-gather.11.cloned.1.call-start = ((), (), s32[]{:S(2)}) async-start(), calls=%async_computation.10 | async-start | bytes 2621440 | tf_op jit(solution)/shard_map/all_gather | solution.py:1143
  9.2 79.3 %collective-permute-start = (bf16[64,69]{1,0:T(8,128)(2,1)S(1)}, bf16[64,69]{1,0:T(8,128)(2,1)S(1)}, u32[]{:S(2)}, u32[]{:S(2)}) collective-permute-start(bf16[64,69]{1,0:T(8,128)(2,1)S(1)} %pad_maximum_fusion.38), channel_id=1, source_target_pairs={{0,1},{1,0},{2,3},{3,2},{4,5},{5,4},{6,7},{7,6},{8,9},{9,8},{10,11... | collective-permute-start | bytes 26504 | tf_op jit(solution)/shard_map/ppermute | solution.py:486
  19.3 114.4 %collective-permute-start.14 = (bf16[64,1280]{1,0:T(8,128)(2,1)S(1)}, bf16[64,1280]{1,0:T(8,128)(2,1)}, u32[]{:S(2)}, u32[]{:S(2)}) collective-permute-start(bf16[64,1280]{1,0:T(8,128)(2,1)S(1)} %get-tuple-element.199), channel_id=1, source_target_pairs={{0,8},{8,0},{16,24},{24,16},{1,9},{9,1},{17,25},{25,17},{2,10},{10... | collective-permute-start | bytes 491528 | tf_op jit(solution)/shard_map/ppermute | solution.py:875
  23.1 111.6 %collective-permute-start.15 = (bf16[64,1280]{1,0:T(8,128)(2,1)S(1)}, bf16[64,1280]{1,0:T(8,128)(2,1)}, u32[]{:S(2)}, u32[]{:S(2)}) collective-permute-start(bf16[64,1280]{1,0:T(8,128)(2,1)S(1)} %get-tuple-element.198), channel_id=1, source_target_pairs={{0,16},{8,24},{16,0},{24,8},{1,17},{9,25},{17,1},{25,9},{2,18},{10... | collective-permute-start | bytes 491528 | tf_op jit(solution)/shard_map/ppermute | solution.py:875
  26.3 109.3 %collective-permute-start.16 = (bf16[64,1280]{1,0:T(8,128)(2,1)S(1)}, bf16[64,1280]{1,0:T(8,128)(2,1)}, u32[]{:S(2)}, u32[]{:S(2)}) collective-permute-start(bf16[64,1280]{1,0:T(8,128)(2,1)S(1)} %get-tuple-element.197), channel_id=1, source_target_pairs={{0,24},{8,16},{16,8},{24,0},{1,25},{9,17},{17,9},{25,1},{2,26},{10... | collective-permute-start | bytes 491528 | tf_op jit(solution)/shard_map/ppermute | solution.py:875
  77.8 384.9 %all-gather.13.cloned.1.call-start = ((), (), s32[]{:S(2)}) async-start(), calls=%async_computation.11 | async-start | bytes 2621440 | tf_op jit(solution)/shard_map/all_gather | solution.py:1143
  120.4 403.7 %all-gather.7.cloned.1.call-start = ((), (), s32[]{:S(2)}) async-start(), calls=%async_computation.4 | async-start | bytes 3276800 | tf_op jit(solution)/shard_map/all_gather | solution.py:1143
  131.4 60.1 %collective-permute-start.6 = (bf16[512,1536]{1,0:T(8,128)(2,1)}, bf16[512,1536]{1,0:T(8,128)(2,1)}, u32[]{:S(2)}, u32[]{:S(2)}) collective-permute-start(bf16[512,1536]{1,0:T(8,128)(2,1)} %get-tuple-element.158), channel_id=1, source_target_pairs={{0,8},{8,0},{16,24},{24,16},{1,9},{9,1},{17,25},{25,17},{2,10},{10... | collective-permute-start | bytes 4718600 | tf_op jit(solution)/shard_map/ppermute | solution.py:875
  132.8 61.4 %collective-permute-start.7 = (bf16[512,1536]{1,0:T(8,128)(2,1)}, bf16[512,1536]{1,0:T(8,128)(2,1)}, u32[]{:S(2)}, u32[]{:S(2)}) collective-permute-start(bf16[512,1536]{1,0:T(8,128)(2,1)} %get-tuple-element.157), channel_id=1, source_target_pairs={{0,16},{8,24},{16,0},{24,8},{1,17},{9,25},{17,1},{25,9},{2,18},{10... | collective-permute-start | bytes 4718600 | tf_op jit(solution)/shard_map/ppermute | solution.py:875
  137.5 684.0 %all-gather.9.cloned.1.call-start = ((), (), s32[]{:S(2)}) async-start(), calls=%async_computation.5 | async-start | bytes 8912896 | tf_op jit(solution)/shard_map/all_gather | solution.py:503
  140.8 75.4 %collective-permute-start.4 = (bf16[1024,1280]{1,0:T(8,128)(2,1)}, bf16[1024,1280]{1,0:T(8,128)(2,1)}, u32[]{:S(2)}, u32[]{:S(2)}) collective-permute-start(bf16[1024,1280]{1,0:T(8,128)(2,1)} %bitcast.22), channel_id=1, source_target_pairs={{0,1},{1,0},{2,3},{3,2},{4,5},{5,4},{6,7},{7,6},{8,9},{9,8},{10,11... | collective-permute-start | bytes 7864328 | tf_op jit(solution)/shard_map/ppermute | solution.py:486
  185.3 29.6 %collective-permute-start.8 = (bf16[512,1536]{1,0:T(8,128)(2,1)}, bf16[512,1536]{1,0:T(8,128)(2,1)S(1)}, u32[]{:S(2)}, u32[]{:S(2)}) collective-permute-start(bf16[512,1536]{1,0:T(8,128)(2,1)} %get-tuple-element.156), channel_id=1, source_target_pairs={{0,24},{8,16},{16,8},{24,0},{1,25},{9,17},{17,9},{25,1},{2,26},{10... | collective-permute-start | bytes 4718600 | tf_op jit(solution)/shard_map/ppermute | solution.py:875
  191.5 1486.8 %reduce-scatter.7.cloned.1.call-start = ((), (), s32[]{:S(2)}) async-start(), calls=%async_computation.7 | async-start | bytes 3276800 | tf_op jit(solution)/shard_map/reduce_scatter | solution.py:1325
  216.1 335.6 %collective-permute-start.12 = (bf16[2048,1536]{1,0:T(8,128)(2,1)}, bf16[2048,1536]{1,0:T(8,128)(2,1)}, u32[]{:S(2)}, u32[]{:S(2)}) collective-permute-start(bf16[2048,1536]{1,0:T(8,128)(2,1)} %bitcast.585), channel_id=1, source_target_pairs={{0,1},{1,0},{2,3},{3,2},{4,5},{5,4},{6,7},{7,6},{8,9},{9,8},{10,11... | collective-permute-start | bytes 18874376 | tf_op jit(solution)/shard_map/ppermute | solution.py:486
  410.8 33.7 %collective-permute-start.9 = (bf16[768,512]{1,0:T(8,128)(2,1)}, bf16[768,512]{1,0:T(8,128)(2,1)}, u32[]{:S(2)}, u32[]{:S(2)}) collective-permute-start(bf16[768,512]{1,0:T(8,128)(2,1)} %get-tuple-element.170), channel_id=1, source_target_pairs={{0,8},{8,0},{16,24},{24,16},{1,9},{9,1},{17,25},{25,17},{2,10},{10... | collective-permute-start | bytes 2359304 | tf_op jit(solution)/shard_map/ppermute | solution.py:875
  411.8 34.3 %collective-permute-start.10 = (bf16[768,512]{1,0:T(8,128)(2,1)}, bf16[768,512]{1,0:T(8,128)(2,1)}, u32[]{:S(2)}, u32[]{:S(2)}) collective-permute-start(bf16[768,512]{1,0:T(8,128)(2,1)} %get-tuple-element.169), channel_id=1, source_target_pairs={{0,16},{8,24},{16,0},{24,8},{1,17},{9,25},{17,1},{25,9},{2,18},{10... | collective-permute-start | bytes 2359304 | tf_op jit(solution)/shard_map/ppermute | solution.py:875
  421.9 25.7 %collective-permute-start.22 = (bf16[768,512]{1,0:T(8,128)(2,1)}, bf16[768,512]{1,0:T(8,128)(2,1)}, u32[]{:S(2)}, u32[]{:S(2)}) collective-permute-start(bf16[768,512]{1,0:T(8,128)(2,1)} %get-tuple-element.173), channel_id=1, source_target_pairs={{0,8},{8,0},{16,24},{24,16},{1,9},{9,1},{17,25},{25,17},{2,10},{10... | collective-permute-start | bytes 2359304 | tf_op jit(solution)/shard_map/ppermute | solution.py:875
  423.1 34.5 %collective-permute-start.23 = (bf16[768,512]{1,0:T(8,128)(2,1)}, bf16[768,512]{1,0:T(8,128)(2,1)}, u32[]{:S(2)}, u32[]{:S(2)}) collective-permute-start(bf16[768,512]{1,0:T(8,128)(2,1)} %get-tuple-element.172), channel_id=1, source_target_pairs={{0,16},{8,24},{16,0},{24,8},{1,17},{9,25},{17,1},{25,9},{2,18},{10... | collective-permute-start | bytes 2359304 | tf_op jit(solution)/shard_map/ppermute | solution.py:875
  446.1 76.8 %collective-permute-start.19 = (bf16[512,1536]{1,0:T(8,128)(2,1)}, bf16[512,1536]{1,0:T(8,128)(2,1)S(1)}, u32[]{:S(2)}, u32[]{:S(2)}) collective-permute-start(bf16[512,1536]{1,0:T(8,128)(2,1)} %get-tuple-element.148), channel_id=1, source_target_pairs={{0,8},{8,0},{16,24},{24,16},{1,9},{9,1},{17,25},{25,17},{2,10},{10... | collective-permute-start | bytes 4718600 | tf_op jit(solution)/shard_map/ppermute | solution.py:875
  447.6 65.2 %collective-permute-start.24 = (bf16[768,512]{1,0:T(8,128)(2,1)}, bf16[768,512]{1,0:T(8,128)(2,1)}, u32[]{:S(2)}, u32[]{:S(2)}) collective-permute-start(bf16[768,512]{1,0:T(8,128)(2,1)} %get-tuple-element.171), channel_id=1, source_target_pairs={{0,24},{8,16},{16,8},{24,0},{1,25},{9,17},{17,9},{25,1},{2,26},{10... | collective-permute-start | bytes 2359304 | tf_op jit(solution)/shard_map/ppermute | solution.py:875
  457.6 88.4 %collective-permute-start.20 = (bf16[512,1536]{1,0:T(8,128)(2,1)}, bf16[512,1536]{1,0:T(8,128)(2,1)}, u32[]{:S(2)}, u32[]{:S(2)}) collective-permute-start(bf16[512,1536]{1,0:T(8,128)(2,1)} %get-tuple-element.147), channel_id=1, source_target_pairs={{0,16},{8,24},{16,0},{24,8},{1,17},{9,25},{17,1},{25,9},{2,18},{10... | collective-permute-start | bytes 4718600 | tf_op jit(solution)/shard_map/ppermute | solution.py:875
  466.1 219.2 %collective-permute-start.18 = (bf16[512,2048]{1,0:T(8,128)(2,1)}, bf16[512,2048]{1,0:T(8,128)(2,1)}, u32[]{:S(2)}, u32[]{:S(2)}) collective-permute-start(bf16[512,2048]{1,0:T(8,128)(2,1)} %bitcast.729), channel_id=1, source_target_pairs={{0,1},{1,0},{2,3},{3,2},{4,5},{5,4},{6,7},{7,6},{8,9},{9,8},{10,11... | collective-permute-start | bytes 6291464 | tf_op jit(solution)/shard_map/ppermute | solution.py:486
  512.9 35.7 %collective-permute-start.21 = (bf16[512,1536]{1,0:T(8,128)(2,1)}, bf16[512,1536]{1,0:T(8,128)(2,1)}, u32[]{:S(2)}, u32[]{:S(2)}) collective-permute-start(bf16[512,1536]{1,0:T(8,128)(2,1)} %get-tuple-element.146), channel_id=1, source_target_pairs={{0,24},{8,16},{16,8},{24,0},{1,25},{9,17},{17,9},{25,1},{2,26},{10... | collective-permute-start | bytes 4718600 | tf_op jit(solution)/shard_map/ppermute | solution.py:875
  522.8 38.2 %collective-permute-start.13 = (bf16[768,2048]{1,0:T(8,128)(2,1)}, bf16[768,2048]{1,0:T(8,128)(2,1)}, u32[]{:S(2)}, u32[]{:S(2)}) collective-permute-start(bf16[768,2048]{1,0:T(8,128)(2,1)} %constant_dynamic-update-slice_fusion.3), channel_id=1, source_target_pairs={{0,1},{1,0},{2,3},{3,2},{4,5},{5,4},{6,7},{7,6},{8,9},{9,8},{10,11... | collective-permute-start | bytes 9437192 | tf_op jit(solution)/shard_map/ppermute | solution.py:486
  545.9 115.5 %collective-permute-start.17 = (bf16[1024,1280]{1,0:T(8,128)(2,1)}, bf16[1024,1280]{1,0:T(8,128)(2,1)}, u32[]{:S(2)}, u32[]{:S(2)}) collective-permute-start(bf16[1024,1280]{1,0:T(8,128)(2,1)} %all-gather.7.cloned.1.call-done), channel_id=1, source_target_pairs={{0,1},{1,0},{2,3},{3,2},{4,5},{5,4},{6,7},{7,6},{8,9},{9,8},{10,11... | collective-permute-start | bytes 7864328 | tf_op jit(solution)/shard_map/ppermute | solution.py:486
  548.6 293.7 %collective-permute-start.26 = (bf16[768,2048]{1,0:T(8,128)(2,1)}, bf16[768,2048]{1,0:T(8,128)(2,1)}, u32[]{:S(2)}, u32[]{:S(2)}) collective-permute-start(bf16[768,2048]{1,0:T(8,128)(2,1)} %constant_dynamic-update-slice_fusion), channel_id=1, source_target_pairs={{0,1},{1,0},{2,3},{3,2},{4,5},{5,4},{6,7},{7,6},{8,9},{9,8},{10,11... | collective-permute-start | bytes 9437192 | tf_op jit(solution)/shard_map/ppermute | solution.py:486
  551.7 260.3 %collective-permute-start.25 = (bf16[2048,1536]{1,0:T(8,128)(2,1)}, bf16[2048,1536]{1,0:T(8,128)(2,1)}, u32[]{:S(2)}, u32[]{:S(2)}) collective-permute-start(bf16[2048,1536]{1,0:T(8,128)(2,1)} %bitcast.115), channel_id=1, source_target_pairs={{0,1},{1,0},{2,3},{3,2},{4,5},{5,4},{6,7},{7,6},{8,9},{9,8},{10,11... | collective-permute-start | bytes 18874376 | tf_op jit(solution)/shard_map/ppermute | solution.py:486
  930.3 140.3 %collective-permute-start.27 = (bf16[2048,1536]{1,0:T(8,128)(2,1)}, bf16[2048,1536]{1,0:T(8,128)(2,1)}, u32[]{:S(2)}, u32[]{:S(2)}) collective-permute-start(bf16[2048,1536]{1,0:T(8,128)(2,1)} %convolution_convert_fusion.6), channel_id=1, source_target_pairs={{0,1},{1,0},{2,3},{3,2},{4,5},{5,4},{6,7},{7,6},{8,9},{9,8},{10,11... | collective-permute-start | bytes 18874376 | tf_op jit(solution)/shard_map/ppermute | solution.py:486
  930.3 95.1 %collective-permute-start.28 = (bf16[768,2048]{1,0:T(8,128)(2,1)}, bf16[768,2048]{1,0:T(8,128)(2,1)}, u32[]{:S(2)}, u32[]{:S(2)}) collective-permute-start(bf16[768,2048]{1,0:T(8,128)(2,1)} %convolution_convert_fusion.14), channel_id=1, source_target_pairs={{0,1},{1,0},{2,3},{3,2},{4,5},{5,4},{6,7},{7,6},{8,9},{9,8},{10,11... | collective-permute-start | bytes 9437192 | tf_op jit(solution)/shard_map/ppermute | solution.py:486
  1030.8 33.4 %collective-permute-start.33 = (bf16[768,512]{1,0:T(8,128)(2,1)S(1)}, bf16[768,512]{1,0:T(8,128)(2,1)S(1)}, u32[]{:S(2)}, u32[]{:S(2)}) collective-permute-start(bf16[768,512]{1,0:T(8,128)(2,1)S(1)} %get-tuple-element.166), channel_id=1, source_target_pairs={{0,16},{8,24},{16,0},{24,8},{1,17},{9,25},{17,1},{25,9},{2,18},{10... | collective-permute-start | bytes 2359304 | tf_op jit(solution)/shard_map/ppermute | solution.py:875
  1032.5 33.5 %collective-permute-start.34 = (bf16[768,512]{1,0:T(8,128)(2,1)S(1)}, bf16[768,512]{1,0:T(8,128)(2,1)S(1)}, u32[]{:S(2)}, u32[]{:S(2)}) collective-permute-start(bf16[768,512]{1,0:T(8,128)(2,1)S(1)} %get-tuple-element.165), channel_id=1, source_target_pairs={{0,24},{8,16},{16,8},{24,0},{1,25},{9,17},{17,9},{25,1},{2,26},{10... | collective-permute-start | bytes 2359304 | tf_op jit(solution)/shard_map/ppermute | solution.py:875
  1115.4 105.9 %collective-permute-start.29 = (bf16[512,1536]{1,0:T(8,128)(2,1)}, bf16[512,1536]{1,0:T(8,128)(2,1)}, u32[]{:S(2)}, u32[]{:S(2)}) collective-permute-start(bf16[512,1536]{1,0:T(8,128)(2,1)} %get-tuple-element.145), channel_id=1, source_target_pairs={{0,8},{8,0},{16,24},{24,16},{1,9},{9,1},{17,25},{25,17},{2,10},{10... | collective-permute-start | bytes 4718600 | tf_op jit(solution)/shard_map/ppermute | solution.py:875
  1115.8 107.9 %collective-permute-start.30 = (bf16[512,1536]{1,0:T(8,128)(2,1)}, bf16[512,1536]{1,0:T(8,128)(2,1)}, u32[]{:S(2)}, u32[]{:S(2)}) collective-permute-start(bf16[512,1536]{1,0:T(8,128)(2,1)} %get-tuple-element.144), channel_id=1, source_target_pairs={{0,16},{8,24},{16,0},{24,8},{1,17},{9,25},{17,1},{25,9},{2,18},{10... | collective-permute-start | bytes 4718600 | tf_op jit(solution)/shard_map/ppermute | solution.py:875
  1117.5 108.8 %collective-permute-start.31 = (bf16[512,1536]{1,0:T(8,128)(2,1)}, bf16[512,1536]{1,0:T(8,128)(2,1)}, u32[]{:S(2)}, u32[]{:S(2)}) collective-permute-start(bf16[512,1536]{1,0:T(8,128)(2,1)} %get-tuple-element.143), channel_id=1, source_target_pairs={{0,24},{8,16},{16,8},{24,0},{1,25},{9,17},{17,9},{25,1},{2,26},{10... | collective-permute-start | bytes 4718600 | tf_op jit(solution)/shard_map/ppermute | solution.py:875
  1206.3 144.2 %collective-permute-start.42 = (bf16[1024,1280]{1,0:T(8,128)(2,1)}, bf16[1024,1280]{1,0:T(8,128)(2,1)}, u32[]{:S(2)}, u32[]{:S(2)}) collective-permute-start(bf16[1024,1280]{1,0:T(8,128)(2,1)} %constant_dynamic-slice_fusion.5), channel_id=1, source_target_pairs={{0,1},{1,0},{2,3},{3,2},{4,5},{5,4},{6,7},{7,6},{8,9},{9,8},{10,11... | collective-permute-start | bytes 7864328 | tf_op jit(solution)/shard_map/ppermute | solution.py:486
  1212.2 280.7 %collective-permute-start.47 = (bf16[512,2048]{1,0:T(8,128)(2,1)}, bf16[512,2048]{1,0:T(8,128)(2,1)}, u32[]{:S(2)}, u32[]{:S(2)}) collective-permute-start(bf16[512,2048]{1,0:T(8,128)(2,1)} %constant_dynamic-slice_fusion.3), channel_id=1, source_target_pairs={{0,1},{1,0},{2,3},{3,2},{4,5},{5,4},{6,7},{7,6},{8,9},{9,8},{10,11... | collective-permute-start | bytes 6291464 | tf_op jit(solution)/shard_map/ppermute | solution.py:486
  1328.7 210.4 %collective-permute-start.35 = (bf16[2048,1536]{1,0:T(8,128)(2,1)}, bf16[2048,1536]{1,0:T(8,128)(2,1)}, u32[]{:S(2)}, u32[]{:S(2)}) collective-permute-start(bf16[2048,1536]{1,0:T(8,128)(2,1)} %convolution_convert_fusion.4), channel_id=1, source_target_pairs={{0,1},{1,0},{2,3},{3,2},{4,5},{5,4},{6,7},{7,6},{8,9},{9,8},{10,11... | collective-permute-start | bytes 18874376 | tf_op jit(solution)/shard_map/ppermute | solution.py:486
  1328.7 152.4 %collective-permute-start.36 = (bf16[768,2048]{1,0:T(8,128)(2,1)}, bf16[768,2048]{1,0:T(8,128)(2,1)}, u32[]{:S(2)}, u32[]{:S(2)}) collective-permute-start(bf16[768,2048]{1,0:T(8,128)(2,1)} %convolution_convert_fusion.10), channel_id=1, source_target_pairs={{0,1},{1,0},{2,3},{3,2},{4,5},{5,4},{6,7},{7,6},{8,9},{9,8},{10,11... | collective-permute-start | bytes 9437192 | tf_op jit(solution)/shard_map/ppermute | solution.py:486
  1354.5 432.0 %reduce-scatter.11.cloned.1.call-start = ((), (), s32[]{:S(2)}) async-start(), calls=%async_computation.9 | async-start | bytes 2621440 | tf_op jit(solution)/shard_map/reduce_scatter | solution.py:1325
  1491.1 35.5 %collective-permute-start.52 = (bf16[768,512]{1,0:T(8,128)(2,1)}, bf16[768,512]{1,0:T(8,128)(2,1)}, u32[]{:S(2)}, u32[]{:S(2)}) collective-permute-start(bf16[768,512]{1,0:T(8,128)(2,1)} %get-tuple-element.161), channel_id=1, source_target_pairs={{0,16},{8,24},{16,0},{24,8},{1,17},{9,25},{17,1},{25,9},{2,18},{10... | collective-permute-start | bytes 2359304 | tf_op jit(solution)/shard_map/ppermute | solution.py:875
  1492.6 36.1 %collective-permute-start.53 = (bf16[768,512]{1,0:T(8,128)(2,1)}, bf16[768,512]{1,0:T(8,128)(2,1)S(1)}, u32[]{:S(2)}, u32[]{:S(2)}) collective-permute-start(bf16[768,512]{1,0:T(8,128)(2,1)} %get-tuple-element.160), channel_id=1, source_target_pairs={{0,24},{8,16},{16,8},{24,0},{1,25},{9,17},{17,9},{25,1},{2,26},{10... | collective-permute-start | bytes 2359304 | tf_op jit(solution)/shard_map/ppermute | solution.py:875
  1496.6 289.9 %reduce-scatter.9.cloned.1.call-start = ((), (), s32[]{:S(2)}) async-start(), calls=%async_computation.8 | async-start | bytes 2621440 | tf_op jit(solution)/shard_map/reduce_scatter | solution.py:1325
  1588.4 23.7 %collective-permute-start.46 = (bf16[512,2048]{1,0:T(8,128)(2,1)}, bf16[512,2048]{1,0:T(8,128)(2,1)}, u32[]{:S(2)}, u32[]{:S(2)}) collective-permute-start(bf16[512,2048]{1,0:T(8,128)(2,1)} %constant_dynamic-slice_fusion.4), channel_id=1, source_target_pairs={{0,1},{1,0},{2,3},{3,2},{4,5},{5,4},{6,7},{7,6},{8,9},{9,8},{10,11... | collective-permute-start | bytes 6291464 | tf_op jit(solution)/shard_map/ppermute | solution.py:486
  1616.0 173.2 %reduce-scatter.5.cloned.1.call-start = ((), (), s32[]{:S(2)}) async-start(), calls=%async_computation.6 | async-start | bytes 3276800 | tf_op jit(solution)/shard_map/reduce_scatter | solution.py:1325
  1623.6 63.0 %collective-permute-start.38 = (bf16[1024,1280]{1,0:T(8,128)(2,1)}, bf16[1024,1280]{1,0:T(8,128)(2,1)}, u32[]{:S(2)}, u32[]{:S(2)}) collective-permute-start(bf16[1024,1280]{1,0:T(8,128)(2,1)} %constant_dynamic-slice_fusion.6), channel_id=1, source_target_pairs={{0,1},{1,0},{2,3},{3,2},{4,5},{5,4},{6,7},{7,6},{8,9},{9,8},{10,11... | collective-permute-start | bytes 7864328 | tf_op jit(solution)/shard_map/ppermute | solution.py:486
  1698.1 38.0 %collective-permute-start.48 = (bf16[512,1536]{1,0:T(8,128)(2,1)}, bf16[512,1536]{1,0:T(8,128)(2,1)}, u32[]{:S(2)}, u32[]{:S(2)}) collective-permute-start(bf16[512,1536]{1,0:T(8,128)(2,1)} %get-tuple-element.140), channel_id=1, source_target_pairs={{0,8},{8,0},{16,24},{24,16},{1,9},{9,1},{17,25},{25,17},{2,10},{10... | collective-permute-start | bytes 4718600 | tf_op jit(solution)/shard_map/ppermute | solution.py:875
  1698.6 71.2 %collective-permute-start.49 = (bf16[512,1536]{1,0:T(8,128)(2,1)}, bf16[512,1536]{1,0:T(8,128)(2,1)}, u32[]{:S(2)}, u32[]{:S(2)}) collective-permute-start(bf16[512,1536]{1,0:T(8,128)(2,1)} %get-tuple-element.139), channel_id=1, source_target_pairs={{0,16},{8,24},{16,0},{24,8},{1,17},{9,25},{17,1},{25,9},{2,18},{10... | collective-permute-start | bytes 4718600 | tf_op jit(solution)/shard_map/ppermute | solution.py:875
  1702.5 70.0 %collective-permute-start.50 = (bf16[512,1536]{1,0:T(8,128)(2,1)S(1)}, bf16[512,1536]{1,0:T(8,128)(2,1)S(1)}, u32[]{:S(2)}, u32[]{:S(2)}) collective-permute-start(bf16[512,1536]{1,0:T(8,128)(2,1)S(1)} %copy-done.99), channel_id=1, source_target_pairs={{0,24},{8,16},{16,8},{24,0},{1,25},{9,17},{17,9},{25,1},{2,26},{10... | collective-permute-start | bytes 4718600 | tf_op jit(solution)/shard_map/ppermute | solution.py:875
  (250 other events, 6755.6 us)
Sparse Core Ops, SparseCore 0:
  77.9 48.5 all-gather.10
  128.6 45.7 all-gather.12
  176.0 53.5 all-gather.6
  232.3 160.7 all-gather.8
  1354.6 84.0 reduce-scatter.6
  1496.8 44.5 reduce-scatter.10
  1616.1 43.3 reduce-scatter.8
  1690.7 50.8 reduce-scatter.4

commit v3 on v2

--- a/solution.py
+++ b/solution.py
@@ -860,6 +860,331 @@
     )(operand.reshape(chips, rows, columns))
 
 
+def expert_work(x_ref, first, second, produced, out_ref, between):
+    blocks, cap, tokens = first[0].shape
+    ff = first[3].shape[0]
+    group = PAIR
+    count = group * cap
+
+    @pl.loop(0, blocks // group)
+    def _(g):
+        at = pl.ds(pl.multiple_of(g * count, 16), count)
+        for k, refs in enumerate((first, second)):
+            pick_ref, gate_ref, up_gate_ref, down_ref, rows_ref, pre_ref, hidden_ref = refs
+
+            for i in range(group):
+                rows_ref[pl.ds(pl.multiple_of(g * count + i * cap, 16), cap)] = jnp.dot(
+                    pick_ref[g * group + i],
+                    x_ref[g * group + i],
+                    preferred_element_type=jnp.float32,
+                ).astype(jnp.bfloat16)
+            pre = jnp.dot(rows_ref[at], up_gate_ref[...], preferred_element_type=jnp.float32)
+            pre_ref[at] = pre.astype(pre_ref.dtype)
+            gate_pre, up_pre = pre[:, :ff], pre[:, ff:]
+            hidden = (gate_pre * (1.0 / (1.0 + jnp.exp(-gate_pre))) * up_pre).astype(jnp.bfloat16)
+            hidden_ref[at] = hidden
+            made = jnp.dot(hidden, down_ref[...], preferred_element_type=jnp.float32)
+            produced[k] = (made * gate_ref[at]).astype(jnp.bfloat16)
+        for i in range(group):
+            total = None
+            for k, refs in enumerate((first, second)):
+                part = lax.dot_general(
+                    refs[0][g * group + i],
+                    produced[k, pl.ds(i * cap, cap)],
+                    (((0,), (0,)), ((), ())),
+                    preferred_element_type=jnp.float32,
+                )
+                total = part if total is None else total + part
+            out_ref[g * group + i] = total.astype(jnp.bfloat16)
+        for number, action in between:
+            pl.when(g == number)(action)
+
+
+def weights_kernel(layer, depth, working, *refs):
+    refs = list(refs)
+
+    def take(count):
+        taken = refs[:count]
+        del refs[:count]
+        return taken
+
+    w_gate, w_up, w_down, qkv_ref, w_out_ref = take(5)
+    inputs = take(9) if working else []
+    up_gate_refs = take(2)
+    down_refs = take(2)
+    dense_refs = take(2)
+    outputs = take(7) if working else []
+    own_sems, send_sems, recv_sems, side_send, side_recv, line_send, line_recv = take(7)
+    here = Place(ALL_CHIPS, depth)
+    share = w_gate.shape[2]
+    ff = w_gate.shape[3]
+    sibling = (here.pair, here.line, 1 - here.core)
+    dense_sources = (qkv_ref, w_out_ref.at[layer])
+
+    def device(bits):
+        return (here.pairs[bits], here.line, here.core)
+
+    def remote(source, target, send, recv, to):
+        return pltpu.make_async_remote_copy(
+            src_ref=source,
+            dst_ref=target,
+            send_sem=send,
+            recv_sem=recv,
+            device_id=to,
+            device_id_type=pl.DeviceIdType.MESH,
+        )
+
+    barrier = pltpu.get_barrier_semaphore()
+    greeted = [device(1), device(2), device(3), sibling]
+    for to in greeted:
+        pl.semaphore_signal(barrier, inc=1, device_id=to, device_id_type=pl.DeviceIdType.MESH)
+    for neighbour in (ABOVE, BELOW):
+
+        def greet(neighbour=neighbour):
+            pl.semaphore_signal(
+                barrier,
+                inc=1,
+                device_id=here.device(neighbour),
+                device_id_type=pl.DeviceIdType.MESH,
+            )
+
+        when(here.holds(0, neighbour), greet)
+    ends = (here.line == 0).astype(jnp.int32) + (here.line == depth - 1).astype(jnp.int32)
+    pl.semaphore_wait(barrier, len(greeted) + 2 - ends)
+
+    def shard(k, expert):
+        return (w_gate, w_up, w_down)[k].at[layer, expert]
+
+    def spot(which, k, origin):
+        start = pl.ds(pl.multiple_of(origin * share, share), share)
+        if k == 2:
+            return down_refs[which].at[:, start]
+        return up_gate_refs[which].at[start, pl.ds(k * ff, ff)]
+
+    def across(bits, k):
+        return remote(
+            shard(k, here.pairs[bits]),
+            spot(0, k, here.pair),
+            send_sems.at[bits - 1, k],
+            recv_sems.at[bits - 1, k],
+            device(bits),
+        )
+
+    def beside(bits, k):
+        source = shard(k, here.pair) if bits == 0 else spot(0, k, here.pairs[bits])
+        return remote(
+            source,
+            spot(1, k, here.pairs[bits]),
+            side_send.at[bits, k],
+            side_recv.at[bits, k],
+            sibling,
+        )
+
+    offsets = [0] + [s * k for k in range(1, depth) for s in (-1, 1)]
+
+    def slab(k, offset):
+        return dense_refs[k].at[here.core, here.line + offset]
+
+    def along(k, offset, neighbour):
+        number = offsets.index(offset)
+        there = offset - 1 if neighbour == ABOVE else offset + 1
+        return remote(
+            dense_sources[k] if offset == 0 else slab(k, offset),
+            slab(k, offset),
+            line_send.at[k, number if offset else (0 if neighbour == ABOVE else len(offsets))],
+            line_recv.at[k, offsets.index(there)],
+            here.device(neighbour),
+        )
+
+    def dense_beside(k, offset):
+        number = PAIR + offsets.index(offset)
+        return remote(
+            dense_sources[k] if offset == 0 else slab(k, offset),
+            slab(k, offset),
+            side_send.at[number, k],
+            side_recv.at[number, k],
+            sibling,
+        )
+
+    def dense_beside_landed(k, offset):
+        number = PAIR + offsets.index(offset)
+        target = dense_refs[k].at[1 - here.core, here.line + offset]
+        return remote(target, target, side_send.at[number, k], side_recv.at[number, k], sibling)
+
+    def onward(offset):
+        neighbour = ABOVE if offset < 0 else BELOW
+        return neighbour if abs(offset) + 1 < depth else None
+
+    kept = [
+        pltpu.make_async_copy(shard(k, here.pair), spot(0, k, here.pair), own_sems.at[k])
+        for k in range(3)
+    ] + [
+        pltpu.make_async_copy(dense_sources[k], slab(k, 0), own_sems.at[3 + k]) for k in range(2)
+    ]
+    for k in range(2):
+        for neighbour in (ABOVE, BELOW):
+            when(here.holds(0, neighbour), lambda k=k, n=neighbour: along(k, 0, n).start())
+    for k in range(3):
+        for bits in (3, 1, 2):
+            across(bits, k).start()
+    for copy in kept:
+        copy.start()
+    for k in range(3):
+        beside(0, k).start()
+    for k in range(2):
+        dense_beside(k, 0).start()
+    def arrived(offset):
+        for k in range(2):
+            remote(
+                slab(k, offset),
+                slab(k, offset),
+                line_send.at[k, 0],
+                line_recv.at[k, offsets.index(offset)],
+                sibling,
+            ).wait_recv()
+            neighbour = onward(offset)
+            if neighbour is not None:
+                when(
+                    here.holds(0, neighbour),
+                    lambda k=k, n=neighbour: along(k, offset, n).start(),
+                )
+            dense_beside(k, offset).start()
+
+    def line_step(distance):
+        for offset in offsets:
+            if abs(offset) == distance:
+                when(here.holds(offset), lambda offset=offset: arrived(offset))
+
+    def crossed(k):
+        for bits in (1, 2, 3):
+            remote(
+                spot(0, k, here.pairs[bits]),
+                spot(0, k, here.pairs[bits]),
+                send_sems.at[bits - 1, k],
+                recv_sems.at[bits - 1, k],
+                sibling,
+            ).wait_recv()
+            beside(bits, k).start()
+
+    steps = [lambda distance=distance: line_step(distance) for distance in range(1, depth)]
+    if working:
+        x_ref, picks, gates, ups, downs = (
+            inputs[0],
+            inputs[1:3],
+            inputs[3:5],
+            inputs[5:7],
+            inputs[7:9],
+        )
+        experts = [
+            (picks[i], gates[i], ups[i], downs[i], outputs[i], outputs[2 + i], outputs[4 + i])
+            for i in range(2)
+        ]
+        turns = x_ref.shape[0] // PAIR
+        between = [(turns - len(steps) + i, step) for i, step in enumerate(steps)]
+        expert_work(x_ref, *experts, refs[0], outputs[6], between)
+    else:
+        for step in steps:
+            step()
+    for k in range(3):
+        crossed(k)
+    for bits in range(PAIR):
+        for k in range(3):
+            beside(bits, k).wait_recv()
+    for offset in offsets:
+
+        def landed(offset=offset):
+            for k in range(2):
+                dense_beside_landed(k, offset).wait_recv()
+
+        when(here.holds(offset), landed)
+    for bits in (1, 2, 3):
+        for k in range(3):
+            across(bits, k).wait_send()
+    for bits in range(PAIR):
+        for k in range(3):
+            beside(bits, k).wait_send()
+    for offset in offsets:
+
+        def left(offset=offset):
+            for k in range(2):
+                dense_beside(k, offset).wait_send()
+                neighbours = (ABOVE, BELOW) if offset == 0 else (onward(offset),)
+                for neighbour in neighbours:
+                    if neighbour is not None:
+                        when(
+                            here.holds(0, neighbour),
+                            lambda k=k, n=neighbour: along(k, offset, n).wait_send(),
+                        )
+
+        when(here.holds(offset), left)
+    for copy in kept:
+        copy.wait()
+
+
+def layer_weights(layer, w_gate, w_up, w_down, qkv_rows, w_out, collective_id, work=None):
+    depth = lax.axis_size(LINE)
+    share, ff = w_gate.shape[2:]
+    model = PAIR * share
+    low = jnp.bfloat16
+    shapes = [
+        jax.ShapeDtypeStruct((model, 2 * ff), low),
+        jax.ShapeDtypeStruct((model, 2 * ff), low),
+        jax.ShapeDtypeStruct((ff, model), low),
+        jax.ShapeDtypeStruct((ff, model), low),
+        jax.ShapeDtypeStruct((2, depth) + qkv_rows.shape, low),
+        jax.ShapeDtypeStruct((2, depth) + w_out.shape[1:], low),
+    ]
+    operands = [w_gate, w_up, w_down, qkv_rows, w_out]
+    in_specs = [pl.BlockSpec(memory_space=pl.ANY)] * len(operands)
+    out_specs = [pl.BlockSpec(memory_space=pl.ANY)] * len(shapes)
+    offsets = 2 * depth - 1
+    scratch = [
+        pltpu.SemaphoreType.DMA((5,)),
+        pltpu.SemaphoreType.DMA((3, 3)),
+        pltpu.SemaphoreType.DMA((3, 3)),
+        pltpu.SemaphoreType.DMA((PAIR + offsets, 3)),
+        pltpu.SemaphoreType.DMA((PAIR + offsets, 3)),
+        pltpu.SemaphoreType.DMA((2, offsets + 1)),
+        pltpu.SemaphoreType.DMA((2, offsets)),
+    ]
+    if work is not None:
+        gathered, picks, row_gates, weights = work
+        blocks, cap, rows = picks[0].shape
+        count = blocks * cap
+        operands += [
+            gathered.reshape(blocks, rows, model),
+            *picks,
+            *row_gates,
+            weights[0][0],
+            weights[1][0],
+            weights[0][1],
+            weights[1][1],
+        ]
+        in_specs += [pl.BlockSpec(memory_space=pltpu.VMEM)] * 9
+        shapes += (
+            [jax.ShapeDtypeStruct((count, model), low)] * 2
+            + [jax.ShapeDtypeStruct((count, 2 * ff), low)] * 2
+            + [jax.ShapeDtypeStruct((count, ff), low)] * 2
+            + [jax.ShapeDtypeStruct((blocks, rows, model), low)]
+        )
+        out_specs += [pl.BlockSpec(memory_space=pltpu.VMEM)] * 7
+        scratch.append(pltpu.VMEM((2, PAIR * cap, model), low))
+    made = pl.pallas_call(
+        partial(weights_kernel, layer, depth, work is not None),
+        out_shape=shapes,
+        in_specs=in_specs,
+        out_specs=out_specs,
+        scratch_shapes=scratch,
+        compiler_params=pltpu.CompilerParams(
+            collective_id=collective_id, has_side_effects=True, vmem_limit_bytes=58 * 2**20
+        ),
+        cost_estimate=pl.CostEstimate(flops=0, bytes_accessed=400 * 2**20, transcendentals=0),
+    )(*operands)
+    qkv = made[4].reshape(-1, qkv_rows.shape[1])
+    out = made[5].reshape(-1, w_out.shape[2])
+    return ((made[0], made[2]), (made[1], made[3])), qkv, out, made[6:]
+
+
 def after(operand, *others):
     there = None
     for other in others:
@@ -977,10 +1302,7 @@
     grad_wqkv = lax.dot_general(
         normed, grad_qkv, (((0,), (0,)), ((), ())), preferred_element_type=jnp.float32
     ).astype(jnp.bfloat16)
-    grad_normed = lax.dot_general(
-        grad_qkv, w_qkv, (((1,), (1,)), ((), ())), preferred_element_type=jnp.float32
-    ).astype(jnp.bfloat16)
-    return scatter_chips(grad_normed, 7, PLANE), grad_wqkv, grad_wout, grad_gq, grad_gk
+    return grad_qkv, grad_wqkv, grad_wout, grad_gq, grad_gk
 
 
 def send_back(picks, pieces):
@@ -1003,17 +1325,16 @@
     memo = []
     pieces = []
     for pick, row_gate, (w_up_gate, w_down) in zip(picks, row_gates, weights):
-        hidden_size = w_down.shape[0]
+        ff = w_down.shape[0]
         rows = jnp.einsum(PICK, pick, grouped, preferred_element_type=jnp.float32)
         rows = rows.astype(jnp.bfloat16).reshape(-1, width)
         pre = jnp.dot(rows, w_up_gate, preferred_element_type=jnp.float32)
-        gate_pre = pre[:, :hidden_size]
-        up_pre = pre[:, hidden_size:]
+        gate_pre, up_pre = pre[:, :ff], pre[:, ff:]
         hidden = (jax.nn.silu(gate_pre) * up_pre).astype(jnp.bfloat16)
         produced = jnp.dot(hidden, w_down, preferred_element_type=jnp.float32)
         produced = (produced * row_gate).astype(jnp.bfloat16)
         pieces.append(produced.reshape(blocks, -1, width))
-        memo.append((rows, gate_pre, up_pre, hidden))
+        memo.append((rows, pre, hidden))
     return send_back(picks, pieces), memo
 
 
@@ -1026,7 +1347,9 @@
     for pick, row_gate, (w_up_gate, w_down), kept, expert in zip(
         picks, row_gates, weights, memo, experts
     ):
-        rows, gate_pre, up_pre, hidden = kept
+        rows, pre, hidden = kept
+        ff = hidden.shape[1]
+        gate_pre, up_pre = pre[:, :ff].astype(jnp.float32), pre[:, ff:].astype(jnp.float32)
         grad_rows = jnp.einsum(PICK, pick, grouped, preferred_element_type=jnp.float32)
         grad_rows = grad_rows.astype(jnp.bfloat16).reshape(-1, width)
         through = lax.dot_general(
@@ -1042,30 +1365,31 @@
         )
         grad_hidden = through * row_gate
         sigmoid_gate = jax.nn.sigmoid(gate_pre)
-        grad_pre = jnp.concatenate(
-            [
-                (
-                    grad_hidden * up_pre * sigmoid_gate * (1.0 + gate_pre * (1.0 - sigmoid_gate))
-                ).astype(jnp.bfloat16),
-                (grad_hidden * gate_pre * sigmoid_gate).astype(jnp.bfloat16),
-            ],
-            axis=1,
-        )
+        grad_gate_pre = (
+            grad_hidden * up_pre * sigmoid_gate * (1.0 + gate_pre * (1.0 - sigmoid_gate))
+        ).astype(jnp.bfloat16)
+        grad_up_pre = (grad_hidden * gate_pre * sigmoid_gate).astype(jnp.bfloat16)
         grad_down = lax.dot_general(
             (hidden_f * row_gate).astype(jnp.bfloat16),
             grad_rows,
             (((0,), (0,)), ((), ())),
             preferred_element_type=jnp.float32,
         ).astype(jnp.bfloat16)
-        grad_up_gate = lax.dot_general(
-            rows, grad_pre, (((0,), (0,)), ((), ())), preferred_element_type=jnp.float32
-        ).astype(jnp.bfloat16)
+        grad_gate, grad_up = [
+            lax.dot_general(
+                rows, part, (((0,), (0,)), ((), ())), preferred_element_type=jnp.float32
+            ).astype(jnp.bfloat16)
+            for part in (grad_gate_pre, grad_up_pre)
+        ]
         grad_in = lax.dot_general(
-            grad_pre, w_up_gate, (((1,), (1,)), ((), ())), preferred_element_type=jnp.float32
+            jnp.concatenate([grad_gate_pre, grad_up_pre], axis=1),
+            w_up_gate,
+            (((1,), (1,)), ((), ())),
+            preferred_element_type=jnp.float32,
         ).astype(jnp.bfloat16)
         piece = jnp.concatenate([grad_in, gate_part], axis=1)
         pieces.append(piece.reshape(blocks, -1, width + GATE_COLUMNS))
-        grads.append((grad_up_gate, grad_down))
+        grads.append((grad_gate, grad_up, grad_down))
     return send_back(picks, pieces), grads
 
 
@@ -1131,29 +1455,16 @@
             axis=2,
         )
 
-    def rows_by_source(source):
-        whole = jnp.zeros((width, short, qkv_columns), jnp.bfloat16)
-        for origin, piece in swap_pieces(
-            lambda to: lax.dynamic_index_in_dim(source, to, 0, keepdims=False), place, width
-        ):
-            whole = lax.dynamic_update_index_in_dim(whole, piece, origin, 0)
-        return whole.reshape(width * short, qkv_columns)
-
-    def line_gather(operand):
-        return lax.all_gather(operand, LINE, axis=0, tiled=True)
-
-    def both_cores(operand):
-        return by_core(core, operand, swap(operand), 0)
-
-    first_rows = gather_chips(rows_by_source(columns_of(0)), 8, LINE_ONLY)
-    dense_qkv = [both_cores(first_rows)]
-    dense_out = [both_cores(line_gather(w_out[0]))]
-    for number in range(1, DECODER_LAYERS):
-        dense_qkv.append(
-            both_cores(line_gather(after(rows_by_source(columns_of(number)), first_rows)))
-        )
-        dense_out.append(both_cores(line_gather(after(w_out[number], first_rows))))
-    cotangent_all = offload_gather(after(cotangent, first_rows))
+    columns = jnp.stack([columns_of(number) for number in range(DECODER_LAYERS)], axis=1)
+    by_source = jnp.zeros_like(columns)
+    for origin, piece in swap_pieces(
+        lambda to: lax.dynamic_index_in_dim(columns, to, 0, keepdims=False), place, width
+    ):
+        by_source = lax.dynamic_update_index_in_dim(by_source, piece, origin, 0)
+
+    def rows_by_source(number):
+        return by_source[:, number].reshape(width * short, qkv_columns)
+
     routers = [
         small[:, number * EXPERTS : (number + 1) * EXPERTS] for number in range(DECODER_LAYERS)
     ]
@@ -1205,34 +1516,28 @@
     )
     g_attn, g_ffn, g_query, g_key = zip(*[split_gains(all_gains[i]) for i in range(DECODER_LAYERS)])
 
+    share = MODEL_WIDTH // width
+
+    def to_experts(part):
+        return lax.all_to_all(part, FSDP, split_axis=0, concat_axis=0, tiled=True)
+
+    def weights_of(number, work=None):
+        return layer_weights(
+            number, w_gate, w_up, w_down, rows_by_source(number), w_out, 10 + number, work
+        )
+
+    weights, qkv_whole, out_whole, unused_made = weights_of(0)
     state = tokens.astype(jnp.float32)
     kept = []
     for number in range(DECODER_LAYERS):
         normed = norm_rows(state, g_attn[number]).astype(jnp.bfloat16)
         normed = gather_chips(by_owner(normed, width), 6, PLANE)
-        dense = (dense_qkv[number], dense_out[number], normed, g_query[number], g_key[number])
-        ready = small if number == 0 else gathered
-        gate_up_source = after(
-            jnp.concatenate([w_gate[number], w_up[number]], axis=2).reshape(-1, 2 * ff), ready
-        ).reshape(width, -1, 2 * ff)
-        down_source = after(w_down[number].reshape(-1, w_down.shape[3]), ready).reshape(
-            width, ff, -1
-        )
-        up_gate = jnp.zeros((width, MODEL_WIDTH // width, 2 * ff), jnp.bfloat16)
-        for origin, piece in swap_pieces(
-            lambda to: lax.dynamic_index_in_dim(gate_up_source, to, 0, keepdims=False), place, width
-        ):
-            up_gate = lax.dynamic_update_index_in_dim(up_gate, piece, origin, 0)
-        up_gate = up_gate.reshape(MODEL_WIDTH, 2 * ff)
-        down = jnp.zeros((ff, MODEL_WIDTH), jnp.bfloat16)
-        for origin, piece in swap_pieces(
-            lambda to: lax.dynamic_index_in_dim(down_source, to, 0, keepdims=False), place, width
-        ):
-            down = lax.dynamic_update_slice_in_dim(down, piece, origin * piece.shape[1], 1)
-        weights = ((up_gate, down), (swap(up_gate), swap(down)))
+        dense = (qkv_whole, out_whole, normed, g_query[number], g_key[number])
         middle, memo = attention_forward(state, dense, angles)
         mixer_in = norm_rows(middle, g_ffn[number]).astype(jnp.bfloat16)
         gathered = gather_chips(mixer_in, 2)
+        if number == 0:
+            cotangent_all = offload_gather(after(cotangent, gathered))
         logits = jnp.dot(gathered, routers[number], preferred_element_type=jnp.float32)
         named = chosen[:, number].reshape(chips * rows, EXPERTS)
         gates = softmax_last(jnp.where(named, logits, -1e30))
@@ -1244,24 +1549,38 @@
                     pick.astype(jnp.float32) * gate.reshape(chips, 1, rows), axis=2
                 ).reshape(-1, 1)
             )
-        produced, expert_memo = expert_forward(gathered, picks[number], row_gates, weights)
+        layer_experts = weights
+        if number + 1 < DECODER_LAYERS:
+            weights, qkv_whole, out_whole, made = weights_of(
+                number + 1, (gathered, picks[number], row_gates, weights)
+            )
+            expert_memo = [(made[i], made[2 + i], made[4 + i]) for i in range(2)]
+            produced = made[6].reshape(gathered.shape)
+        else:
+            produced, expert_memo = expert_forward(gathered, picks[number], row_gates, weights)
         new_state = middle + scatter_chips(produced, 3).astype(jnp.float32)
         own_gates = lax.dynamic_slice_in_dim(gates, chip * rows, rows, 0)
         kept.append(
-            (state, middle, mixer_in, own_gates, row_gates, dense, weights, memo, expert_memo)
+            (state, middle, mixer_in, own_gates, row_gates, dense, layer_experts, memo, expert_memo)
         )
         state = new_state
     result = state.astype(jnp.bfloat16)
+
+    def half_sum(operand):
+        half = operand.shape[0] // 2
+        mine = lax.dynamic_slice_in_dim(operand, core * half, half, 0)
+        return mine, swap(lax.dynamic_slice_in_dim(operand, (1 - core) * half, half, 0))
+
+    def line_sum(mine, other):
+        return lax.psum_scatter(mine + other, LINE, scatter_dimension=0, tiled=True)
 
     grad_state = cotangent.astype(jnp.float32)
     grad_low = cotangent
     grad_gathered = cotangent_all
     small_grads = []
     d_out = []
-    d_qkv = []
-    share = MODEL_WIDTH // width
-    d_up_gate = jnp.zeros((DECODER_LAYERS, width, share, 2 * ff), jnp.bfloat16)
-    d_down = jnp.zeros((DECODER_LAYERS, width, ff, share), jnp.bfloat16)
+    back_qkv = []
+    d_experts = []
     for number in reversed(range(DECODER_LAYERS)):
         state, middle, mixer_in, own_gates, row_gates, dense, weights, memo, expert_memo = kept[
             number
@@ -1269,22 +1588,9 @@
         back, expert_grads = expert_backward(
             grad_gathered, picks[number], row_gates, weights, expert_memo, (first, second)
         )
-        (own_up_gate, own_down), (other_up_gate, other_down) = expert_grads
-        grad_up_gate = own_up_gate + swap(other_up_gate)
-        grad_down = own_down + swap(other_down)
-        received = []
-        for origin, piece in swap_pieces(
-            lambda to: lax.dynamic_slice_in_dim(grad_up_gate, to * share, share, 0), place, width
-        ):
-            received.append(piece)
-            d_up_gate = lax.dynamic_update_slice(
-                d_up_gate, piece[None, None], (number, origin, 0, 0)
-            )
-        for origin, piece in swap_pieces(
-            lambda to: lax.dynamic_slice_in_dim(grad_down, to * share, share, 1), place, width
-        ):
-            received.append(piece)
-            d_down = lax.dynamic_update_slice(d_down, piece[None, None], (number, origin, 0, 0))
+        d_expert = [mine + swap(other) for mine, other in zip(*expert_grads)]
+        d_expert[2] = d_expert[2].reshape(ff, width, share).transpose(1, 0, 2)
+        d_experts.insert(0, [to_experts(part.reshape(width, -1, part.shape[-1])) for part in d_expert])
         back = scatter_chips(back, 5).astype(jnp.float32)
         grad_gates = (
             back[:, MODEL_WIDTH : MODEL_WIDTH + EXPERTS]
@@ -1306,38 +1612,39 @@
         unused_mid, norm_back = jax.vjp(norm_rows, middle, g_ffn[number])
         grad_mid_part, grad_g_ffn = norm_back(grad_mixer)
         grad_middle = grad_state + grad_mid_part
-        low = gather_chips(after(grad_middle.astype(jnp.bfloat16), grad_up_gate, grad_down), 6, PLANE)
-        grad_normed, grad_wqkv, grad_wout, grad_gq, grad_gk = attention_backward(
+        low = gather_chips(after(grad_middle.astype(jnp.bfloat16), *d_expert), 6, PLANE)
+        grad_qkv, grad_wqkv, grad_wout, grad_gq, grad_gk = attention_backward(
             low, memo, dense, angles
         )
+        d_out.insert(0, line_sum(*half_sum(grad_wout)).astype(jnp.float32))
+        mine, other = half_sum(grad_wqkv)
+        summed = line_sum(mine, other).reshape(width, short, qkv_columns)
+        grad_normed = lax.dot_general(
+            after(grad_qkv, other),
+            dense[0],
+            (((1,), (1,)), ((), ())),
+            preferred_element_type=jnp.float32,
+        ).astype(jnp.bfloat16)
+        grad_normed = scatter_chips(grad_normed, 7, PLANE)
         grad_normed = by_place(grad_normed.astype(jnp.float32), width)
         unused_state, norm_front = jax.vjp(norm_rows, state, g_attn[number])
         grad_in_part, grad_g_attn = norm_front(grad_normed)
         grad_state = grad_middle + grad_in_part
         grad_low = grad_state.astype(jnp.bfloat16)
         if number > 0:
-            grad_gathered = gather_chips(after(grad_low, *received), 2)
-
-        def line_sum(operand):
-            half = operand.shape[0] // 2
-            mine = lax.dynamic_slice_in_dim(operand, core * half, half, 0)
-            other = swap(lax.dynamic_slice_in_dim(operand, (1 - core) * half, half, 0))
-            return lax.psum_scatter(mine + other, LINE, scatter_dimension=0, tiled=True)
-
-        d_out.insert(0, line_sum(grad_wout).astype(jnp.float32))
-        summed = line_sum(grad_wqkv).reshape(width, short, qkv_columns)
-        whole = jnp.zeros_like(summed)
-        for origin, piece in swap_pieces(
-            lambda to: lax.dynamic_index_in_dim(summed, to, 0, keepdims=False), place, width
-        ):
-            whole = lax.dynamic_update_index_in_dim(whole, piece, origin, 0)
-        d_qkv.insert(0, whole)
+            grad_gathered = gather_chips(grad_low, 2)
+        back_qkv.insert(
+            0,
+            swap_pieces(
+                lambda to: lax.dynamic_index_in_dim(summed, to, 0, keepdims=False), place, width
+            ),
+        )
         gain_grads = jnp.concatenate([grad_g_attn, grad_g_ffn, grad_gq, grad_gk])
         small_grads.insert(0, (grad_router, gain_grads.reshape(devices, -1)))
     d_out = jnp.stack(d_out)
-    d_gate = d_up_gate[..., :ff].astype(jnp.float32)
-    d_up = d_up_gate[..., ff:].astype(jnp.float32)
-    d_down = d_down.astype(jnp.float32)
+    d_gate, d_up, d_down = [
+        jnp.stack([entry[i].astype(jnp.float32) for entry in d_experts]) for i in range(3)
+    ]
     own_gains = jnp.concatenate([gain_grad for _, gain_grad in small_grads], axis=1)
     own_gains = jnp.pad(own_gains, ((0, 0), (0, gain_columns * short - gains.size)))
     side = jnp.concatenate(
@@ -1354,7 +1661,13 @@
     )
     d_gains = small[:, router_columns : router_columns + gain_columns].reshape(-1)[: gains.size]
     d_gains = d_gains.reshape(gains.shape)
-    d_qkv = jnp.stack(d_qkv).astype(jnp.float32)
+    d_qkv = jnp.zeros((DECODER_LAYERS, width, short, qkv_columns), jnp.bfloat16)
+    for number in reversed(range(DECODER_LAYERS)):
+        for origin, piece in back_qkv[number]:
+            if number > 0:
+                piece = after(piece, side)
+            d_qkv = lax.dynamic_update_slice(d_qkv, piece[None, None], (number, origin, 0, 0))
+    d_qkv = d_qkv.astype(jnp.float32)
     cut = group * HEAD_SIZE
     d_query = (
         d_qkv[..., :cut]

time: 1830 us -> 1670 us (0.913)
  Pallas kernels: 877 us -> 1030 us
  waiting for transfers between devices: 201 us -> 78.4 us
  local copies, waits for them, and re-layouts: 219 us -> 115 us
  matrix products: 296 us -> 238 us
    pallas_call x0 -> x2, Pallas kernels: none -> 281 us  [layer_weights(): pl.pallas_call(partial(weights_kernel, layer, depth, work is not None), o...]
    ppermute x36 -> x9, waiting for transfers between devices: 201 us -> 6.58 us  [swap_pieces(): got = lax.ppermute(sent, FSDP, [(i, i ^ step) for i in range(width)])]
    pallas_call x9 -> x8, Pallas kernels: 428 us -> 323 us  [gather_chips(): pl.pallas_call(partial(gather_kernel, grid, depth), out_shape=jax.ShapeDt...]
    all_to_all x0 -> x6, waiting for transfers between devices: none -> 66.6 us  [to_experts(): return lax.all_to_all(part, FSDP, split_axis=0, concat_axis=0, tiled=True)]
    dynamic_update_slice x44 -> x7, local copies, waits for them, and re-layouts: 65.9 us -> 4.15 us  [the longest x3 3.18 us: chip_shards(): by_source = lax.dynamic_update_index_in_dim(by_source, piece, origin, 0)]
    ppermute x36 -> x9, starting transfers between devices: 43.8 us -> 11.1 us  [swap_pieces(): got = lax.ppermute(sent, FSDP, [(i, i ^ step) for i in range(width)])]
    all_to_all x0 -> x6, starting transfers between devices: none -> 29 us  [to_experts(): return lax.all_to_all(part, FSDP, split_axis=0, concat_axis=0, tiled=True)]
    pallas_call x9, Pallas kernels: 448 us -> 423 us  [scatter_chips(): pl.pallas_call(partial(scatter_kernel, grid, depth), out_shape=jax.ShapeD...]
  transfers between devices with their start and end apart: 62 -> 32, of which waited for: 13 -> 7; matrix products, arithmetic and copies ran while one was open for 31% -> 20% of each run, Pallas kernels for 44% -> 49%
where the time goes in v3:
time: 1670 us; the launch traced here: 1660 us
  Pallas kernels  1030 us (62%)
  matrix products  238 us (14%)
  other arithmetic  126 us (8%)
  local copies, waits for them, and re-layouts  115 us (7%)
  waiting for transfers between devices  78.4 us (5%)
  starting transfers between devices  42.4 us (3%)
  between operations  31.9 us (2%)
    pallas_call x9, Pallas kernels, scatter_chips(): pl.pallas_call(partial(scatter_kernel, grid, depth), out_shape=jax.ShapeD...  423 us
    pallas_call x8, Pallas kernels, gather_chips(): pl.pallas_call(partial(gather_kernel, grid, depth), out_shape=jax.ShapeDt...  323 us
    pallas_call x2, Pallas kernels, layer_weights(): pl.pallas_call(partial(weights_kernel, layer, depth, work is not None), o...  281 us
    all_to_all x6, waiting for transfers between devices, to_experts(): return lax.all_to_all(part, FSDP, split_axis=0, concat_axis=0, tiled=True)  66.6 us
    dot_general x8, matrix products, expert_backward(): lax.dot_general(rows, part, (((0,), (0,)), ((), ())), preferred_element_t...  36.2 us
    unnamed x536, local copies, waits for them, and re-layouts  35.3 us
  transfers between devices with their start and end apart: 32, of which 7 were waited for; matrix products, arithmetic and copies ran while one was open for 20% of the time, Pallas kernels for 49%

profile of v3, /device:TPU:0, one launch (start us, length us, event | category | flops | bytes accessed | tf_op | source)
XLA Modules:
  0.0 1658.9 jit_solution(7606867916034554990)
XLA Ops:
  21.6 30.3 %shard_map.212 = bf16[16,128,128]{2,1,0:T(8,128)(2,1)} custom-call(bf16[128,128]{1,0:T(8,128)(2,1)} %pad.42.x_ref), custom_call_target="tpu_custom_call" | custom-call | bytes 17301504 | tf_op jit(solution)/shard_map/pallas_call | solution.py:745
  58.9 18.2 %shard_map.213 = bf16[4,128,2048]{2,1,0:T(8,128)(2,1)} custom-call(bf16[128,2048]{1,0:T(8,128)(2,1)} %copy.439.x_ref), custom_call_target="tpu_custom_call" | custom-call | bytes 69206016 | tf_op jit(solution)/shard_map/pallas_call | solution.py:745
  82.5 111.1 %shard_map.214 = (bf16[2048,1536]{1,0:T(8,128)(2,1)}, bf16[2048,1536]{1,0:T(8,128)(2,1)}, bf16[768,2048]{1,0:T(8,128)(2,1)}, bf16[768,2048]{1,0:T(8,128)(2,1)}, ...) custom-call(bf16[2,4,512,768]{3,2,1,0:T(8,128)(2,1)} %refs_0_.3, bf16[2,4,512,768]{3,2,1,0:T(8,128)(2,1)} %refs_1_.3, ...), custom_call_target="tpu_custom_call" | custom-call | bytes 419430400 | tf_op jit(solution)/shard_map/pallas_call | solution.py:1172
  193.6 5.4 fusion.253
  217.1 19.7 %shard_map.215 = bf16[128,2048]{1,0:T(8,128)(2,1)S(1)} custom-call(bf16[4,128,2048]{2,1,0:T(8,128)(2,1)S(1)} %bitcast.481), custom_call_target="tpu_custom_call" | custom-call | bytes 69206016 | tf_op jit(solution)/shard_map/pallas_call | solution.py:842
  238.2 64.4 %shard_map.216.refs_5_ = bf16[16,128,2048]{2,1,0:T(8,128)(2,1)} custom-call(bf16[128,2048]{1,0:T(8,128)(2,1)} %multiply_convert_fusion.10.x_ref), custom_call_target="tpu_custom_call" | custom-call | bytes 276824064 | tf_op jit(solution)/shard_map/pallas_call | solution.py:745
  314.4 5.9 fusion.250
  326.1 170.1 %shard_map.217 = (bf16[2048,1536]{1,0:T(8,128)(2,1)}, bf16[2048,1536]{1,0:T(8,128)(2,1)}, bf16[768,2048]{1,0:T(8,128)(2,1)}, bf16[768,2048]{1,0:T(8,128)(2,1)}, ...) custom-call(bf16[2,4,512,768]{3,2,1,0:T(8,128)(2,1)} %refs_0_.3, ...), custom_call_target="tpu_custom_call" | custom-call | bytes 419430400 | tf_op jit(solution)/shard_map/pallas_call | solution.py:1172
  496.3 67.7 %shard_map.218 = bf16[128,2048]{1,0:T(8,128)(2,1)S(1)} custom-call(bf16[16,128,2048]{2,1,0:T(8,128)(2,1)} %get-tuple-element.36.x_ref), custom_call_target="tpu_custom_call" | custom-call | bytes 276824064 | tf_op jit(solution)/shard_map/pallas_call | solution.py:842
  566.2 19.6 %shard_map.219 = bf16[4,128,2048]{2,1,0:T(8,128)(2,1)} custom-call(bf16[128,2048]{1,0:T(8,128)(2,1)} %copy.464.x_ref), custom_call_target="tpu_custom_call" | custom-call | bytes 69206016 | tf_op jit(solution)/shard_map/pallas_call | solution.py:745
  585.8 6.0 fusion.254
  614.6 17.1 %shard_map.220 = bf16[128,2048]{1,0:T(8,128)(2,1)S(1)} custom-call(bf16[4,128,2048]{2,1,0:T(8,128)(2,1)S(1)} %bitcast.482), custom_call_target="tpu_custom_call" | custom-call | bytes 69206016 | tf_op jit(solution)/shard_map/pallas_call | solution.py:842
  633.5 70.2 %shard_map.221 = bf16[16,128,2048]{2,1,0:T(8,128)(2,1)} custom-call(bf16[128,2048]{1,0:T(8,128)(2,1)} %multiply_convert_fusion.8.x_ref), custom_call_target="tpu_custom_call" | custom-call | bytes 276824064 | tf_op jit(solution)/shard_map/pallas_call | solution.py:745
  703.7 5.9 fusion.252
  717.7 5.8 convolution_convert_fusion.23
  723.5 6.7 fusion.256
  730.2 7.0 fusion.255
  753.3 5.3 convolution_convert_fusion.26
  767.6 6.9 multiply_convert_fusion.4
  774.5 5.3 convolution_convert_fusion.27
  782.1 4.9 convolution_convert_fusion.1.x_ref
  787.0 71.7 %shard_map.223 = bf16[128,2176]{1,0:T(8,128)(2,1)S(1)} custom-call(bf16[16,128,2176]{2,1,0:T(8,128)(2,1)} %convolution_convert_fusion.1.x_ref), custom_call_target="tpu_custom_call" | custom-call | bytes 294125568 | tf_op jit(solution)/shard_map/pallas_call | solution.py:842
  885.1 20.2 %shard_map.224 = bf16[4,128,2048]{2,1,0:T(8,128)(2,1)} custom-call(bf16[128,2048]{1,0:T(8,128)(2,1)} %convert_select_fusion.1.x_ref), custom_call_target="tpu_custom_call" | custom-call | bytes 69206016 | tf_op jit(solution)/shard_map/pallas_call | solution.py:745
  905.3 5.3 fusion.67
  940.9 5.1 collective-permute-done.7
  961.2 5.0 multiply_convert_fusion
  973.8 92.5 %shard_map.222 = bf16[128,2048]{1,0:T(8,128)(2,1)S(1)} custom-call(bf16[16,128,2048]{2,1,0:T(8,128)(2,1)} %fusion.10.x_ref), custom_call_target="tpu_custom_call" | custom-call | bytes 276824064 | tf_op jit(solution)/shard_map/pallas_call | solution.py:842
  1077.6 5.7 convolution_convert_fusion.31
  1083.3 41.9 %shard_map.225 = bf16[128,2048]{1,0:T(8,128)(2,1)S(1)} custom-call(bf16[4,128,2048]{2,1,0:T(8,128)(2,1)S(1)} %bitcast.479), custom_call_target="tpu_custom_call" | custom-call | bytes 69206016 | tf_op jit(solution)/shard_map/pallas_call | solution.py:842
  1133.0 71.1 %shard_map.226 = bf16[16,128,2048]{2,1,0:T(8,128)(2,1)} custom-call(bf16[128,2048]{1,0:T(8,128)(2,1)} %get-tuple-element.150.x_ref), custom_call_target="tpu_custom_call" | custom-call | bytes 276824064 | tf_op jit(solution)/shard_map/pallas_call | solution.py:745
  1219.5 5.3 convolution_convert_fusion.24
  1237.7 5.3 convolution_convert_fusion.25
  1250.2 71.7 %shard_map.227 = bf16[128,2176]{1,0:T(8,128)(2,1)S(1)} custom-call(bf16[16,128,2176]{2,1,0:T(8,128)(2,1)} %convolution_convert_fusion.x_ref), custom_call_target="tpu_custom_call" | custom-call | bytes 294125568 | tf_op jit(solution)/shard_map/pallas_call | solution.py:842
  1324.7 5.1 all-to-all-start.1
  1329.8 6.0 fusion.16
  1354.9 28.5 %shard_map.228 = bf16[4,128,2048]{2,1,0:T(8,128)(2,1)} custom-call(bf16[128,2048]{1,0:T(8,128)(2,1)} %convert_select_fusion.x_ref), custom_call_target="tpu_custom_call" | custom-call | bytes 69206016 | tf_op jit(solution)/shard_map/pallas_call | solution.py:745
  1383.4 5.0 all-to-all-start.3
  1408.3 16.1 all-to-all-done.3
  1449.7 15.2 all-to-all-done.2
  1477.7 27.5 %all-to-all-done.4 = bf16[4,768,512]{2,1,0:T(8,128)(2,1)} async-done(((bf16[4,768,512]{2,1,0:T(8,128)(2,1)}), bf16[4,768,512]{2,1,0:T(8,128)(2,1)}, u32[]{:S(2)}, u32[]{:S(2)}) %all-to-all-start.4) | async-done | bytes 3145760 | tf_op jit(solution)/shard_map/all_to_all | solution.py:1522
  1519.6 8.5 maximum_convert_fusion.2
  1532.2 8.4 maximum_convert_fusion.1
  1540.6 7.8 all-to-all-done
  1548.4 8.4 maximum_convert_fusion
  1559.3 5.9 convolution_convert_fusion.30
  1565.2 20.9 %shard_map.229 = bf16[128,2048]{1,0:T(8,128)(2,1)S(1)} custom-call(bf16[4,128,2048]{2,1,0:T(8,128)(2,1)S(1)} %bitcast.480), custom_call_target="tpu_custom_call" | custom-call | bytes 69206016 | tf_op jit(solution)/shard_map/pallas_call | solution.py:842
  1596.0 19.9 %shard_map.230 = bf16[128,128]{1,0:T(8,128)(2,1)S(1)} custom-call(bf16[16,128,128]{2,1,0:T(8,128)(2,1)S(1)} %bitcast.483), custom_call_target="tpu_custom_call" | custom-call | bytes 17301504 | tf_op jit(solution)/shard_map/pallas_call | solution.py:842
  1633.3 6.2 collective-permute-done.16
  (903 shorter events, 383.1 us)
Async XLA Ops:
  7.2 730.1 %all-gather.2.cloned.1.call-start = ((), (), s32[]{:S(2)}) async-start(), calls=%async_computation.10 | async-start | bytes 8912896 | tf_op jit(solution)/shard_map/all_gather | solution.py:503
  9.2 11.6 collective-permute-start
  16.0 64.3 %collective-permute-start.3 = (bf16[2,64,1280]{2,1,0:T(8,128)(2,1)}, bf16[2,64,1280]{2,1,0:T(8,128)(2,1)}, u32[]{:S(2)}, u32[]{:S(2)}) collective-permute-start(bf16[2,64,1280]{2,1,0:T(8,128)(2,1)} %get-tuple-element.189), channel_id=1, source_target_pairs={{0,24},{8,16},{16,8},{24,0},{1,25},{9,17},{17,9},{25,1},{2,26},{10... | collective-permute-start | bytes 983048 | tf_op jit(solution)/shard_map/ppermute | solution.py:1200
  19.5 58.6 %collective-permute-start.1 = (bf16[2,64,1280]{2,1,0:T(8,128)(2,1)}, bf16[2,64,1280]{2,1,0:T(8,128)(2,1)}, u32[]{:S(2)}, u32[]{:S(2)}) collective-permute-start(bf16[2,64,1280]{2,1,0:T(8,128)(2,1)} %get-tuple-element.191), channel_id=1, source_target_pairs={{0,8},{8,0},{16,24},{24,16},{1,9},{9,1},{17,25},{25,17},{2,10},{10... | collective-permute-start | bytes 983048 | tf_op jit(solution)/shard_map/ppermute | solution.py:1200
  20.0 59.3 %collective-permute-start.2 = (bf16[2,64,1280]{2,1,0:T(8,128)(2,1)}, bf16[2,64,1280]{2,1,0:T(8,128)(2,1)}, u32[]{:S(2)}, u32[]{:S(2)}) collective-permute-start(bf16[2,64,1280]{2,1,0:T(8,128)(2,1)} %get-tuple-element.192), channel_id=1, source_target_pairs={{0,16},{8,24},{16,0},{24,8},{1,17},{9,25},{17,1},{25,9},{2,18},{10... | collective-permute-start | bytes 983048 | tf_op jit(solution)/shard_map/ppermute | solution.py:1200
  20.5 180.2 %copy-start.173 = (f32[64]{0:T(128)}, f32[64]{0:T(128)S(1)}, u32[]{:S(2)}) copy-start(f32[64]{0:T(128)S(1)} %multiply_exponential_fusion) | copy-start | bytes 772
  53.2 147.5 %copy-start.152 = (f32[512]{0:T(512)}, f32[512]{0:T(512)S(1)}, u32[]{:S(2)}) copy-start(f32[512]{0:T(512)S(1)} %convert_bitcast_fusion.2) | copy-start | bytes 6148
  57.6 142.7 %copy-start.177 = (f32[128]{0:T(128)}, f32[128]{0:T(128)S(1)}, u32[]{:S(2)}) copy-start(f32[128]{0:T(128)S(1)} %get-tuple-element.230) | copy-start | bytes 1540
  78.1 128.7 %copy-start.54 = (f32[512,64]{1,0:T(8,128)}, f32[512,64]{1,0:T(8,128)S(1)}, u32[]{:S(2)}) copy-start(f32[512,64]{1,0:T(8,128)S(1)} %get-tuple-element.240) | copy-start | bytes 393220
  78.1 522.8 %copy-start.51 = (f32[512,64]{1,0:T(8,128)}, f32[512,64]{1,0:T(8,128)S(1)}, u32[]{:S(2)}) copy-start(f32[512,64]{1,0:T(8,128)S(1)} %get-tuple-element.239) | copy-start | bytes 393220
  82.5 111.1 %copy-start.87 = (bf16[4,128,2048]{2,1,0:T(8,128)(2,1)S(1)}, bf16[4,128,2048]{2,1,0:T(8,128)(2,1)}, u32[]{:S(2)}) copy-start(bf16[4,128,2048]{2,1,0:T(8,128)(2,1)} %shard_map.213) | copy-start | bytes 6291460
  236.9 327.1 %copy-start = (bf16[128,2048]{1,0:T(8,128)(2,1)}, bf16[128,2048]{1,0:T(8,128)(2,1)S(1)}, u32[]{:S(2)}) copy-start(bf16[128,2048]{1,0:T(8,128)(2,1)S(1)} %shard_map.215) | copy-start | bytes 1572868
  305.9 1208.1 %reduce-scatter.5.cloned.1.call-start = ((), (), s32[]{:S(2)}) async-start(), calls=%async_computation.11 | async-start | bytes 3276800 | tf_op jit(solution)/shard_map/reduce_scatter | solution.py:1575
  324.1 172.2 %copy-start.156 = (f32[16,48]{1,0:T(8,128)}, f32[16,48]{1,0:T(8,128)S(1)}, u32[]{:S(2)}) copy-start(f32[16,48]{1,0:T(8,128)S(1)} %multiply_reduce_fusion.17) | copy-start | bytes 9220
  325.2 171.1 %copy-start.158 = (f32[16,48]{1,0:T(8,128)}, f32[16,48]{1,0:T(8,128)S(1)}, u32[]{:S(2)}) copy-start(f32[16,48]{1,0:T(8,128)S(1)} %multiply_reduce_fusion.18) | copy-start | bytes 9220
  564.3 318.8 %copy-start.8 = (f32[128,2048]{1,0:T(8,128)}, f32[128,2048]{1,0:T(8,128)S(1)}, u32[]{:S(2)}) copy-start(f32[128,2048]{1,0:T(8,128)S(1)} %get-tuple-element.161) | copy-start | bytes 3145732
  711.1 147.9 %copy-start.24 = (f32[2048,32]{1,0:T(8,128)}, f32[2048,32]{1,0:T(8,128)S(1)}, u32[]{:S(2)}) copy-start(f32[2048,32]{1,0:T(8,128)S(1)} %fusion.108) | copy-start | bytes 786436
  767.1 94.7 %collective-permute-start.4 = (bf16[2048,768]{1,0:T(8,128)(2,1)}, bf16[2048,768]{1,0:T(8,128)(2,1)}, u32[]{:S(2)}, u32[]{:S(2)}) collective-permute-start(bf16[2048,768]{1,0:T(8,128)(2,1)} %convolution_convert_fusion.18), channel_id=1, source_target_pairs={{0,1},{1,0},{2,3},{3,2},{4,5},{5,4},{6,7},{7,6},{8,9},{9,8},{10,11... | collective-permute-start | bytes 9437192 | tf_op jit(solution)/shard_map/ppermute | solution.py:486
  767.1 101.3 %collective-permute-start.5 = (bf16[2048,768]{1,0:T(8,128)(2,1)}, bf16[2048,768]{1,0:T(8,128)(2,1)}, u32[]{:S(2)}, u32[]{:S(2)}) collective-permute-start(bf16[2048,768]{1,0:T(8,128)(2,1)} %convolution_convert_fusion.16), channel_id=1, source_target_pairs={{0,1},{1,0},{2,3},{3,2},{4,5},{5,4},{6,7},{7,6},{8,9},{9,8},{10,11... | collective-permute-start | bytes 9437192 | tf_op jit(solution)/shard_map/ppermute | solution.py:486
  767.6 107.2 %collective-permute-start.6 = (bf16[768,2048]{1,0:T(8,128)(2,1)}, bf16[768,2048]{1,0:T(8,128)(2,1)}, u32[]{:S(2)}, u32[]{:S(2)}) collective-permute-start(bf16[768,2048]{1,0:T(8,128)(2,1)} %convolution_convert_fusion.14), channel_id=1, source_target_pairs={{0,1},{1,0},{2,3},{3,2},{4,5},{5,4},{6,7},{7,6},{8,9},{9,8},{10,11... | collective-permute-start | bytes 9437192 | tf_op jit(solution)/shard_map/ppermute | solution.py:486
  940.9 5.1 collective-permute-start.7
  959.7 111.6 %collective-permute-start.20 = (bf16[512,2048]{1,0:T(8,128)(2,1)}, bf16[512,2048]{1,0:T(8,128)(2,1)S(1)}, u32[]{:S(2)}, u32[]{:S(2)}) collective-permute-start(bf16[512,2048]{1,0:T(8,128)(2,1)} %constant_dynamic-slice_fusion.13), channel_id=1, source_target_pairs={{0,1},{1,0},{2,3},{3,2},{4,5},{5,4},{6,7},{7,6},{8,9},{9,8},{10,11... | collective-permute-start | bytes 6291464 | tf_op jit(solution)/shard_map/ppermute | solution.py:486
  1066.4 258.3 %all-to-all-start.5 = ((bf16[4,768,512]{2,1,0:T(8,128)(2,1)}), bf16[4,768,512]{2,1,0:T(8,128)(2,1)}, u32[]{:S(2)}, u32[]{:S(2)}) async-start(bf16[4,768,512]{2,1,0:T(8,128)(2,1)} %bitcast.500), calls=%async_computation.9 | async-start | bytes 6291456 | tf_op jit(solution)/shard_map/all_to_all | solution.py:1522
  1071.1 554.0 %reduce-scatter.11.cloned.1.call-start = ((), (), s32[]{:S(2)}) async-start(), calls=%async_computation.14 | async-start | bytes 2621440 | tf_op jit(solution)/shard_map/reduce_scatter | solution.py:1575
  1233.3 96.6 %collective-permute-start.8 = (bf16[2048,768]{1,0:T(8,128)(2,1)}, bf16[2048,768]{1,0:T(8,128)(2,1)}, u32[]{:S(2)}, u32[]{:S(2)}) collective-permute-start(bf16[2048,768]{1,0:T(8,128)(2,1)} %convolution_convert_fusion.10), channel_id=1, source_target_pairs={{0,1},{1,0},{2,3},{3,2},{4,5},{5,4},{6,7},{7,6},{8,9},{9,8},{10,11... | collective-permute-start | bytes 9437192 | tf_op jit(solution)/shard_map/ppermute | solution.py:486
  1233.3 105.5 %collective-permute-start.9 = (bf16[2048,768]{1,0:T(8,128)(2,1)}, bf16[2048,768]{1,0:T(8,128)(2,1)}, u32[]{:S(2)}, u32[]{:S(2)}) collective-permute-start(bf16[2048,768]{1,0:T(8,128)(2,1)} %convolution_convert_fusion.8), channel_id=1, source_target_pairs={{0,1},{1,0},{2,3},{3,2},{4,5},{5,4},{6,7},{7,6},{8,9},{9,8},{10,11... | collective-permute-start | bytes 9437192 | tf_op jit(solution)/shard_map/ppermute | solution.py:486
  1233.8 111.4 %collective-permute-start.10 = (bf16[768,2048]{1,0:T(8,128)(2,1)}, bf16[768,2048]{1,0:T(8,128)(2,1)}, u32[]{:S(2)}, u32[]{:S(2)}) collective-permute-start(bf16[768,2048]{1,0:T(8,128)(2,1)} %convolution_convert_fusion.6), channel_id=1, source_target_pairs={{0,1},{1,0},{2,3},{3,2},{4,5},{5,4},{6,7},{7,6},{8,9},{9,8},{10,11... | collective-permute-start | bytes 9437192 | tf_op jit(solution)/shard_map/ppermute | solution.py:486
  1250.2 72.9 %copy-start.1 = (bf16[128,2048]{1,0:T(8,128)(2,1)S(1)}, bf16[128,2048]{1,0:T(8,128)(2,1)}, u32[]{:S(2)}) copy-start(bf16[128,2048]{1,0:T(8,128)(2,1)} %copy-done) | copy-start | bytes 1572868
  1250.2 73.0 %copy-start.17 = (bf16[128,2048]{1,0:T(8,128)(2,1)S(1)}, bf16[128,2048]{1,0:T(8,128)(2,1)}, u32[]{:S(2)}) copy-start(bf16[128,2048]{1,0:T(8,128)(2,1)} %param.13) | copy-start | bytes 1572868
  1250.2 73.0 %copy-start.50 = (bf16[16,128,128]{2,1,0:T(8,128)(2,1)S(1)}, bf16[16,128,128]{2,1,0:T(8,128)(2,1)}, u32[]{:S(2)}) copy-start(bf16[16,128,128]{2,1,0:T(8,128)(2,1)} %shard_map.212) | copy-start | bytes 1572868
  1250.2 73.0 %copy-start.138 = (f32[1,2048]{1,0:T(1,128)S(1)}, f32[1,2048]{1,0:T(1,128)}, u32[]{:S(2)}) copy-start(f32[1,2048]{1,0:T(1,128)} %get-tuple-element.233) | copy-start | bytes 24580
  1250.2 73.0 %copy-start.190 = (f32[128]{0:T(128)S(1)}, f32[128]{0:T(128)}, u32[]{:S(2)}) copy-start(f32[128]{0:T(128)} %copy-done.189) | copy-start | bytes 1540
  1324.7 58.7 %all-to-all-start.1 = ((bf16[4,512,768]{2,1,0:T(8,128)(2,1)}), bf16[4,512,768]{2,1,0:T(8,128)(2,1)}, u32[]{:S(2)}, u32[]{:S(2)}) async-start(bf16[4,512,768]{2,1,0:T(8,128)(2,1)} %bitcast.548), calls=%async_computation.5 | async-start | bytes 6291456 | tf_op jit(solution)/shard_map/all_to_all | solution.py:1522
  1383.4 41.0 %all-to-all-start.3 = ((bf16[4,512,768]{2,1,0:T(8,128)(2,1)}), bf16[4,512,768]{2,1,0:T(8,128)(2,1)}, u32[]{:S(2)}, u32[]{:S(2)}) async-start(bf16[4,512,768]{2,1,0:T(8,128)(2,1)} %bitcast.547), calls=%async_computation.7 | async-start | bytes 6291456 | tf_op jit(solution)/shard_map/all_to_all | solution.py:1522
  1405.6 40.3 %collective-permute-start.19 = (bf16[512,2048]{1,0:T(8,128)(2,1)}, bf16[512,2048]{1,0:T(8,128)(2,1)}, u32[]{:S(2)}, u32[]{:S(2)}) collective-permute-start(bf16[512,2048]{1,0:T(8,128)(2,1)} %constant_dynamic-slice_fusion), channel_id=1, source_target_pairs={{0,1},{1,0},{2,3},{3,2},{4,5},{5,4},{6,7},{7,6},{8,9},{9,8},{10,11... | collective-permute-start | bytes 6291464 | tf_op jit(solution)/shard_map/ppermute | solution.py:486
  1424.4 40.5 %all-to-all-start.2 = ((bf16[4,512,768]{2,1,0:T(8,128)(2,1)}), bf16[4,512,768]{2,1,0:T(8,128)(2,1)}, u32[]{:S(2)}, u32[]{:S(2)}) async-start(bf16[4,512,768]{2,1,0:T(8,128)(2,1)} %bitcast.550), calls=%async_computation.6 | async-start | bytes 6291456 | tf_op jit(solution)/shard_map/all_to_all | solution.py:1522
  1429.2 195.9 %reduce-scatter.9.cloned.1.call-start = ((), (), s32[]{:S(2)}) async-start(), calls=%async_computation.13 | async-start | bytes 2621440 | tf_op jit(solution)/shard_map/reduce_scatter | solution.py:1575
  1464.9 40.3 %all-to-all-start.4 = ((bf16[4,768,512]{2,1,0:T(8,128)(2,1)}), bf16[4,768,512]{2,1,0:T(8,128)(2,1)}, u32[]{:S(2)}, u32[]{:S(2)}) async-start(bf16[4,768,512]{2,1,0:T(8,128)(2,1)} %bitcast.502), calls=%async_computation.8 | async-start | bytes 6291456 | tf_op jit(solution)/shard_map/all_to_all | solution.py:1522
  1477.7 50.4 %collective-permute-start.11 = (bf16[1024,1280]{1,0:T(8,128)(2,1)}, bf16[1024,1280]{1,0:T(8,128)(2,1)}, u32[]{:S(2)}, u32[]{:S(2)}) collective-permute-start(bf16[1024,1280]{1,0:T(8,128)(2,1)} %constant_dynamic-slice_fusion.2), channel_id=1, source_target_pairs={{0,1},{1,0},{2,3},{3,2},{4,5},{5,4},{6,7},{7,6},{8,9},{9,8},{10,11... | collective-permute-start | bytes 7864328 | tf_op jit(solution)/shard_map/ppermute | solution.py:486
  1505.2 43.2 %all-to-all-start = ((bf16[4,512,768]{2,1,0:T(8,128)(2,1)}), bf16[4,512,768]{2,1,0:T(8,128)(2,1)}, u32[]{:S(2)}, u32[]{:S(2)}) async-start(bf16[4,512,768]{2,1,0:T(8,128)(2,1)} %bitcast.549), calls=%async_computation.4 | async-start | bytes 6291456 | tf_op jit(solution)/shard_map/all_to_all | solution.py:1522
  1510.0 117.7 %reduce-scatter.7.cloned.1.call-start = ((), (), s32[]{:S(2)}) async-start(), calls=%async_computation.12 | async-start | bytes 3276800 | tf_op jit(solution)/shard_map/reduce_scatter | solution.py:1575
  1516.1 106.3 %collective-permute-start.15 = (bf16[64,1280]{1,0:T(8,128)(2,1)}, bf16[64,1280]{1,0:T(8,128)(2,1)}, u32[]{:S(2)}, u32[]{:S(2)}) collective-permute-start(bf16[64,1280]{1,0:T(8,128)(2,1)} %get-tuple-element.198), channel_id=1, source_target_pairs={{0,24},{8,16},{16,8},{24,0},{1,25},{9,17},{17,9},{25,1},{2,26},{10... | collective-permute-start | bytes 491528 | tf_op jit(solution)/shard_map/ppermute | solution.py:1200
  1518.9 102.6 %collective-permute-start.14 = (bf16[64,1280]{1,0:T(8,128)(2,1)}, bf16[64,1280]{1,0:T(8,128)(2,1)}, u32[]{:S(2)}, u32[]{:S(2)}) collective-permute-start(bf16[64,1280]{1,0:T(8,128)(2,1)} %get-tuple-element.199), channel_id=1, source_target_pairs={{0,16},{8,24},{16,0},{24,8},{1,17},{9,25},{17,1},{25,9},{2,18},{10... | collective-permute-start | bytes 491528 | tf_op jit(solution)/shard_map/ppermute | solution.py:1200
  1519.4 101.0 %collective-permute-start.13 = (bf16[64,1280]{1,0:T(8,128)(2,1)}, bf16[64,1280]{1,0:T(8,128)(2,1)}, u32[]{:S(2)}, u32[]{:S(2)}) collective-permute-start(bf16[64,1280]{1,0:T(8,128)(2,1)} %get-tuple-element.200), channel_id=1, source_target_pairs={{0,8},{8,0},{16,24},{24,16},{1,9},{9,1},{17,25},{25,17},{2,10},{10... | collective-permute-start | bytes 491528 | tf_op jit(solution)/shard_map/ppermute | solution.py:1200
  1617.8 5.6 collective-permute-start.12
  1628.8 11.1 collective-permute-start.18
  1630.4 9.5 collective-permute-start.17
  1631.4 8.1 collective-permute-start.16
  (242 other events, 2067.2 us)
Sparse Core Ops, SparseCore 0:
  306.0 185.0 all-gather.1
  951.1 76.4 reduce-scatter.4
  1075.2 50.0 reduce-scatter.10
  1449.8 46.4 reduce-scatter.8
  1532.3 54.7 reduce-scatter.6

commit v4 on v3

--- a/solution.py
+++ b/solution.py
@@ -671,20 +671,32 @@
         pl.when(test)(action)
 
 
-def gather_kernel(grid, depth, x_ref, out_ref, own_sem, send_sems, recv_sems):
-    plan = routes_of_shards(grid, depth)
+def gather_steps(plan, here, x_ref, out_ref, own_sem, send_sems, recv_sems):
     number_of = {item: i for i, (item, _) in enumerate(plan)}
     unit = x_ref.shape[0] // ROW_UNITS
-    here = Place(grid, depth)
     own = pltpu.make_async_copy(x_ref, out_ref.at[here.shard(0, 0)], own_sem)
-    own.start()
-    here.meet()
     sent = []
+    steps = []
+
+    def passing(bits, offset, neighbour, first, last, there, site, own_piece):
+        rows = pl.ds(first * unit, (last - first) * unit)
+        target = out_ref.at[here.shard(bits, offset), rows]
+        return pltpu.make_async_remote_copy(
+            src_ref=x_ref.at[rows] if own_piece else target,
+            dst_ref=target,
+            send_sem=send_sems.at[site],
+            recv_sem=recv_sems.at[number_of[there]],
+            device_id=here.device(neighbour),
+            device_id_type=pl.DeviceIdType.MESH,
+        )
+
     for item, hops in plan:
         bits, offset = (0, 0) if item is None else item[:2]
 
         def step(item=item, hops=hops, bits=bits, offset=offset, site=len(sent)):
-            if item is not None:
+            if item is None:
+                own.start()
+            else:
                 piece = out_ref.at[
                     here.shard(bits, offset), pl.ds(item[2] * unit, (item[3] - item[2]) * unit)
                 ]
@@ -699,33 +711,36 @@
             for hop, (neighbour, first, last, there) in enumerate(hops):
                 when(
                     here.holds(0, neighbour) if neighbour in (ABOVE, BELOW) else None,
-                    lambda n=neighbour, f=first, l=last, t=there, s=site + hop: passing(
-                        bits, offset, n, f, l, t, s, item is None
+                    lambda n=neighbour, f=first, l=last, t=there, k=site + hop: passing(
+                        bits, offset, n, f, l, t, k, item is None
                     ).start(),
                 )
 
-        def passing(bits, offset, neighbour, first, last, there, site, own_piece):
-            rows = pl.ds(first * unit, (last - first) * unit)
-            target = out_ref.at[here.shard(bits, offset), rows]
-            return pltpu.make_async_remote_copy(
-                src_ref=x_ref.at[rows] if own_piece else target,
-                dst_ref=target,
-                send_sem=send_sems.at[site],
-                recv_sem=recv_sems.at[number_of[there]],
-                device_id=here.device(neighbour),
-                device_id_type=pl.DeviceIdType.MESH,
+        steps.append(
+            lambda step=step, item=item, offset=offset: when(
+                None if item is None else here.holds(offset), step
             )
-
-        when(None if item is None else here.holds(offset), step)
+        )
         for neighbour, first, last, there in hops:
             sent.append((bits, offset, neighbour, first, last, there, len(sent), item is None))
-    for bits, offset, neighbour, first, last, there, site, own_piece in sent:
-
-        def finish(a=(bits, offset, neighbour, first, last, there, site, own_piece)):
-            passing(*a).wait_send()
-
-        when(here.holds(offset, neighbour), finish)
-    own.wait()
+
+    def finish():
+        for one in sent:
+            when(here.holds(one[1], one[2]), lambda one=one: passing(*one).wait_send())
+        own.wait()
+
+    return steps, finish
+
+
+def gather_kernel(grid, depth, x_ref, out_ref, own_sem, send_sems, recv_sems):
+    here = Place(grid, depth)
+    here.meet()
+    steps, finish = gather_steps(
+        routes_of_shards(grid, depth), here, x_ref, out_ref, own_sem, send_sems, recv_sems
+    )
+    for step in steps:
+        step()
+    finish()
 
 
 def count_plan(grid, depth):
@@ -900,7 +915,7 @@
             pl.when(g == number)(action)
 
 
-def weights_kernel(layer, depth, working, *refs):
+def weights_kernel(layer, depth, working, gathering, *refs):
     refs = list(refs)
 
     def take(count):
@@ -910,10 +925,12 @@
 
     w_gate, w_up, w_down, qkv_ref, w_out_ref = take(5)
     inputs = take(9) if working else []
+    small_in = take(1) if gathering else []
     up_gate_refs = take(2)
     down_refs = take(2)
     dense_refs = take(2)
     outputs = take(7) if working else []
+    small_out = take(1) if gathering else []
     own_sems, send_sems, recv_sems, side_send, side_recv, line_send, line_recv = take(7)
     here = Place(ALL_CHIPS, depth)
     share = w_gate.shape[2]
@@ -1024,15 +1041,28 @@
     for k in range(2):
         for neighbour in (ABOVE, BELOW):
             when(here.holds(0, neighbour), lambda k=k, n=neighbour: along(k, 0, n).start())
-    for k in range(3):
+
+    def send_across(k):
         for bits in (3, 1, 2):
             across(bits, k).start()
+
+    if gathering:
+        gather, gathered = gather_steps(
+            routes_of_shards(ALL_CHIPS, depth), here, small_in[0], small_out[0], *refs
+        )
+        gather[0]()
+    send_across(0)
     for copy in kept:
         copy.start()
     for k in range(3):
         beside(0, k).start()
     for k in range(2):
         dense_beside(k, 0).start()
+    if gathering:
+        for step in gather[1:]:
+            step()
+    for k in range(1, 3):
+        send_across(k)
     def arrived(offset):
         for k in range(2):
             remote(
@@ -1119,9 +1149,13 @@
         when(here.holds(offset), left)
     for copy in kept:
         copy.wait()
-
-
-def layer_weights(layer, w_gate, w_up, w_down, qkv_rows, w_out, collective_id, work=None):
+    if gathering:
+        gathered()
+
+
+def layer_weights(
+    layer, w_gate, w_up, w_down, qkv_rows, w_out, collective_id, work=None, small=None
+):
     depth = lax.axis_size(LINE)
     share, ff = w_gate.shape[2:]
     model = PAIR * share
@@ -1169,8 +1203,19 @@
         )
         out_specs += [pl.BlockSpec(memory_space=pltpu.VMEM)] * 7
         scratch.append(pltpu.VMEM((2, PAIR * cap, model), low))
+    if small is not None:
+        items, hops = count_plan(ALL_CHIPS, depth)
+        operands.append(small)
+        in_specs.append(pl.BlockSpec(memory_space=pl.ANY))
+        shapes.append(jax.ShapeDtypeStruct((PAIR * depth,) + small.shape, small.dtype))
+        out_specs.append(pl.BlockSpec(memory_space=pl.ANY))
+        scratch += [
+            pltpu.SemaphoreType.DMA,
+            pltpu.SemaphoreType.DMA((hops,)),
+            pltpu.SemaphoreType.DMA((items,)),
+        ]
     made = pl.pallas_call(
-        partial(weights_kernel, layer, depth, work is not None),
+        partial(weights_kernel, layer, depth, work is not None, small is not None),
         out_shape=shapes,
         in_specs=in_specs,
         out_specs=out_specs,
@@ -1305,11 +1350,14 @@
     return grad_qkv, grad_wqkv, grad_wout, grad_gq, grad_gk
 
 
-def send_back(picks, pieces):
+def send_back(picks, pieces, waits=()):
+    pick = jnp.concatenate(picks, axis=1)
+    if waits:
+        pick = after(pick, *waits)
     return (
         jnp.einsum(
             SPREAD,
-            jnp.concatenate(picks, axis=1),
+            pick,
             jnp.concatenate(pieces, axis=1),
             preferred_element_type=jnp.float32,
         )
@@ -1338,7 +1386,7 @@
     return send_back(picks, pieces), memo
 
 
-def expert_backward(gathered, picks, row_gates, weights, memo, experts):
+def expert_backward(gathered, picks, row_gates, weights, memo, experts, waits):
     blocks = picks[0].shape[0]
     width = gathered.shape[1]
     grouped = gathered.reshape(blocks, -1, width)
@@ -1390,7 +1438,7 @@
         piece = jnp.concatenate([grad_in, gate_part], axis=1)
         pieces.append(piece.reshape(blocks, -1, width + GATE_COLUMNS))
         grads.append((grad_gate, grad_up, grad_down))
-    return send_back(picks, pieces), grads
+    return send_back(picks, pieces, waits), grads
 
 
 def chip_shards(
@@ -1438,7 +1486,6 @@
     )
     small = jnp.pad(small, ((0, 0), (0, -small.shape[1] % 128)))
 
-    small = gather_chips(small, 1)
 
     qkv_columns = (group + 2) * HEAD_SIZE
 
@@ -1465,6 +1512,13 @@
     def rows_by_source(number):
         return by_source[:, number].reshape(width * short, qkv_columns)
 
+    def weights_of(number, work=None, beside=None):
+        return layer_weights(
+            number, w_gate, w_up, w_down, rows_by_source(number), w_out, 10 + number, work, beside
+        )
+
+    weights, qkv_whole, out_whole, made = weights_of(0, beside=small)
+    small = made[0].reshape(chips * rows, -1)
     routers = [
         small[:, number * EXPERTS : (number + 1) * EXPERTS] for number in range(DECODER_LAYERS)
     ]
@@ -1521,12 +1575,6 @@
     def to_experts(part):
         return lax.all_to_all(part, FSDP, split_axis=0, concat_axis=0, tiled=True)
 
-    def weights_of(number, work=None):
-        return layer_weights(
-            number, w_gate, w_up, w_down, rows_by_source(number), w_out, 10 + number, work
-        )
-
-    weights, qkv_whole, out_whole, unused_made = weights_of(0)
     state = tokens.astype(jnp.float32)
     kept = []
     for number in range(DECODER_LAYERS):
@@ -1574,6 +1622,15 @@
     def line_sum(mine, other):
         return lax.psum_scatter(mine + other, LINE, scatter_dimension=0, tiled=True)
 
+    def out_sum(mine, other):
+        return line_sum(mine, other).astype(jnp.float32)
+
+    def qkv_sum(mine, other):
+        summed = line_sum(mine, other).reshape(width, short, qkv_columns)
+        return swap_pieces(
+            lambda to: lax.dynamic_index_in_dim(summed, to, 0, keepdims=False), place, width
+        )
+
     grad_state = cotangent.astype(jnp.float32)
     grad_low = cotangent
     grad_gathered = cotangent_all
@@ -1581,17 +1638,24 @@
     d_out = []
     back_qkv = []
     d_experts = []
+    earlier = []
+    held = None
     for number in reversed(range(DECODER_LAYERS)):
         state, middle, mixer_in, own_gates, row_gates, dense, weights, memo, expert_memo = kept[
             number
         ]
         back, expert_grads = expert_backward(
-            grad_gathered, picks[number], row_gates, weights, expert_memo, (first, second)
+            grad_gathered, picks[number], row_gates, weights, expert_memo, (first, second), earlier
         )
         d_expert = [mine + swap(other) for mine, other in zip(*expert_grads)]
         d_expert[2] = d_expert[2].reshape(ff, width, share).transpose(1, 0, 2)
         d_experts.insert(0, [to_experts(part.reshape(width, -1, part.shape[-1])) for part in d_expert])
-        back = scatter_chips(back, 5).astype(jnp.float32)
+        back_low = scatter_chips(back, 5)
+        if held is not None:
+            out_halves, qkv_halves = held
+            d_out.insert(0, out_sum(after(out_halves[0], grad_gathered), out_halves[1]))
+            back_qkv.insert(0, qkv_sum(after(qkv_halves[0], back_low), qkv_halves[1]))
+        back = back_low.astype(jnp.float32)
         grad_gates = (
             back[:, MODEL_WIDTH : MODEL_WIDTH + EXPERTS]
             + back[:, MODEL_WIDTH + EXPERTS : MODEL_WIDTH + 2 * EXPERTS]
@@ -1612,13 +1676,18 @@
         unused_mid, norm_back = jax.vjp(norm_rows, middle, g_ffn[number])
         grad_mid_part, grad_g_ffn = norm_back(grad_mixer)
         grad_middle = grad_state + grad_mid_part
-        low = gather_chips(after(grad_middle.astype(jnp.bfloat16), *d_expert), 6, PLANE)
+        low = gather_chips(
+            after(grad_middle.astype(jnp.bfloat16), *d_expert), 6, PLANE
+        )
+        earlier = d_experts[0]
         grad_qkv, grad_wqkv, grad_wout, grad_gq, grad_gk = attention_backward(
             low, memo, dense, angles
         )
-        d_out.insert(0, line_sum(*half_sum(grad_wout)).astype(jnp.float32))
-        mine, other = half_sum(grad_wqkv)
-        summed = line_sum(mine, other).reshape(width, short, qkv_columns)
+        held = half_sum(grad_wout), half_sum(grad_wqkv)
+        other = held[1][1]
+        if number == 0:
+            d_out.insert(0, out_sum(*held[0]))
+            back_qkv.insert(0, qkv_sum(*held[1]))
         grad_normed = lax.dot_general(
             after(grad_qkv, other),
             dense[0],
@@ -1633,12 +1702,6 @@
         grad_low = grad_state.astype(jnp.bfloat16)
         if number > 0:
             grad_gathered = gather_chips(grad_low, 2)
-        back_qkv.insert(
-            0,
-            swap_pieces(
-                lambda to: lax.dynamic_index_in_dim(summed, to, 0, keepdims=False), place, width
-            ),
-        )
         gain_grads = jnp.concatenate([grad_g_attn, grad_g_ffn, grad_gq, grad_gk])
         small_grads.insert(0, (grad_router, gain_grads.reshape(devices, -1)))
     d_out = jnp.stack(d_out)

time: 1670 us -> 1660 us (level)
  Pallas kernels: 1030 us -> 995 us
    pallas_call x9, Pallas kernels: 423 us -> 382 us  [scatter_chips(): pl.pallas_call(partial(scatter_kernel, grid, depth), out_shape=jax.ShapeD...]
    unnamed x536 -> x534, local copies, waits for them, and re-layouts: 35.3 us -> 44.8 us
    pallas_call x8 -> x7, Pallas kernels: 323 us -> 321 us  [gather_chips(): pl.pallas_call(partial(gather_kernel, grid, depth), out_shape=jax.ShapeDt...]
  transfers between devices with their start and end apart: 32 -> 32, of which waited for: 7 -> 6; matrix products, arithmetic and copies ran while one was open for 20% -> 20% of each run, Pallas kernels for 49% -> 38%
where the time goes in v4:
time: 1660 us; the launch traced here: 1640 us
  Pallas kernels  995 us (60%)
  matrix products  237 us (14%)
  local copies, waits for them, and re-layouts  129 us (8%)
  other arithmetic  127 us (8%)
  waiting for transfers between devices  75.2 us (5%)
  starting transfers between devices  42.2 us (3%)
  between operations  38.2 us (2%)
    pallas_call x9, Pallas kernels, scatter_chips(): pl.pallas_call(partial(scatter_kernel, grid, depth), out_shape=jax.ShapeD...  382 us
    pallas_call x7, Pallas kernels, gather_chips(): pl.pallas_call(partial(gather_kernel, grid, depth), out_shape=jax.ShapeDt...  321 us
    pallas_call x2, Pallas kernels, layer_weights(): pl.pallas_call(partial(weights_kernel, layer, depth, work is not None, sm...  293 us
    all_to_all x6, waiting for transfers between devices, to_experts(): return lax.all_to_all(part, FSDP, split_axis=0, concat_axis=0, tiled=True)  55.7 us
    unnamed x534, local copies, waits for them, and re-layouts  44.8 us
    dot_general x8, matrix products, expert_backward(): lax.dot_general(rows, part, (((0,), (0,)), ((), ())), preferred_element_t...  36.2 us
  transfers between devices with their start and end apart: 32, of which 6 were waited for; matrix products, arithmetic and copies ran while one was open for 20% of the time, Pallas kernels for 38%

profile of v4, /device:TPU:0, one launch (start us, length us, event | category | flops | bytes accessed | tf_op | source)
XLA Modules:
  0.0 1644.2 jit_solution(3832856325146377335)
XLA Ops:
  22.3 12.8 collective-permute-done
  37.3 122.2 %shard_map.212 = (bf16[2048,1536]{1,0:T(8,128)(2,1)}, bf16[2048,1536]{1,0:T(8,128)(2,1)}, bf16[768,2048]{1,0:T(8,128)(2,1)}, bf16[768,2048]{1,0:T(8,128)(2,1)}, ...) custom-call(bf16[2,4,512,768]{3,2,1,0:T(8,128)(2,1)} %refs_0_.3, ...), custom_call_target="tpu_custom_call" | custom-call | bytes 419430400 | tf_op jit(solution)/shard_map/pallas_call | solution.py:1217
  166.2 23.0 %shard_map.213 = bf16[4,128,2048]{2,1,0:T(8,128)(2,1)} custom-call(bf16[128,2048]{1,0:T(8,128)(2,1)} %copy.445.x_ref), custom_call_target="tpu_custom_call" | custom-call | bytes 69206016 | tf_op jit(solution)/shard_map/pallas_call | solution.py:760
  189.2 6.0 fusion.255
  217.1 19.2 %shard_map.214 = bf16[128,2048]{1,0:T(8,128)(2,1)S(1)} custom-call(bf16[4,128,2048]{2,1,0:T(8,128)(2,1)S(1)} %bitcast.485), custom_call_target="tpu_custom_call" | custom-call | bytes 69206016 | tf_op jit(solution)/shard_map/pallas_call | solution.py:857
  237.6 62.3 %shard_map.215.refs_5_ = bf16[16,128,2048]{2,1,0:T(8,128)(2,1)} custom-call(bf16[128,2048]{1,0:T(8,128)(2,1)} %multiply_convert_fusion.10.x_ref), custom_call_target="tpu_custom_call" | custom-call | bytes 276824064 | tf_op jit(solution)/shard_map/pallas_call | solution.py:760
  308.4 6.2 fusion.252
  323.0 170.4 %shard_map.216 = (bf16[2048,1536]{1,0:T(8,128)(2,1)}, bf16[2048,1536]{1,0:T(8,128)(2,1)}, bf16[768,2048]{1,0:T(8,128)(2,1)}, bf16[768,2048]{1,0:T(8,128)(2,1)}, ...) custom-call(bf16[2,4,512,768]{3,2,1,0:T(8,128)(2,1)} %refs_0_.3, ...), custom_call_target="tpu_custom_call" | custom-call | bytes 419430400 | tf_op jit(solution)/shard_map/pallas_call | solution.py:1217
  493.5 67.7 %shard_map.217 = bf16[128,2048]{1,0:T(8,128)(2,1)S(1)} custom-call(bf16[16,128,2048]{2,1,0:T(8,128)(2,1)} %get-tuple-element.38.x_ref), custom_call_target="tpu_custom_call" | custom-call | bytes 276824064 | tf_op jit(solution)/shard_map/pallas_call | solution.py:857
  563.3 19.6 %shard_map.218 = bf16[4,128,2048]{2,1,0:T(8,128)(2,1)} custom-call(bf16[128,2048]{1,0:T(8,128)(2,1)} %copy.464.x_ref), custom_call_target="tpu_custom_call" | custom-call | bytes 69206016 | tf_op jit(solution)/shard_map/pallas_call | solution.py:760
  582.9 6.0 fusion.256
  611.7 17.0 %shard_map.219 = bf16[128,2048]{1,0:T(8,128)(2,1)S(1)} custom-call(bf16[4,128,2048]{2,1,0:T(8,128)(2,1)S(1)} %bitcast.486), custom_call_target="tpu_custom_call" | custom-call | bytes 69206016 | tf_op jit(solution)/shard_map/pallas_call | solution.py:857
  630.0 70.6 %shard_map.220 = bf16[16,128,2048]{2,1,0:T(8,128)(2,1)} custom-call(bf16[128,2048]{1,0:T(8,128)(2,1)} %multiply_convert_fusion.8.x_ref), custom_call_target="tpu_custom_call" | custom-call | bytes 276824064 | tf_op jit(solution)/shard_map/pallas_call | solution.py:760
  700.6 5.9 fusion.254
  721.8 6.6 fusion.258
  728.5 7.0 fusion.257
  751.6 5.3 convolution_convert_fusion.26
  765.8 6.9 multiply_convert_fusion.4
  772.7 5.3 convolution_convert_fusion.27
  779.6 5.0 convolution_convert_fusion.1.x_ref
  784.5 71.7 %shard_map.222 = bf16[128,2176]{1,0:T(8,128)(2,1)S(1)} custom-call(bf16[16,128,2176]{2,1,0:T(8,128)(2,1)} %convolution_convert_fusion.1.x_ref), custom_call_target="tpu_custom_call" | custom-call | bytes 294125568 | tf_op jit(solution)/shard_map/pallas_call | solution.py:857
  866.2 5.0 all-to-all-start.2
  871.2 5.7 fusion.13
  889.2 34.6 %shard_map.223 = bf16[4,128,2048]{2,1,0:T(8,128)(2,1)} custom-call(bf16[128,2048]{1,0:T(8,128)(2,1)} %convert_select_fusion.1.x_ref), custom_call_target="tpu_custom_call" | custom-call | bytes 69206016 | tf_op jit(solution)/shard_map/pallas_call | solution.py:760
  923.8 5.2 fusion.67
  966.8 20.3 %all-to-all-done = bf16[4,512,768]{2,1,0:T(8,128)(2,1)} async-done(((bf16[4,512,768]{2,1,0:T(8,128)(2,1)}), bf16[4,512,768]{2,1,0:T(8,128)(2,1)}, u32[]{:S(2)}, u32[]{:S(2)}) %all-to-all-start) | async-done | bytes 3145760 | tf_op jit(solution)/shard_map/all_to_all | solution.py:1576
  992.1 5.0 multiply_convert_fusion
  1004.7 82.7 %shard_map.221 = bf16[128,2048]{1,0:T(8,128)(2,1)S(1)} custom-call(bf16[16,128,2048]{2,1,0:T(8,128)(2,1)} %fusion.10.x_ref), custom_call_target="tpu_custom_call" | custom-call | bytes 276824064 | tf_op jit(solution)/shard_map/pallas_call | solution.py:857
  1097.4 5.6 convolution_convert_fusion.31
  1103.0 18.3 %shard_map.224 = bf16[128,2048]{1,0:T(8,128)(2,1)S(1)} custom-call(bf16[4,128,2048]{2,1,0:T(8,128)(2,1)S(1)} %bitcast.483), custom_call_target="tpu_custom_call" | custom-call | bytes 69206016 | tf_op jit(solution)/shard_map/pallas_call | solution.py:857
  1129.6 65.6 %shard_map.225 = bf16[16,128,2048]{2,1,0:T(8,128)(2,1)} custom-call(bf16[128,2048]{1,0:T(8,128)(2,1)} %get-tuple-element.152.x_ref), custom_call_target="tpu_custom_call" | custom-call | bytes 276824064 | tf_op jit(solution)/shard_map/pallas_call | solution.py:760
  1213.7 5.5 convolution_convert_fusion.25
  1219.3 5.3 convolution_convert_fusion.24
  1226.9 4.9 convolution_convert_fusion.x_ref
  1231.8 63.9 %shard_map.226 = bf16[128,2176]{1,0:T(8,128)(2,1)S(1)} custom-call(bf16[16,128,2176]{2,1,0:T(8,128)(2,1)} %convolution_convert_fusion.x_ref), custom_call_target="tpu_custom_call" | custom-call | bytes 294125568 | tf_op jit(solution)/shard_map/pallas_call | solution.py:857
  1337.9 5.1 fusion.16
  1356.1 6.0 fusion.18
  1367.1 45.1 %shard_map.227 = bf16[4,128,2048]{2,1,0:T(8,128)(2,1)} custom-call(bf16[128,2048]{1,0:T(8,128)(2,1)} %convert_select_fusion.x_ref), custom_call_target="tpu_custom_call" | custom-call | bytes 69206016 | tf_op jit(solution)/shard_map/pallas_call | solution.py:760
  1412.2 5.2 fusion.68
  1461.8 27.9 %all-to-all-done.5 = bf16[4,768,512]{2,1,0:T(8,128)(2,1)} async-done(((bf16[4,768,512]{2,1,0:T(8,128)(2,1)}), bf16[4,768,512]{2,1,0:T(8,128)(2,1)}, u32[]{:S(2)}, u32[]{:S(2)}) %all-to-all-start.5) | async-done | bytes 3145760 | tf_op jit(solution)/shard_map/all_to_all | solution.py:1576
  1504.3 8.5 maximum_convert_fusion.2
  1516.9 8.4 maximum_convert_fusion.1
  1525.4 7.5 all-to-all-done.3
  1532.9 8.5 maximum_convert_fusion
  1543.8 5.7 convolution_convert_fusion.30
  1549.5 20.8 %shard_map.228 = bf16[128,2048]{1,0:T(8,128)(2,1)S(1)} custom-call(bf16[4,128,2048]{2,1,0:T(8,128)(2,1)S(1)} %bitcast.484), custom_call_target="tpu_custom_call" | custom-call | bytes 69206016 | tf_op jit(solution)/shard_map/pallas_call | solution.py:857
  1580.2 20.9 %shard_map.229 = bf16[128,128]{1,0:T(8,128)(2,1)S(1)} custom-call(bf16[16,128,128]{2,1,0:T(8,128)(2,1)S(1)} %bitcast.487), custom_call_target="tpu_custom_call" | custom-call | bytes 17301504 | tf_op jit(solution)/shard_map/pallas_call | solution.py:857
  1618.6 6.3 collective-permute-done.16
  (908 shorter events, 385.9 us)
Async XLA Ops:
  7.2 728.4 %all-gather.2.cloned.1.call-start = ((), (), s32[]{:S(2)}) async-start(), calls=%async_computation.10 | async-start | bytes 8912896 | tf_op jit(solution)/shard_map/all_gather | solution.py:503
  9.2 12.3 collective-permute-start.3
  15.9 20.3 %collective-permute-start.2 = (bf16[2,64,1280]{2,1,0:T(8,128)(2,1)S(1)}, bf16[2,64,1280]{2,1,0:T(8,128)(2,1)S(1)}, u32[]{:S(2)}, u32[]{:S(2)}) collective-permute-start(bf16[2,64,1280]{2,1,0:T(8,128)(2,1)S(1)} %get-tuple-element.191), channel_id=1, source_target_pairs={{0,24},{8,16},{16,8},{24,0},{1,25},{9,17},{17,9},{25,1},{2,26},{10... | collective-permute-start | bytes 983048 | tf_op jit(solution)/shard_map/ppermute | solution.py:1245
  19.3 15.8 collective-permute-start
  19.9 16.2 collective-permute-start.1
  19.9 177.5 %copy-start.167 = (f32[64]{0:T(128)}, f32[64]{0:T(128)S(1)}, u32[]{:S(2)}) copy-start(f32[64]{0:T(128)S(1)} %multiply_exponential_fusion) | copy-start | bytes 772
  20.7 143.4 %copy-start.182 = (f32[128]{0:T(128)}, f32[128]{0:T(128)S(1)}, u32[]{:S(2)}) copy-start(f32[128]{0:T(128)S(1)} %fusion.215) | copy-start | bytes 1540
  164.1 72.5 %copy-start.136 = (f32[1,2048]{1,0:T(1,128)}, f32[1,2048]{1,0:T(1,128)S(1)}, u32[]{:S(2)}) copy-start(f32[1,2048]{1,0:T(1,128)S(1)} %get-tuple-element.235) | copy-start | bytes 24580
  164.1 464.9 %copy-start.126 = (f32[1,2048]{1,0:T(1,128)}, f32[1,2048]{1,0:T(1,128)S(1)}, u32[]{:S(2)}) copy-start(f32[1,2048]{1,0:T(1,128)S(1)} %get-tuple-element.234) | copy-start | bytes 24580
  198.5 399.6 %copy-start.55 = (f32[512,64]{1,0:T(8,128)}, f32[512,64]{1,0:T(8,128)S(1)}, u32[]{:S(2)}) copy-start(f32[512,64]{1,0:T(8,128)S(1)} %get-tuple-element.241) | copy-start | bytes 393220
  236.3 324.9 %copy-start = (bf16[128,2048]{1,0:T(8,128)(2,1)}, bf16[128,2048]{1,0:T(8,128)(2,1)S(1)}, u32[]{:S(2)}) copy-start(bf16[128,2048]{1,0:T(8,128)(2,1)S(1)} %shard_map.214) | copy-start | bytes 1572868
  319.3 174.1 %copy-start.120 = (f32[16,1,128,1]{2,3,1,0:T(1,128)}, f32[16,1,128,1]{2,3,1,0:T(1,128)S(1)}, u32[]{:S(2)}) copy-start(f32[16,1,128,1]{2,3,1,0:T(1,128)S(1)} %get-tuple-element.216) | copy-start | bytes 24580
  319.3 174.1 %copy-start.122 = (f32[16,1,128,1]{2,3,1,0:T(1,128)}, f32[16,1,128,1]{2,3,1,0:T(1,128)S(1)}, u32[]{:S(2)}) copy-start(f32[16,1,128,1]{2,3,1,0:T(1,128)S(1)} %get-tuple-element.215) | copy-start | bytes 24580
  319.5 173.9 %copy-start.151 = (f32[16,48]{1,0:T(8,128)}, f32[16,48]{1,0:T(8,128)S(1)}, u32[]{:S(2)}) copy-start(f32[16,48]{1,0:T(8,128)S(1)} %multiply_reduce_fusion.17) | copy-start | bytes 9220
  320.6 172.8 %copy-start.153 = (f32[16,48]{1,0:T(8,128)}, f32[16,48]{1,0:T(8,128)S(1)}, u32[]{:S(2)}) copy-start(f32[16,48]{1,0:T(8,128)S(1)} %multiply_reduce_fusion.18) | copy-start | bytes 9220
  561.5 326.4 %copy-start.8 = (f32[128,2048]{1,0:T(8,128)}, f32[128,2048]{1,0:T(8,128)S(1)}, u32[]{:S(2)}) copy-start(f32[128,2048]{1,0:T(8,128)S(1)} %get-tuple-element.163) | copy-start | bytes 3145732
  629.0 71.6 %copy-start.210 = (f32[128]{0:T(128)}, f32[128]{0:T(128)S(1)}, u32[]{:S(2)}) copy-start(f32[128]{0:T(128)S(1)} %multiply_reduce_fusion.12) | copy-start | bytes 1540
  629.0 71.6 %copy-start.179 = (f32[128]{0:T(128)}, f32[128]{0:T(128)S(1)}, u32[]{:S(2)}) copy-start(f32[128]{0:T(128)S(1)} %fusion.218) | copy-start | bytes 1540
  708.0 148.5 %copy-start.27 = (f32[2048,32]{1,0:T(8,128)}, f32[2048,32]{1,0:T(8,128)S(1)}, u32[]{:S(2)}) copy-start(f32[2048,32]{1,0:T(8,128)S(1)} %fusion.108) | copy-start | bytes 786436
  765.2 106.0 %collective-permute-start.4 = (bf16[2048,768]{1,0:T(8,128)(2,1)}, bf16[2048,768]{1,0:T(8,128)(2,1)}, u32[]{:S(2)}, u32[]{:S(2)}) collective-permute-start(bf16[2048,768]{1,0:T(8,128)(2,1)} %convolution_convert_fusion.18), channel_id=1, source_target_pairs={{0,1},{1,0},{2,3},{3,2},{4,5},{5,4},{6,7},{7,6},{8,9},{9,8},{10,11... | collective-permute-start | bytes 9437192 | tf_op jit(solution)/shard_map/ppermute | solution.py:486
  765.2 113.6 %collective-permute-start.5 = (bf16[2048,768]{1,0:T(8,128)(2,1)}, bf16[2048,768]{1,0:T(8,128)(2,1)}, u32[]{:S(2)}, u32[]{:S(2)}) collective-permute-start(bf16[2048,768]{1,0:T(8,128)(2,1)} %convolution_convert_fusion.16), channel_id=1, source_target_pairs={{0,1},{1,0},{2,3},{3,2},{4,5},{5,4},{6,7},{7,6},{8,9},{9,8},{10,11... | collective-permute-start | bytes 9437192 | tf_op jit(solution)/shard_map/ppermute | solution.py:486
  765.7 93.0 %collective-permute-start.6 = (bf16[768,2048]{1,0:T(8,128)(2,1)}, bf16[768,2048]{1,0:T(8,128)(2,1)}, u32[]{:S(2)}, u32[]{:S(2)}) collective-permute-start(bf16[768,2048]{1,0:T(8,128)(2,1)} %convolution_convert_fusion.14), channel_id=1, source_target_pairs={{0,1},{1,0},{2,3},{3,2},{4,5},{5,4},{6,7},{7,6},{8,9},{9,8},{10,11... | collective-permute-start | bytes 9437192 | tf_op jit(solution)/shard_map/ppermute | solution.py:486
  784.5 72.0 %copy-start.127 = (f32[1,2048]{1,0:T(1,128)S(1)}, f32[1,2048]{1,0:T(1,128)}, u32[]{:S(2)}) copy-start(f32[1,2048]{1,0:T(1,128)} %copy-done.126) | copy-start | bytes 24580
  784.5 72.0 %copy-start.180 = (f32[128]{0:T(128)S(1)}, f32[128]{0:T(128)}, u32[]{:S(2)}) copy-start(f32[128]{0:T(128)} %copy-done.179) | copy-start | bytes 1540
  866.2 81.9 %all-to-all-start.2 = ((bf16[4,768,512]{2,1,0:T(8,128)(2,1)}), bf16[4,768,512]{2,1,0:T(8,128)(2,1)}, u32[]{:S(2)}, u32[]{:S(2)}) async-start(bf16[4,768,512]{2,1,0:T(8,128)(2,1)} %bitcast.509), calls=%async_computation.2 | async-start | bytes 6291456 | tf_op jit(solution)/shard_map/all_to_all | solution.py:1576
  948.1 39.0 %all-to-all-start = ((bf16[4,512,768]{2,1,0:T(8,128)(2,1)}), bf16[4,512,768]{2,1,0:T(8,128)(2,1)}, u32[]{:S(2)}, u32[]{:S(2)}) async-start(bf16[4,512,768]{2,1,0:T(8,128)(2,1)} %bitcast.557), calls=%async_computation | async-start | bytes 6291456 | tf_op jit(solution)/shard_map/all_to_all | solution.py:1576
  966.8 128.0 %collective-permute-start.7 = (bf16[1024,1280]{1,0:T(8,128)(2,1)}, bf16[1024,1280]{1,0:T(8,128)(2,1)}, u32[]{:S(2)}, u32[]{:S(2)}) collective-permute-start(bf16[1024,1280]{1,0:T(8,128)(2,1)} %constant_dynamic-slice_fusion.3), channel_id=1, source_target_pairs={{0,1},{1,0},{2,3},{3,2},{4,5},{5,4},{6,7},{7,6},{8,9},{9,8},{10,11... | collective-permute-start | bytes 7864328 | tf_op jit(solution)/shard_map/ppermute | solution.py:486
  987.1 105.3 %all-to-all-start.1 = ((bf16[4,512,768]{2,1,0:T(8,128)(2,1)}), bf16[4,512,768]{2,1,0:T(8,128)(2,1)}, u32[]{:S(2)}, u32[]{:S(2)}) async-start(bf16[4,512,768]{2,1,0:T(8,128)(2,1)} %bitcast.555), calls=%async_computation.1 | async-start | bytes 6291456 | tf_op jit(solution)/shard_map/all_to_all | solution.py:1576
  991.9 506.9 %reduce-scatter.5.cloned.1.call-start = ((), (), s32[]{:S(2)}) async-start(), calls=%async_computation.11 | async-start | bytes 3276800 | tf_op jit(solution)/shard_map/reduce_scatter | solution.py:1623
  1302.3 308.0 %reduce-scatter.11.cloned.1.call-start = ((), (), s32[]{:S(2)}) async-start(), calls=%async_computation.14 | async-start | bytes 2621440 | tf_op jit(solution)/shard_map/reduce_scatter | solution.py:1623
  1309.1 19.5 %collective-permute-start.20 = (bf16[512,2048]{1,0:T(8,128)(2,1)}, bf16[512,2048]{1,0:T(8,128)(2,1)S(1)}, u32[]{:S(2)}, u32[]{:S(2)}) collective-permute-start(bf16[512,2048]{1,0:T(8,128)(2,1)} %constant_dynamic-slice_fusion.13), channel_id=1, source_target_pairs={{0,1},{1,0},{2,3},{3,2},{4,5},{5,4},{6,7},{7,6},{8,9},{9,8},{10,11... | collective-permute-start | bytes 6291464 | tf_op jit(solution)/shard_map/ppermute | solution.py:486
  1316.2 21.7 %collective-permute-start.8 = (bf16[2048,768]{1,0:T(8,128)(2,1)}, bf16[2048,768]{1,0:T(8,128)(2,1)}, u32[]{:S(2)}, u32[]{:S(2)}) collective-permute-start(bf16[2048,768]{1,0:T(8,128)(2,1)} %convolution_convert_fusion.10), channel_id=1, source_target_pairs={{0,1},{1,0},{2,3},{3,2},{4,5},{5,4},{6,7},{7,6},{8,9},{9,8},{10,11... | collective-permute-start | bytes 9437192 | tf_op jit(solution)/shard_map/ppermute | solution.py:486
  1320.3 24.6 %collective-permute-start.9 = (bf16[2048,768]{1,0:T(8,128)(2,1)}, bf16[2048,768]{1,0:T(8,128)(2,1)}, u32[]{:S(2)}, u32[]{:S(2)}) collective-permute-start(bf16[2048,768]{1,0:T(8,128)(2,1)} %convolution_convert_fusion.8), channel_id=1, source_target_pairs={{0,1},{1,0},{2,3},{3,2},{4,5},{5,4},{6,7},{7,6},{8,9},{9,8},{10,11... | collective-permute-start | bytes 9437192 | tf_op jit(solution)/shard_map/ppermute | solution.py:486
  1325.0 31.1 %collective-permute-start.10 = (bf16[768,2048]{1,0:T(8,128)(2,1)}, bf16[768,2048]{1,0:T(8,128)(2,1)}, u32[]{:S(2)}, u32[]{:S(2)}) collective-permute-start(bf16[768,2048]{1,0:T(8,128)(2,1)} %convolution_convert_fusion.6), channel_id=1, source_target_pairs={{0,1},{1,0},{2,3},{3,2},{4,5},{5,4},{6,7},{7,6},{8,9},{9,8},{10,11... | collective-permute-start | bytes 9437192 | tf_op jit(solution)/shard_map/ppermute | solution.py:486
  1351.1 97.7 %all-to-all-start.4 = ((bf16[4,512,768]{2,1,0:T(8,128)(2,1)}), bf16[4,512,768]{2,1,0:T(8,128)(2,1)}, u32[]{:S(2)}, u32[]{:S(2)}) async-start(bf16[4,512,768]{2,1,0:T(8,128)(2,1)} %bitcast.556), calls=%async_computation.8 | async-start | bytes 6291456 | tf_op jit(solution)/shard_map/all_to_all | solution.py:1576
  1355.8 254.5 %reduce-scatter.9.cloned.1.call-start = ((), (), s32[]{:S(2)}) async-start(), calls=%async_computation.13 | async-start | bytes 2621440 | tf_op jit(solution)/shard_map/reduce_scatter | solution.py:1623
  1427.3 17.8 %collective-permute-start.19 = (bf16[512,2048]{1,0:T(8,128)(2,1)}, bf16[512,2048]{1,0:T(8,128)(2,1)}, u32[]{:S(2)}, u32[]{:S(2)}) collective-permute-start(bf16[512,2048]{1,0:T(8,128)(2,1)} %constant_dynamic-slice_fusion), channel_id=1, source_target_pairs={{0,1},{1,0},{2,3},{3,2},{4,5},{5,4},{6,7},{7,6},{8,9},{9,8},{10,11... | collective-permute-start | bytes 6291464 | tf_op jit(solution)/shard_map/ppermute | solution.py:486
  1448.9 40.8 %all-to-all-start.5 = ((bf16[4,768,512]{2,1,0:T(8,128)(2,1)}), bf16[4,768,512]{2,1,0:T(8,128)(2,1)}, u32[]{:S(2)}, u32[]{:S(2)}) async-start(bf16[4,768,512]{2,1,0:T(8,128)(2,1)} %bitcast.507), calls=%async_computation.9 | async-start | bytes 6291456 | tf_op jit(solution)/shard_map/all_to_all | solution.py:1576
  1461.8 51.0 %collective-permute-start.11 = (bf16[1024,1280]{1,0:T(8,128)(2,1)}, bf16[1024,1280]{1,0:T(8,128)(2,1)}, u32[]{:S(2)}, u32[]{:S(2)}) collective-permute-start(bf16[1024,1280]{1,0:T(8,128)(2,1)} %constant_dynamic-slice_fusion.2), channel_id=1, source_target_pairs={{0,1},{1,0},{2,3},{3,2},{4,5},{5,4},{6,7},{7,6},{8,9},{9,8},{10,11... | collective-permute-start | bytes 7864328 | tf_op jit(solution)/shard_map/ppermute | solution.py:486
  1489.7 43.2 %all-to-all-start.3 = ((bf16[4,512,768]{2,1,0:T(8,128)(2,1)}), bf16[4,512,768]{2,1,0:T(8,128)(2,1)}, u32[]{:S(2)}, u32[]{:S(2)}) async-start(bf16[4,512,768]{2,1,0:T(8,128)(2,1)} %bitcast.554), calls=%async_computation.7 | async-start | bytes 6291456 | tf_op jit(solution)/shard_map/all_to_all | solution.py:1576
  1494.5 118.5 %reduce-scatter.7.cloned.1.call-start = ((), (), s32[]{:S(2)}) async-start(), calls=%async_computation.12 | async-start | bytes 3276800 | tf_op jit(solution)/shard_map/reduce_scatter | solution.py:1623
  1500.8 106.9 %collective-permute-start.15 = (bf16[64,1280]{1,0:T(8,128)(2,1)}, bf16[64,1280]{1,0:T(8,128)(2,1)}, u32[]{:S(2)}, u32[]{:S(2)}) collective-permute-start(bf16[64,1280]{1,0:T(8,128)(2,1)} %get-tuple-element.200), channel_id=1, source_target_pairs={{0,24},{8,16},{16,8},{24,0},{1,25},{9,17},{17,9},{25,1},{2,26},{10... | collective-permute-start | bytes 491528 | tf_op jit(solution)/shard_map/ppermute | solution.py:1245
  1503.6 103.1 %collective-permute-start.14 = (bf16[64,1280]{1,0:T(8,128)(2,1)}, bf16[64,1280]{1,0:T(8,128)(2,1)}, u32[]{:S(2)}, u32[]{:S(2)}) collective-permute-start(bf16[64,1280]{1,0:T(8,128)(2,1)} %get-tuple-element.201), channel_id=1, source_target_pairs={{0,16},{8,24},{16,0},{24,8},{1,17},{9,25},{17,1},{25,9},{2,18},{10... | collective-permute-start | bytes 491528 | tf_op jit(solution)/shard_map/ppermute | solution.py:1245
  1504.2 101.6 %collective-permute-start.13 = (bf16[64,1280]{1,0:T(8,128)(2,1)}, bf16[64,1280]{1,0:T(8,128)(2,1)}, u32[]{:S(2)}, u32[]{:S(2)}) collective-permute-start(bf16[64,1280]{1,0:T(8,128)(2,1)} %get-tuple-element.202), channel_id=1, source_target_pairs={{0,8},{8,0},{16,24},{24,16},{1,9},{9,1},{17,25},{25,17},{2,10},{10... | collective-permute-start | bytes 491528 | tf_op jit(solution)/shard_map/ppermute | solution.py:1245
  1603.0 5.6 collective-permute-start.12
  1614.1 11.1 collective-permute-start.18
  1615.6 9.5 collective-permute-start.17
  1616.7 8.1 collective-permute-start.16
  (241 other events, 1776.5 us)
Sparse Core Ops, SparseCore 0:
  303.4 185.4 all-gather.1
  1302.4 53.8 reduce-scatter.4
  1358.6 43.5 reduce-scatter.10
  1449.0 45.5 reduce-scatter.8
  1517.0 55.2 reduce-scatter.6

commit v5 on v4

--- a/solution.py
+++ b/solution.py
@@ -1649,7 +1649,6 @@
         )
         d_expert = [mine + swap(other) for mine, other in zip(*expert_grads)]
         d_expert[2] = d_expert[2].reshape(ff, width, share).transpose(1, 0, 2)
-        d_experts.insert(0, [to_experts(part.reshape(width, -1, part.shape[-1])) for part in d_expert])
         back_low = scatter_chips(back, 5)
         if held is not None:
             out_halves, qkv_halves = held
@@ -1679,7 +1678,10 @@
         low = gather_chips(
             after(grad_middle.astype(jnp.bfloat16), *d_expert), 6, PLANE
         )
-        earlier = d_experts[0]
+        if number == 0:
+            d_expert = [after(part, low) for part in d_expert]
+        earlier = [to_experts(part.reshape(width, -1, part.shape[-1])) for part in d_expert]
+        d_experts.insert(0, earlier)
         grad_qkv, grad_wqkv, grad_wout, grad_gq, grad_gk = attention_backward(
             low, memo, dense, angles
         )

time: 1660 us -> 1640 us (0.988)
  Pallas kernels: 995 us -> 975 us
    pallas_call x7, Pallas kernels: 321 us -> 302 us  [gather_chips(): pl.pallas_call(partial(gather_kernel, grid, depth), out_shape=jax.ShapeDt...]
    unnamed x534 -> x538, local copies, waits for them, and re-layouts: 44.8 us -> 43.1 us
  transfers between devices with their start and end apart: 32 -> 32, of which waited for: 6 -> 7; matrix products, arithmetic and copies ran while one was open for 20% -> 20% of each run, Pallas kernels for 38% -> 37%
where the time goes in v5:
time: 1640 us; the launch traced here: 1630 us
  Pallas kernels  975 us (59%)
  matrix products  237 us (14%)
  other arithmetic  133 us (8%)
  local copies, waits for them, and re-layouts  127 us (8%)
  waiting for transfers between devices  78 us (5%)
  starting transfers between devices  42.3 us (3%)
  between operations  39.7 us (2%)
    pallas_call x9, Pallas kernels, scatter_chips(): pl.pallas_call(partial(scatter_kernel, grid, depth), out_shape=jax.ShapeD...  380 us
    pallas_call x7, Pallas kernels, gather_chips(): pl.pallas_call(partial(gather_kernel, grid, depth), out_shape=jax.ShapeDt...  302 us
    pallas_call x2, Pallas kernels, layer_weights(): pl.pallas_call(partial(weights_kernel, layer, depth, work is not None, sm...  292 us
    all_to_all x6, waiting for transfers between devices, to_experts(): return lax.all_to_all(part, FSDP, split_axis=0, concat_axis=0, tiled=True)  58.5 us
    unnamed x538, local copies, waits for them, and re-layouts  43.1 us
    dot_general x8, matrix products, expert_backward(): lax.dot_general(rows, part, (((0,), (0,)), ((), ())), preferred_element_t...  36.3 us
  transfers between devices with their start and end apart: 32, of which 7 were waited for; matrix products, arithmetic and copies ran while one was open for 20% of the time, Pallas kernels for 37%

profile of v5, /device:TPU:0, one launch (start us, length us, event | category | flops | bytes accessed | tf_op | source)
XLA Modules:
  0.0 1632.2 jit_solution(16271001558353324418)
XLA Ops:
  22.3 12.8 collective-permute-done
  37.3 122.2 %shard_map.212 = (bf16[2048,1536]{1,0:T(8,128)(2,1)}, bf16[2048,1536]{1,0:T(8,128)(2,1)}, bf16[768,2048]{1,0:T(8,128)(2,1)}, bf16[768,2048]{1,0:T(8,128)(2,1)}, ...) custom-call(bf16[2,4,512,768]{3,2,1,0:T(8,128)(2,1)} %refs_0_.3, ...), custom_call_target="tpu_custom_call" | custom-call | bytes 419430400 | tf_op jit(solution)/shard_map/pallas_call | solution.py:1217
  166.1 23.0 %shard_map.213 = bf16[4,128,2048]{2,1,0:T(8,128)(2,1)} custom-call(bf16[128,2048]{1,0:T(8,128)(2,1)} %copy.445.x_ref), custom_call_target="tpu_custom_call" | custom-call | bytes 69206016 | tf_op jit(solution)/shard_map/pallas_call | solution.py:760
  189.2 6.0 fusion.255
  217.0 19.2 %shard_map.214 = bf16[128,2048]{1,0:T(8,128)(2,1)S(1)} custom-call(bf16[4,128,2048]{2,1,0:T(8,128)(2,1)S(1)} %bitcast.490), custom_call_target="tpu_custom_call" | custom-call | bytes 69206016 | tf_op jit(solution)/shard_map/pallas_call | solution.py:857
  237.5 62.4 %shard_map.215.refs_5_ = bf16[16,128,2048]{2,1,0:T(8,128)(2,1)} custom-call(bf16[128,2048]{1,0:T(8,128)(2,1)} %multiply_convert_fusion.10.x_ref), custom_call_target="tpu_custom_call" | custom-call | bytes 276824064 | tf_op jit(solution)/shard_map/pallas_call | solution.py:760
  308.5 6.2 fusion.252
  323.1 170.2 %shard_map.216 = (bf16[2048,1536]{1,0:T(8,128)(2,1)}, bf16[2048,1536]{1,0:T(8,128)(2,1)}, bf16[768,2048]{1,0:T(8,128)(2,1)}, bf16[768,2048]{1,0:T(8,128)(2,1)}, ...) custom-call(bf16[2,4,512,768]{3,2,1,0:T(8,128)(2,1)} %refs_0_.3, ...), custom_call_target="tpu_custom_call" | custom-call | bytes 419430400 | tf_op jit(solution)/shard_map/pallas_call | solution.py:1217
  493.4 67.7 %shard_map.217 = bf16[128,2048]{1,0:T(8,128)(2,1)S(1)} custom-call(bf16[16,128,2048]{2,1,0:T(8,128)(2,1)} %get-tuple-element.38.x_ref), custom_call_target="tpu_custom_call" | custom-call | bytes 276824064 | tf_op jit(solution)/shard_map/pallas_call | solution.py:857
  563.3 19.6 %shard_map.218 = bf16[4,128,2048]{2,1,0:T(8,128)(2,1)} custom-call(bf16[128,2048]{1,0:T(8,128)(2,1)} %copy.464.x_ref), custom_call_target="tpu_custom_call" | custom-call | bytes 69206016 | tf_op jit(solution)/shard_map/pallas_call | solution.py:760
  582.9 6.0 fusion.256
  611.6 17.1 %shard_map.219 = bf16[128,2048]{1,0:T(8,128)(2,1)S(1)} custom-call(bf16[4,128,2048]{2,1,0:T(8,128)(2,1)S(1)} %bitcast.491), custom_call_target="tpu_custom_call" | custom-call | bytes 69206016 | tf_op jit(solution)/shard_map/pallas_call | solution.py:857
  629.9 68.5 %shard_map.220 = bf16[16,128,2048]{2,1,0:T(8,128)(2,1)} custom-call(bf16[128,2048]{1,0:T(8,128)(2,1)} %multiply_convert_fusion.8.x_ref), custom_call_target="tpu_custom_call" | custom-call | bytes 276824064 | tf_op jit(solution)/shard_map/pallas_call | solution.py:760
  698.5 5.9 fusion.254
  719.7 6.6 fusion.258
  726.4 7.0 fusion.257
  749.5 5.3 convolution_convert_fusion.26
  763.7 6.9 multiply_convert_fusion.4
  770.6 5.3 convolution_convert_fusion.27
  777.4 5.0 convolution_convert_fusion.1.x_ref
  782.4 71.7 %shard_map.222 = bf16[128,2176]{1,0:T(8,128)(2,1)S(1)} custom-call(bf16[16,128,2176]{2,1,0:T(8,128)(2,1)} %convolution_convert_fusion.1.x_ref), custom_call_target="tpu_custom_call" | custom-call | bytes 294125568 | tf_op jit(solution)/shard_map/pallas_call | solution.py:857
  864.1 5.0 all-to-all-start.2
  869.1 5.7 fusion.13
  887.2 34.4 %shard_map.223 = bf16[4,128,2048]{2,1,0:T(8,128)(2,1)} custom-call(bf16[128,2048]{1,0:T(8,128)(2,1)} %convert_select_fusion.1.x_ref), custom_call_target="tpu_custom_call" | custom-call | bytes 69206016 | tf_op jit(solution)/shard_map/pallas_call | solution.py:760
  921.6 5.2 fusion.67
  964.6 20.8 %all-to-all-done = bf16[4,512,768]{2,1,0:T(8,128)(2,1)} async-done(((bf16[4,512,768]{2,1,0:T(8,128)(2,1)}), bf16[4,512,768]{2,1,0:T(8,128)(2,1)}, u32[]{:S(2)}, u32[]{:S(2)}) %all-to-all-start) | async-done | bytes 3145760 | tf_op jit(solution)/shard_map/all_to_all | solution.py:1576
  990.4 5.0 multiply_convert_fusion
  1003.0 83.1 %shard_map.221 = bf16[128,2048]{1,0:T(8,128)(2,1)S(1)} custom-call(bf16[16,128,2048]{2,1,0:T(8,128)(2,1)} %fusion.10.x_ref), custom_call_target="tpu_custom_call" | custom-call | bytes 276824064 | tf_op jit(solution)/shard_map/pallas_call | solution.py:857
  1096.1 5.6 convolution_convert_fusion.31
  1101.7 18.4 %shard_map.224 = bf16[128,2048]{1,0:T(8,128)(2,1)S(1)} custom-call(bf16[4,128,2048]{2,1,0:T(8,128)(2,1)S(1)} %bitcast.488), custom_call_target="tpu_custom_call" | custom-call | bytes 69206016 | tf_op jit(solution)/shard_map/pallas_call | solution.py:857
  1128.5 69.4 %shard_map.225 = bf16[16,128,2048]{2,1,0:T(8,128)(2,1)} custom-call(bf16[128,2048]{1,0:T(8,128)(2,1)} %get-tuple-element.152.x_ref), custom_call_target="tpu_custom_call" | custom-call | bytes 276824064 | tf_op jit(solution)/shard_map/pallas_call | solution.py:760
  1216.3 5.5 convolution_convert_fusion.25
  1221.9 5.3 convolution_convert_fusion.24
  1229.5 4.9 convolution_convert_fusion.x_ref
  1234.4 62.0 %shard_map.226 = bf16[128,2176]{1,0:T(8,128)(2,1)S(1)} custom-call(bf16[16,128,2176]{2,1,0:T(8,128)(2,1)} %convolution_convert_fusion.x_ref), custom_call_target="tpu_custom_call" | custom-call | bytes 294125568 | tf_op jit(solution)/shard_map/pallas_call | solution.py:857
  1338.6 5.0 fusion.16
  1361.5 24.6 %shard_map.227 = bf16[4,128,2048]{2,1,0:T(8,128)(2,1)} custom-call(bf16[128,2048]{1,0:T(8,128)(2,1)} %convert_select_fusion.x_ref), custom_call_target="tpu_custom_call" | custom-call | bytes 69206016 | tf_op jit(solution)/shard_map/pallas_call | solution.py:760
  1387.3 5.3 fusion.68
  1431.3 6.4 all-to-all-done.5
  1454.4 23.7 %all-to-all-done.4 = bf16[4,512,768]{2,1,0:T(8,128)(2,1)} async-done(((bf16[4,512,768]{2,1,0:T(8,128)(2,1)}), bf16[4,512,768]{2,1,0:T(8,128)(2,1)}, u32[]{:S(2)}, u32[]{:S(2)}) %all-to-all-start.4) | async-done | bytes 3145760 | tf_op jit(solution)/shard_map/all_to_all | solution.py:1576
  1492.7 8.5 maximum_convert_fusion.1
  1505.4 8.4 maximum_convert_fusion.2
  1513.8 7.6 all-to-all-done.3
  1521.4 8.4 maximum_convert_fusion
  1532.3 5.7 convolution_convert_fusion.30
  1537.9 20.8 %shard_map.228 = bf16[128,2048]{1,0:T(8,128)(2,1)S(1)} custom-call(bf16[4,128,2048]{2,1,0:T(8,128)(2,1)S(1)} %bitcast.489), custom_call_target="tpu_custom_call" | custom-call | bytes 69206016 | tf_op jit(solution)/shard_map/pallas_call | solution.py:857
  1568.7 20.5 %shard_map.229 = bf16[128,128]{1,0:T(8,128)(2,1)S(1)} custom-call(bf16[16,128,128]{2,1,0:T(8,128)(2,1)S(1)} %bitcast.492), custom_call_target="tpu_custom_call" | custom-call | bytes 17301504 | tf_op jit(solution)/shard_map/pallas_call | solution.py:857
  1606.6 6.2 collective-permute-done.16
  (916 shorter events, 396.4 us)
Async XLA Ops:
  7.2 726.3 %all-gather.2.cloned.1.call-start = ((), (), s32[]{:S(2)}) async-start(), calls=%async_computation.10 | async-start | bytes 8912896 | tf_op jit(solution)/shard_map/all_gather | solution.py:503
  9.2 12.3 collective-permute-start.3
  15.9 20.3 %collective-permute-start.2 = (bf16[2,64,1280]{2,1,0:T(8,128)(2,1)S(1)}, bf16[2,64,1280]{2,1,0:T(8,128)(2,1)S(1)}, u32[]{:S(2)}, u32[]{:S(2)}) collective-permute-start(bf16[2,64,1280]{2,1,0:T(8,128)(2,1)S(1)} %get-tuple-element.191), channel_id=1, source_target_pairs={{0,24},{8,16},{16,8},{24,0},{1,25},{9,17},{17,9},{25,1},{2,26},{10... | collective-permute-start | bytes 983048 | tf_op jit(solution)/shard_map/ppermute | solution.py:1245
  19.3 15.8 collective-permute-start
  19.9 16.2 collective-permute-start.1
  19.9 177.5 %copy-start.168 = (f32[64]{0:T(128)}, f32[64]{0:T(128)S(1)}, u32[]{:S(2)}) copy-start(f32[64]{0:T(128)S(1)} %multiply_exponential_fusion) | copy-start | bytes 772
  20.7 143.3 %copy-start.183 = (f32[128]{0:T(128)}, f32[128]{0:T(128)S(1)}, u32[]{:S(2)}) copy-start(f32[128]{0:T(128)S(1)} %fusion.215) | copy-start | bytes 1540
  164.0 72.4 %copy-start.137 = (f32[1,2048]{1,0:T(1,128)}, f32[1,2048]{1,0:T(1,128)S(1)}, u32[]{:S(2)}) copy-start(f32[1,2048]{1,0:T(1,128)S(1)} %get-tuple-element.235) | copy-start | bytes 24580
  164.0 464.9 %copy-start.127 = (f32[1,2048]{1,0:T(1,128)}, f32[1,2048]{1,0:T(1,128)S(1)}, u32[]{:S(2)}) copy-start(f32[1,2048]{1,0:T(1,128)S(1)} %get-tuple-element.234) | copy-start | bytes 24580
  198.4 399.6 %copy-start.59 = (f32[512,64]{1,0:T(8,128)}, f32[512,64]{1,0:T(8,128)S(1)}, u32[]{:S(2)}) copy-start(f32[512,64]{1,0:T(8,128)S(1)} %get-tuple-element.241) | copy-start | bytes 393220
  236.2 324.9 %copy-start = (bf16[128,2048]{1,0:T(8,128)(2,1)}, bf16[128,2048]{1,0:T(8,128)(2,1)S(1)}, u32[]{:S(2)}) copy-start(bf16[128,2048]{1,0:T(8,128)(2,1)S(1)} %shard_map.214) | copy-start | bytes 1572868
  319.4 173.9 %copy-start.121 = (f32[16,1,128,1]{2,3,1,0:T(1,128)}, f32[16,1,128,1]{2,3,1,0:T(1,128)S(1)}, u32[]{:S(2)}) copy-start(f32[16,1,128,1]{2,3,1,0:T(1,128)S(1)} %get-tuple-element.216) | copy-start | bytes 24580
  319.4 173.9 %copy-start.123 = (f32[16,1,128,1]{2,3,1,0:T(1,128)}, f32[16,1,128,1]{2,3,1,0:T(1,128)S(1)}, u32[]{:S(2)}) copy-start(f32[16,1,128,1]{2,3,1,0:T(1,128)S(1)} %get-tuple-element.215) | copy-start | bytes 24580
  319.6 173.7 %copy-start.152 = (f32[16,48]{1,0:T(8,128)}, f32[16,48]{1,0:T(8,128)S(1)}, u32[]{:S(2)}) copy-start(f32[16,48]{1,0:T(8,128)S(1)} %multiply_reduce_fusion.17) | copy-start | bytes 9220
  320.7 172.6 %copy-start.154 = (f32[16,48]{1,0:T(8,128)}, f32[16,48]{1,0:T(8,128)S(1)}, u32[]{:S(2)}) copy-start(f32[16,48]{1,0:T(8,128)S(1)} %multiply_reduce_fusion.18) | copy-start | bytes 9220
  561.4 324.5 %copy-start.8 = (f32[128,2048]{1,0:T(8,128)}, f32[128,2048]{1,0:T(8,128)S(1)}, u32[]{:S(2)}) copy-start(f32[128,2048]{1,0:T(8,128)S(1)} %get-tuple-element.163) | copy-start | bytes 3145732
  628.9 69.5 %copy-start.211 = (f32[128]{0:T(128)}, f32[128]{0:T(128)S(1)}, u32[]{:S(2)}) copy-start(f32[128]{0:T(128)S(1)} %multiply_reduce_fusion.12) | copy-start | bytes 1540
  628.9 69.5 %copy-start.180 = (f32[128]{0:T(128)}, f32[128]{0:T(128)S(1)}, u32[]{:S(2)}) copy-start(f32[128]{0:T(128)S(1)} %fusion.218) | copy-start | bytes 1540
  705.8 148.5 %copy-start.28 = (f32[2048,32]{1,0:T(8,128)}, f32[2048,32]{1,0:T(8,128)S(1)}, u32[]{:S(2)}) copy-start(f32[2048,32]{1,0:T(8,128)S(1)} %fusion.108) | copy-start | bytes 786436
  763.1 106.0 %collective-permute-start.4 = (bf16[2048,768]{1,0:T(8,128)(2,1)}, bf16[2048,768]{1,0:T(8,128)(2,1)}, u32[]{:S(2)}, u32[]{:S(2)}) collective-permute-start(bf16[2048,768]{1,0:T(8,128)(2,1)} %convolution_convert_fusion.18), channel_id=1, source_target_pairs={{0,1},{1,0},{2,3},{3,2},{4,5},{5,4},{6,7},{7,6},{8,9},{9,8},{10,11... | collective-permute-start | bytes 9437192 | tf_op jit(solution)/shard_map/ppermute | solution.py:486
  763.1 113.6 %collective-permute-start.5 = (bf16[2048,768]{1,0:T(8,128)(2,1)}, bf16[2048,768]{1,0:T(8,128)(2,1)}, u32[]{:S(2)}, u32[]{:S(2)}) collective-permute-start(bf16[2048,768]{1,0:T(8,128)(2,1)} %convolution_convert_fusion.16), channel_id=1, source_target_pairs={{0,1},{1,0},{2,3},{3,2},{4,5},{5,4},{6,7},{7,6},{8,9},{9,8},{10,11... | collective-permute-start | bytes 9437192 | tf_op jit(solution)/shard_map/ppermute | solution.py:486
  763.6 93.0 %collective-permute-start.6 = (bf16[768,2048]{1,0:T(8,128)(2,1)}, bf16[768,2048]{1,0:T(8,128)(2,1)}, u32[]{:S(2)}, u32[]{:S(2)}) collective-permute-start(bf16[768,2048]{1,0:T(8,128)(2,1)} %convolution_convert_fusion.14), channel_id=1, source_target_pairs={{0,1},{1,0},{2,3},{3,2},{4,5},{5,4},{6,7},{7,6},{8,9},{9,8},{10,11... | collective-permute-start | bytes 9437192 | tf_op jit(solution)/shard_map/ppermute | solution.py:486
  782.4 72.0 %copy-start.128 = (f32[1,2048]{1,0:T(1,128)S(1)}, f32[1,2048]{1,0:T(1,128)}, u32[]{:S(2)}) copy-start(f32[1,2048]{1,0:T(1,128)} %copy-done.127) | copy-start | bytes 24580
  782.4 72.0 %copy-start.181 = (f32[128]{0:T(128)S(1)}, f32[128]{0:T(128)}, u32[]{:S(2)}) copy-start(f32[128]{0:T(128)} %copy-done.180) | copy-start | bytes 1540
  864.1 81.9 %all-to-all-start.2 = ((bf16[4,768,512]{2,1,0:T(8,128)(2,1)}), bf16[4,768,512]{2,1,0:T(8,128)(2,1)}, u32[]{:S(2)}, u32[]{:S(2)}) async-start(bf16[4,768,512]{2,1,0:T(8,128)(2,1)} %bitcast.512), calls=%async_computation.2 | async-start | bytes 6291456 | tf_op jit(solution)/shard_map/all_to_all | solution.py:1576
  945.9 39.4 %all-to-all-start = ((bf16[4,512,768]{2,1,0:T(8,128)(2,1)}), bf16[4,512,768]{2,1,0:T(8,128)(2,1)}, u32[]{:S(2)}, u32[]{:S(2)}) async-start(bf16[4,512,768]{2,1,0:T(8,128)(2,1)} %bitcast.562), calls=%async_computation | async-start | bytes 6291456 | tf_op jit(solution)/shard_map/all_to_all | solution.py:1576
  964.6 129.0 %collective-permute-start.7 = (bf16[1024,1280]{1,0:T(8,128)(2,1)}, bf16[1024,1280]{1,0:T(8,128)(2,1)}, u32[]{:S(2)}, u32[]{:S(2)}) collective-permute-start(bf16[1024,1280]{1,0:T(8,128)(2,1)} %constant_dynamic-slice_fusion.3), channel_id=1, source_target_pairs={{0,1},{1,0},{2,3},{3,2},{4,5},{5,4},{6,7},{7,6},{8,9},{9,8},{10,11... | collective-permute-start | bytes 7864328 | tf_op jit(solution)/shard_map/ppermute | solution.py:486
  985.4 105.7 %all-to-all-start.1 = ((bf16[4,512,768]{2,1,0:T(8,128)(2,1)}), bf16[4,512,768]{2,1,0:T(8,128)(2,1)}, u32[]{:S(2)}, u32[]{:S(2)}) async-start(bf16[4,512,768]{2,1,0:T(8,128)(2,1)} %bitcast.561), calls=%async_computation.1 | async-start | bytes 6291456 | tf_op jit(solution)/shard_map/all_to_all | solution.py:1576
  990.2 497.1 %reduce-scatter.5.cloned.1.call-start = ((), (), s32[]{:S(2)}) async-start(), calls=%async_computation.11 | async-start | bytes 3276800 | tf_op jit(solution)/shard_map/reduce_scatter | solution.py:1623
  1303.0 295.3 %reduce-scatter.11.cloned.1.call-start = ((), (), s32[]{:S(2)}) async-start(), calls=%async_computation.14 | async-start | bytes 2621440 | tf_op jit(solution)/shard_map/reduce_scatter | solution.py:1623
  1309.8 19.4 %collective-permute-start.20 = (bf16[512,2048]{1,0:T(8,128)(2,1)}, bf16[512,2048]{1,0:T(8,128)(2,1)S(1)}, u32[]{:S(2)}, u32[]{:S(2)}) collective-permute-start(bf16[512,2048]{1,0:T(8,128)(2,1)} %constant_dynamic-slice_fusion.13), channel_id=1, source_target_pairs={{0,1},{1,0},{2,3},{3,2},{4,5},{5,4},{6,7},{7,6},{8,9},{9,8},{10,11... | collective-permute-start | bytes 6291464 | tf_op jit(solution)/shard_map/ppermute | solution.py:486
  1316.9 21.7 %collective-permute-start.8 = (bf16[2048,768]{1,0:T(8,128)(2,1)}, bf16[2048,768]{1,0:T(8,128)(2,1)}, u32[]{:S(2)}, u32[]{:S(2)}) collective-permute-start(bf16[2048,768]{1,0:T(8,128)(2,1)} %convolution_convert_fusion.10), channel_id=1, source_target_pairs={{0,1},{1,0},{2,3},{3,2},{4,5},{5,4},{6,7},{7,6},{8,9},{9,8},{10,11... | collective-permute-start | bytes 9437192 | tf_op jit(solution)/shard_map/ppermute | solution.py:486
  1321.0 24.6 %collective-permute-start.9 = (bf16[2048,768]{1,0:T(8,128)(2,1)}, bf16[2048,768]{1,0:T(8,128)(2,1)}, u32[]{:S(2)}, u32[]{:S(2)}) collective-permute-start(bf16[2048,768]{1,0:T(8,128)(2,1)} %convolution_convert_fusion.8), channel_id=1, source_target_pairs={{0,1},{1,0},{2,3},{3,2},{4,5},{5,4},{6,7},{7,6},{8,9},{9,8},{10,11... | collective-permute-start | bytes 9437192 | tf_op jit(solution)/shard_map/ppermute | solution.py:486
  1325.6 26.4 %collective-permute-start.10 = (bf16[768,2048]{1,0:T(8,128)(2,1)}, bf16[768,2048]{1,0:T(8,128)(2,1)}, u32[]{:S(2)}, u32[]{:S(2)}) collective-permute-start(bf16[768,2048]{1,0:T(8,128)(2,1)} %convolution_convert_fusion.6), channel_id=1, source_target_pairs={{0,1},{1,0},{2,3},{3,2},{4,5},{5,4},{6,7},{7,6},{8,9},{9,8},{10,11... | collective-permute-start | bytes 9437192 | tf_op jit(solution)/shard_map/ppermute | solution.py:486
  1397.1 40.6 %all-to-all-start.5 = ((bf16[4,768,512]{2,1,0:T(8,128)(2,1)}), bf16[4,768,512]{2,1,0:T(8,128)(2,1)}, u32[]{:S(2)}, u32[]{:S(2)}) async-start(bf16[4,768,512]{2,1,0:T(8,128)(2,1)} %broadcast_select_fusion), calls=%async_computation.9 | async-start | bytes 6291456 | tf_op jit(solution)/shard_map/all_to_all | solution.py:1576
  1401.9 196.5 %reduce-scatter.9.cloned.1.call-start = ((), (), s32[]{:S(2)}) async-start(), calls=%async_computation.13 | async-start | bytes 2621440 | tf_op jit(solution)/shard_map/reduce_scatter | solution.py:1623
  1418.1 11.0 collective-permute-start.19
  1437.7 40.4 %all-to-all-start.4 = ((bf16[4,512,768]{2,1,0:T(8,128)(2,1)}), bf16[4,512,768]{2,1,0:T(8,128)(2,1)}, u32[]{:S(2)}, u32[]{:S(2)}) async-start(bf16[4,512,768]{2,1,0:T(8,128)(2,1)} %bitcast.514), calls=%async_computation.8 | async-start | bytes 6291456 | tf_op jit(solution)/shard_map/all_to_all | solution.py:1576
  1450.7 50.6 %collective-permute-start.11 = (bf16[1024,1280]{1,0:T(8,128)(2,1)}, bf16[1024,1280]{1,0:T(8,128)(2,1)}, u32[]{:S(2)}, u32[]{:S(2)}) collective-permute-start(bf16[1024,1280]{1,0:T(8,128)(2,1)} %constant_dynamic-slice_fusion.2), channel_id=1, source_target_pairs={{0,1},{1,0},{2,3},{3,2},{4,5},{5,4},{6,7},{7,6},{8,9},{9,8},{10,11... | collective-permute-start | bytes 7864328 | tf_op jit(solution)/shard_map/ppermute | solution.py:486
  1478.2 43.2 %all-to-all-start.3 = ((bf16[4,512,768]{2,1,0:T(8,128)(2,1)}), bf16[4,512,768]{2,1,0:T(8,128)(2,1)}, u32[]{:S(2)}, u32[]{:S(2)}) async-start(bf16[4,512,768]{2,1,0:T(8,128)(2,1)} %bitcast.513), calls=%async_computation.7 | async-start | bytes 6291456 | tf_op jit(solution)/shard_map/all_to_all | solution.py:1576
  1483.0 118.1 %reduce-scatter.7.cloned.1.call-start = ((), (), s32[]{:S(2)}) async-start(), calls=%async_computation.12 | async-start | bytes 3276800 | tf_op jit(solution)/shard_map/reduce_scatter | solution.py:1623
  1489.2 106.5 %collective-permute-start.15 = (bf16[64,1280]{1,0:T(8,128)(2,1)}, bf16[64,1280]{1,0:T(8,128)(2,1)}, u32[]{:S(2)}, u32[]{:S(2)}) collective-permute-start(bf16[64,1280]{1,0:T(8,128)(2,1)} %get-tuple-element.200), channel_id=1, source_target_pairs={{0,24},{8,16},{16,8},{24,0},{1,25},{9,17},{17,9},{25,1},{2,26},{10... | collective-permute-start | bytes 491528 | tf_op jit(solution)/shard_map/ppermute | solution.py:1245
  1492.1 102.7 %collective-permute-start.14 = (bf16[64,1280]{1,0:T(8,128)(2,1)}, bf16[64,1280]{1,0:T(8,128)(2,1)}, u32[]{:S(2)}, u32[]{:S(2)}) collective-permute-start(bf16[64,1280]{1,0:T(8,128)(2,1)} %get-tuple-element.201), channel_id=1, source_target_pairs={{0,16},{8,24},{16,0},{24,8},{1,17},{9,25},{17,1},{25,9},{2,18},{10... | collective-permute-start | bytes 491528 | tf_op jit(solution)/shard_map/ppermute | solution.py:1245
  1492.6 101.1 %collective-permute-start.13 = (bf16[64,1280]{1,0:T(8,128)(2,1)}, bf16[64,1280]{1,0:T(8,128)(2,1)}, u32[]{:S(2)}, u32[]{:S(2)}) collective-permute-start(bf16[64,1280]{1,0:T(8,128)(2,1)} %get-tuple-element.202), channel_id=1, source_target_pairs={{0,8},{8,0},{16,24},{24,16},{1,9},{9,1},{17,25},{25,17},{2,10},{10... | collective-permute-start | bytes 491528 | tf_op jit(solution)/shard_map/ppermute | solution.py:1245
  1591.1 5.6 collective-permute-start.12
  1602.1 11.1 collective-permute-start.18
  1603.7 9.5 collective-permute-start.17
  1604.7 8.1 collective-permute-start.16
  (243 other events, 1784.6 us)
Sparse Core Ops, SparseCore 0:
  303.4 185.4 all-gather.1
  1303.2 55.5 reduce-scatter.4
  1361.0 43.5 reduce-scatter.10
  1431.4 46.4 reduce-scatter.8
  1505.5 54.7 reduce-scatter.6
